TPU v7x, 32 devices: a whole 2x2x4 slice. The times are simulated.
32 devices in a mesh: replica: 16 (over z, y, core), tensor: 2 (over x).
Axes of the slice: x: 2, y: 2, z: 4, core: 2. Of those that a mesh axis runs over, the one named last changes fastest.
Arguments:
- prompt_rows: bfloat16 [2048, 2048], P('replica', 'tensor'), may hold values from -6 to 6
- request_rows: bfloat16 [2048, 2048], P('replica', 'tensor'), may hold values from -6 to 6
- request_keyval_cache: bfloat16 [2048, 64, 512], P('replica', None, 'tensor'), may hold values from -9 to 9
- cache_len: int32 [2048], P('replica'), may hold values from 1 to 64, as said below
- destination: int32 [2048, 1], P('replica'), may hold values from 0 to 15; in each aligned block of 128 rows (0 to 127, 128 to 255, ...) at most 16 rows name the same one
- prefix_cache: bfloat16 [32768, 512], P('replica', 'tensor'), as said below
- attn_gain: float32 [2048], replicated, may hold values from 0.1 to 1.9
- w_query: bfloat16 [2048, 1024], P(None, 'tensor'), may hold values from -0.125 to 0.125
- keyval_weight: bfloat16 [2048, 512], P(None, 'tensor'), may hold values from -0.125 to 0.125
- w_out: bfloat16 [1024, 2048], P('tensor'), may hold values from -0.75 to 0.75
- mlp_gain: float32 [2048], replicated, may hold values from 0.1 to 1.9
- w_gate: bfloat16 [2048, 2560], P(None, 'tensor'), may hold values from -0.125 to 0.125
- w_up: bfloat16 [2048, 2560], P(None, 'tensor'), may hold values from -0.125 to 0.125
- w_down: bfloat16 [2560, 2048], P('tensor'), may hold values from -0.125 to 0.125
Outputs:
- prompt_out: bfloat16 [2048, 2048], P('replica', 'tensor')
- request_out: bfloat16 [2048, 2048], P('replica', 'tensor')
Inputs may be any that keep to these rules, and one draw needn't show every extreme that they name: `cache_len`: the first of each replica's 128 requests has exactly 64 cached tokens. `destination`: among the 128 requests of one replica no replica is named more than 16 times, and in every draw some replica is named exactly 16 times by some replica. `prefix_cache`: keys and values of each replica's shared prefix.
All inputs are finite; a program needn't handle non-finite values.
Results may differ from a plain program's by a relative error of at most 0.019.
The roundings to bfloat16 on the way count: a program that leaves them out, or rounds other values in their place, can miss the bound.
Values may be sent and summed in bfloat16 or wider, within the bound.
No kernel may reach another device: no remote copies, remote signals or barrier semaphores. Data moves between devices by JAX's collectives and lax.ppermute only.
A program may use at most 128 MiB of HBM per device.

v0:
```python
import jax
import jax.numpy as jnp
from jax import lax
from jax.sharding import PartitionSpec as P

HEAD_SIZE = 64


EPS = 1e-05


def rms_norm(row_vals, gain_vec):
    values = row_vals.astype(jnp.float32)
    inv_scale = lax.rsqrt(jnp.mean(values * values, axis=1, keepdims=True) + EPS)
    return (values * inv_scale * gain_vec).astype(jnp.bfloat16)


def prompt_attend(queries, keyval, prefix_cache):
    row_count = queries.shape[0]
    kv_heads = keyval.shape[1] // (2 * HEAD_SIZE)
    prefix_len = prefix_cache.shape[0]
    key_rows = jnp.concatenate((prefix_cache, keyval), axis=0).reshape(-1, kv_heads, 2, HEAD_SIZE)
    grouped = queries.reshape(row_count, kv_heads, -1, HEAD_SIZE)
    scores = jnp.einsum(
        "rkgd,skd->rkgs", grouped, key_rows[:, :, 0], preferred_element_type=jnp.float32
    ) * HEAD_SIZE ** (-0.5)
    row_ids = lax.broadcasted_iota(jnp.int32, (row_count, key_rows.shape[0]), 0)
    col_ids = lax.broadcasted_iota(jnp.int32, (row_count, key_rows.shape[0]), 1)
    visible = (col_ids < prefix_len) | (col_ids - prefix_len <= row_ids)
    scores = jnp.where(visible[:, None, None, :], scores, -jnp.inf)
    row_max = jnp.max(scores, axis=3, keepdims=True)
    exp_vals = jnp.exp(scores - row_max)
    weights = (exp_vals / jnp.sum(exp_vals, axis=3, keepdims=True)).astype(jnp.bfloat16)
    mixed_out = jnp.einsum(
        "rkgs,skd->rkgd", weights, key_rows[:, :, 1], preferred_element_type=jnp.float32
    )
    return mixed_out.reshape(row_count, -1).astype(jnp.bfloat16)


def slot_attend(queries, keyval, slot_cache, slot_len, prefix_cache):
    slot_total = queries.shape[0]
    kv_heads = keyval.shape[1] // (2 * HEAD_SIZE)
    factor = HEAD_SIZE ** (-0.5)
    grouped = queries.reshape(slot_total, kv_heads, -1, HEAD_SIZE)
    prefix_kv = prefix_cache.reshape(-1, kv_heads, 2, HEAD_SIZE)
    past_kv = slot_cache.reshape(slot_total, slot_cache.shape[1], kv_heads, 2, HEAD_SIZE)
    own_kv = keyval.reshape(slot_total, kv_heads, 2, HEAD_SIZE)
    score_prefix = (
        jnp.einsum(
            "skgd,pkd->skgp", grouped, prefix_kv[:, :, 0], preferred_element_type=jnp.float32
        )
        * factor
    )
    score_past = (
        jnp.einsum(
            "skgd,slkd->skgl", grouped, past_kv[:, :, :, 0], preferred_element_type=jnp.float32
        )
        * factor
    )
    score_own = (
        jnp.einsum("skgd,skd->skg", grouped, own_kv[:, :, 0], preferred_element_type=jnp.float32)
        * factor
    )
    positions = lax.broadcasted_iota(jnp.float32, (slot_total, slot_cache.shape[1]), 1)
    live_mask = positions < slot_len.astype(jnp.float32)[:, None]
    score_past = jnp.where(live_mask[:, None, None, :], score_past, -jnp.inf)
    row_max = jnp.maximum(
        jnp.maximum(jnp.max(score_prefix, axis=3), jnp.max(score_past, axis=3)), score_own
    )
    exp_prefix = jnp.exp(score_prefix - row_max[..., None])
    exp_past = jnp.exp(score_past - row_max[..., None])
    exp_own = jnp.exp(score_own - row_max)
    denominator = jnp.sum(exp_prefix, axis=3) + jnp.sum(exp_past, axis=3) + exp_own
    w_prefix = (exp_prefix / denominator[..., None]).astype(jnp.bfloat16)
    w_past = (exp_past / denominator[..., None]).astype(jnp.bfloat16)
    w_own = (exp_own / denominator).astype(jnp.bfloat16)
    mixed_out = jnp.einsum(
        "skgp,pkd->skgd", w_prefix, prefix_kv[:, :, 1], preferred_element_type=jnp.float32
    )
    mixed_out = mixed_out + jnp.einsum(
        "skgl,slkd->skgd", w_past, past_kv[:, :, :, 1], preferred_element_type=jnp.float32
    )
    mixed_out = (
        mixed_out
        + w_own.astype(jnp.float32)[..., None] * own_kv[:, :, 1].astype(jnp.float32)[:, :, None, :]
    )
    return mixed_out.reshape(slot_total, -1).astype(jnp.bfloat16)


def tensor_layer(row_block, attend_fn, layer_params):
    attn_gain, w_query, keyval_weight, w_out, mlp_gain, w_gate, w_up, w_down = layer_params
    whole_rows = lax.all_gather(row_block, "tensor", axis=1, tiled=True)
    normed = rms_norm(whole_rows, attn_gain)
    queries = jnp.dot(normed, w_query, preferred_element_type=jnp.float32).astype(jnp.bfloat16)
    keyval = jnp.dot(normed, keyval_weight, preferred_element_type=jnp.float32).astype(jnp.bfloat16)
    attended = attend_fn(queries, keyval)
    head_terms = jnp.dot(attended, w_out, preferred_element_type=jnp.float32)
    mixed_sum = lax.psum_scatter(
        head_terms.astype(jnp.bfloat16), "tensor", scatter_dimension=1, tiled=True
    ).astype(jnp.float32)
    residual = (row_block.astype(jnp.float32) + mixed_sum).astype(jnp.bfloat16)
    whole_mid = lax.all_gather(residual, "tensor", axis=1, tiled=True)
    normed_mid = rms_norm(whole_mid, mlp_gain)
    gate_act = jnp.dot(normed_mid, w_gate, preferred_element_type=jnp.float32)
    up_act = jnp.dot(normed_mid, w_up, preferred_element_type=jnp.float32)
    hidden = (jax.nn.silu(gate_act) * up_act).astype(jnp.bfloat16)
    unit_terms = jnp.dot(hidden, w_down, preferred_element_type=jnp.float32)
    summed = lax.psum_scatter(
        unit_terms.astype(jnp.bfloat16), "tensor", scatter_dimension=1, tiled=True
    ).astype(jnp.float32)
    return (residual.astype(jnp.float32) + summed).astype(jnp.bfloat16)


def body(
    prompt_rows,
    request_rows,
    request_keyval_cache,
    cache_len,
    destination,
    prefix_cache,
    attn_gain,
    w_query,
    keyval_weight,
    w_out,
    mlp_gain,
    w_gate,
    w_up,
    w_down,
):
    layer_params = (attn_gain, w_query, keyval_weight, w_out, mlp_gain, w_gate, w_up, w_down)
    replicas = lax.axis_size("replica")
    requests = request_rows.shape[0]
    per_peer = 2 * requests // replicas
    slot_count = replicas * per_peer
    target = destination[:, 0]
    earlier = lax.broadcasted_iota(jnp.int32, (requests, requests), 1) < lax.broadcasted_iota(
        jnp.int32, (requests, requests), 0
    )
    peer_rank = jnp.sum(((target[:, None] == target[None, :]) & earlier).astype(jnp.int32), axis=1)
    slot_place = target * per_peer + peer_rank
    lengths = cache_len.astype(jnp.bfloat16)
    send_rows = (
        jnp.zeros((slot_count,) + request_rows.shape[1:], jnp.bfloat16)
        .at[slot_place]
        .set(request_rows)
    )
    send_cache = (
        jnp.zeros((slot_count,) + request_keyval_cache.shape[1:], jnp.bfloat16)
        .at[slot_place]
        .set(request_keyval_cache)
    )
    send_len = jnp.zeros((slot_count,), jnp.bfloat16).at[slot_place].set(lengths)
    slot_rows, slot_cache, slot_len = (
        lax.all_to_all(send_rows, "replica", split_axis=0, concat_axis=0, tiled=True),
        lax.all_to_all(send_cache, "replica", split_axis=0, concat_axis=0, tiled=True),
        lax.all_to_all(send_len, "replica", split_axis=0, concat_axis=0, tiled=True),
    )

    def serve_requests(queries, keyval):
        return slot_attend(queries, keyval, slot_cache, slot_len, prefix_cache)

    def serve_prompts(queries, keyval):
        return prompt_attend(queries, keyval, prefix_cache)

    prompts = prompt_rows.shape[0]

    def serve_both(queries, keyval):
        return jnp.concatenate(
            (
                serve_prompts(queries[:prompts], keyval[:prompts]),
                serve_requests(queries[prompts:], keyval[prompts:]),
            ),
            axis=0,
        )

    joined = tensor_layer(
        jnp.concatenate((prompt_rows, slot_rows), axis=0), serve_both, layer_params
    )
    prompt_out = joined[:prompts]
    block_out = joined[prompts:]
    returned = lax.all_to_all(block_out, "replica", split_axis=0, concat_axis=0, tiled=True)
    request_out = jnp.take(returned, slot_place, axis=0)
    return (prompt_out, request_out)


def solution(mesh):
    return jax.shard_map(
        body,
        mesh=mesh,
        in_specs=(
            P("replica", "tensor"),
            P("replica", "tensor"),
            P("replica", None, "tensor"),
            P("replica"),
            P("replica", None),
            P("replica", "tensor"),
            P(),
            P(None, "tensor"),
            P(None, "tensor"),
            P("tensor", None),
            P(),
            P(None, "tensor"),
            P(None, "tensor"),
            P("tensor", None),
        ),
        out_specs=(P("replica", "tensor"), P("replica", "tensor")),
        check_vma=False,
    )
```

profile of v0, /device:TPU:0, one launch (start us, length us, event | category | flops | bytes accessed | tf_op | source)
XLA Modules:
  0.0 462.3 jit_solution(13626056713486042965)
XLA Ops:
  12.1 7.4 %all-to-all-start.1 = ((bf16[16,16,1]{1,2,0:T(2,128)(2,1)}), bf16[16,16,1]{1,2,0:T(2,128)(2,1)S(1)}, u32[]{:S(2)}, u32[]{:S(2)}) async-start(bf16[16,16,1]{1,2,0:T(2,128)(2,1)} %all_to_all.34), calls=%async_computation.1 | async-start | bytes 16384 | tf_op jit(solution)/shard_map/all_to_all | solution.py:156
  19.5 2.4 scatter_custom_fusion
  21.9 4.0 all-to-all-done.1
  25.8 3.6 all-to-all-start
  29.4 4.3 broadcast_in_dim.66
  33.7 19.4 %scatter_fusion = bf16[256,64,256]{2,1,0:T(8,128)(2,1)} fusion(bf16[256,64,256]{2,1,0:T(8,128)(2,1)} %broadcast_in_dim.66, s32[128]{0:T(128)S(1)} %bitcast.157, bf16[128,64,256]{2,1,0:T(8,128)(2,1)} %param.16), kind=kCustom, calls=%fused_computation.3 | custom fusion | bytes 12583424 | tf_op jit(solution)/shard_map/scatter | solution.py:150
  53.1 6.2 %all-to-all-start.2 = ((bf16[256,64,256]{2,1,0:T(8,128)(2,1)}), bf16[256,64,256]{2,1,0:T(8,128)(2,1)}, u32[]{:S(2)}, u32[]{:S(2)}) async-start(bf16[256,64,256]{2,1,0:T(8,128)(2,1)} %scatter_fusion), calls=%async_computation.2 | async-start | bytes 16777216 | tf_op jit(solution)/shard_map/all_to_all | solution.py:155
  61.9 2.4 fusion.33
  65.2 25.0 %all-gather.3.cloned.1.call-done = bf16[384,2048]{1,0:T(8,128)(2,1)} async-done(((bf16[384,1024]{1,0:T(8,128)(2,1)}), bf16[384,2048]{1,0:T(8,128)(2,1)}) %all-gather.3.cloned.1.call-update) | async-done | bytes 1572880 | tf_op jit(solution)/shard_map/all_gather | solution.py:92
  92.1 2.6 convolution_convert_fusion.3
  104.3 4.1 fusion.67
  108.4 6.1 %fusion.29 = bf16[2,64,128,4]{2,1,3,0:T(8,128)(2,1)} fusion(f32[128,2,4]{0,2,1:T(4,128)S(1)} %fusion.67, bf16[2176,2,2,64]{0,3,2,1:T(8,128)(2,1)} %bitcast.151, pred[128,2176]{0,1:T(8,128)(4,1)} %fusion.33, bf16[128,2,4,64]{0,3,2,1:T(8,128)(2,1)S(1)} %bitcast.154), kind=kOutput, calls=%fused_computation.47 | convolution fusion | flops 581635200 | bytes 1658880 | tf_op jit(solution)/shard_map/rkgs,skd->rkgd/dot_general | solution.py:34
  114.5 8.1 %bitcast_reduce_fusion = (f32[256,2,4]{0,2,1:T(4,128)S(1)}, f32[2,256,4,2048]{3,1,2,0:T(8,128)}) fusion(bf16[256,2,4,64]{0,3,2,1:T(8,128)(2,1)S(1)} %bitcast.149, bf16[2048,2,2,64]{0,3,2,1:T(8,128)(2,1)S(1)} %bitcast.144), kind=kOutput, calls=%fused_computation.6 | convolution fusion | flops 545257472 | bytes 17571840 | tf_op jit(solution)/shard_map/skgd,pkd->skgp/dot_general | solution.py:49
  122.6 87.4 %all-to-all-done.2 = bf16[256,64,256]{2,1,0:T(8,128)(2,1)} async-done(((bf16[256,64,256]{2,1,0:T(8,128)(2,1)}), bf16[256,64,256]{2,1,0:T(8,128)(2,1)}, u32[]{:S(2)}, u32[]{:S(2)}) %all-to-all-start.2) | async-done | bytes 8388640 | tf_op jit(solution)/shard_map/all_to_all | solution.py:155
  210.0 13.1 %copy.85 = bf16[256,64,256]{0,2,1:T(8,128)(2,1)} copy(bf16[256,64,256]{2,1,0:T(8,128)(2,1)} %all-to-all-done.2) | data formatting | bytes 16777216 | tf_op jit(solution)/shard_map/all_to_all | solution.py:155
  223.0 6.1 %fusion.65 = (bf16[256,64,2,1,64]{0,4,3,2,1:T(8,128)(2,1)}, bf16[256,64,2,1,64]{0,4,3,2,1:T(8,128)(2,1)}) fusion(bf16[256,64,2,2,64]{0,4,3,2,1:T(8,128)(2,1)} %bitcast.142), kind=kLoop, calls=%fused_computation.103 | loop fusion | bytes 16777216 | tf_op jit(solution)/shard_map/slice | solution.py:56
  229.1 13.0 %copy.109 = bf16[256,64,2,1,64]{4,1,2,0,3:T(8,128)(2,1)} copy(bf16[256,64,2,1,64]{0,4,3,2,1:T(8,128)(2,1)} %get-tuple-element.6) | data formatting | bytes 8388608
  242.1 9.2 %fusion.66 = (f32[256,2,4]{2,1,0:T(2,128)S(1)}, f32[256,2,4,64]{3,2,1,0:T(4,128)}) fusion(bf16[256,2,4,64]{3,2,1,0:T(4,128)(2,1)} %copy.87, bf16[256,64,2,1,64]{4,1,2,0,3:T(8,128)(2,1)} %copy.109, pred[256,64]{1,0:T(8,128)(4,1)S(1)} %copy-done.9), kind=kOutput, calls=%fused_computation.104 | convolution fusion | flops 17168384 | bytes 5005312 | tf_op jit(solution)/shard_map/skgd,slkd->skgl/dot_general | solution.py:55
  251.5 13.0 %copy.111 = bf16[256,64,2,1,64]{4,1,2,0,3:T(8,128)(2,1)} copy(bf16[256,64,2,1,64]{0,4,3,2,1:T(8,128)(2,1)} %get-tuple-element.7) | data formatting | bytes 8388608
  264.7 7.6 %fusion.2 = f32[256,2,4]{0,2,1:T(4,128)S(1)} fusion(f32[2,256,4,2048]{3,1,2,0:T(8,128)} %get-tuple-element.11, f32[256,2,4]{0,2,1:T(4,128)S(1)} %maximum_maximum_fusion), kind=kLoop, calls=%fused_computation.9 | loop fusion | flops 12580864 | bytes 16793600 | tf_op jit(solution)/shard_map/reduce_sum | solution.py:73
  277.1 7.2 %fusion.3 = f32[256,2,4,64]{3,2,1,0:T(4,128)} fusion(bf16[256,64,2,1,64]{4,1,2,0,3:T(8,128)(2,1)} %copy.111, f32[256,2,4,64]{3,2,1,0:T(4,128)} %get-tuple-element.13, f32[256,2,4]{2,1,0:T(2,128)} %copy.92, f32[256,2,4]{2,1,0:T(2,128)S(1)} %copy.89), kind=kOutput, calls=%fused_computation.13 | convolution fusion | flops 17170432 | bytes 5259264 | tf_op jit(solution)/shard_map/skgl,slkd->skgd/dot_general | solution.py:80
  284.2 2.3 copy.94
  286.6 8.1 %fusion.28 = bf16[256,2,4,64]{0,3,2,1:T(8,128)(2,1)S(1)} fusion(f32[256,2,4,64]{0,3,2,1:T(8,128)} %copy.94, f32[2,256,4,2048]{3,1,2,0:T(8,128)} %get-tuple-element.11, f32[256,2,4]{0,2,1:T(4,128)S(1)} %get-tuple-element.5, f32[256,2,4]{0,2,1:T(4,128)S(1)} %maximum_maximum_fusion, bf16[2048,2,2,64]{0,3,2,1:T(8,128)(2,1)S(1)} %bitcast.145, ...), kind=kOutput, calls=%fused_computation.45 | convolution fusion | flops 554172416 | bytes 18243584 | tf_op jit(solution)/shard_map/skgp,pkd->skgd/dot_general | solution.py:77
  294.7 2.2 convolution_convert_fusion.1
  297.0 58.0 %reduce-scatter.3.cloned.1.call-done = bf16[384,1024]{1,0:T(8,128)(2,1)} async-done(((bf16[384,2048]{1,0:T(8,128)(2,1)}), bf16[384,1024]{1,0:T(8,128)(2,1)}) %reduce-scatter.3.cloned.1.call-update) | async-done | bytes 786448 | tf_op jit(solution)/shard_map/reduce_scatter | solution.py:98
  355.0 2.3 add_convert_fusion.1
  357.4 27.3 %all-gather.5.cloned.1.call-done = bf16[384,2048]{1,0:T(8,128)(2,1)} async-done(((bf16[384,1024]{1,0:T(8,128)(2,1)}), bf16[384,2048]{1,0:T(8,128)(2,1)}) %all-gather.5.cloned.1.call-update) | async-done | bytes 1572880 | tf_op jit(solution)/shard_map/all_gather | solution.py:102
  386.5 6.5 %fusion.41 = f32[384,1280]{1,0:T(8,128)} fusion(bf16[2048,1280]{1,0:T(8,128)(2,1)} %param.25, bf16[384,2048]{1,0:T(8,128)(2,1)} %all-gather.5.cloned.1.call-done, f32[2048]{0:T(1024)S(1)} %copy-done.17, f32[384]{0:T(512)S(1)} %add_rsqrt_fusion), kind=kOutput, calls=%fused_computation.65 | convolution fusion | flops 2016411648 | bytes 8791552 | tf_op jit(solution)/shard_map/dot_general | solution.py:104
  393.0 11.2 %convolution_convert_fusion = bf16[384,2048]{1,0:T(8,128)(2,1)} fusion(bf16[1280,2048]{1,0:T(8,128)(2,1)} %param.27, bf16[2048,1280]{1,0:T(8,128)(2,1)} %param.26, f32[384,1280]{1,0:T(8,128)} %fusion.41, bf16[384,2048]{1,0:T(8,128)(2,1)} %all-gather.5.cloned.1.call-done, f32[2048]{0:T(1024)S(1)} %copy-done.17, f32[384]{0:T(512)S(1)} %add_rsqrt_fusion), kind=kOutput, calls=%fused_computation.34 | convolution fusion | flops 4033413120 | bytes 15607296 | tf_op jit(solution)/shard_map/dot_general | solution.py:107
  404.2 26.2 %reduce-scatter.5.cloned.1.call-done = bf16[384,1024]{1,0:T(8,128)(2,1)} async-done(((bf16[384,2048]{1,0:T(8,128)(2,1)}), bf16[384,1024]{1,0:T(8,128)(2,1)}) %reduce-scatter.5.cloned.1.call-update) | async-done | bytes 786448 | tf_op jit(solution)/shard_map/reduce_scatter | solution.py:108
  433.6 5.6 %all-to-all-start.3 = ((bf16[16,16,1024]{2,1,0:T(8,128)(2,1)}), bf16[16,16,1024]{2,1,0:T(8,128)(2,1)S(1)}, u32[]{:S(2)}, u32[]{:S(2)}) async-start(bf16[16,16,1024]{2,1,0:T(8,128)(2,1)} %bitcast.37), calls=%async_computation.5 | async-start | bytes 1048576 | tf_op jit(solution)/shard_map/all_to_all | solution.py:181
  440.9 12.8 %all-to-all-done.3 = bf16[16,16,1024]{2,1,0:T(8,128)(2,1)S(1)} async-done(((bf16[16,16,1024]{2,1,0:T(8,128)(2,1)}), bf16[16,16,1024]{2,1,0:T(8,128)(2,1)S(1)}, u32[]{:S(2)}, u32[]{:S(2)}) %all-to-all-start.3) | async-done | bytes 524320 | tf_op jit(solution)/shard_map/all_to_all | solution.py:181
  (87 shorter events, 33.3 us)
Async XLA Ops:
  7.2 287.5 %copy-start = (bf16[512,2048]{1,0:T(8,128)(2,1)S(1)}, bf16[512,2048]{1,0:T(8,128)(2,1)}, u32[]{:S(2)}) copy-start(bf16[512,2048]{1,0:T(8,128)(2,1)} %param.23) | copy-start | bytes 6291460
  10.1 23.6 %copy-start.12 = (s32[128,1]{0,1:T(1,128)}, s32[128,1]{0,1:T(1,128)S(1)}, u32[]{:S(2)}) copy-start(s32[128,1]{0,1:T(1,128)S(1)} %get-tuple-element.3) | copy-start | bytes 1540
  12.1 13.7 %all-to-all-start.1 = ((bf16[16,16,1]{1,2,0:T(2,128)(2,1)}), bf16[16,16,1]{1,2,0:T(2,128)(2,1)S(1)}, u32[]{:S(2)}, u32[]{:S(2)}) async-start(bf16[16,16,1]{1,2,0:T(2,128)(2,1)} %all_to_all.34), calls=%async_computation.1 | async-start | bytes 16384 | tf_op jit(solution)/shard_map/all_to_all | solution.py:156
  25.8 27.2 %all-to-all-start = ((bf16[16,16,1024]{2,1,0:T(8,128)(2,1)}), bf16[16,16,1024]{2,1,0:T(8,128)(2,1)S(1)}, u32[]{:S(2)}, u32[]{:S(2)}) async-start(bf16[16,16,1024]{2,1,0:T(8,128)(2,1)} %bitcast.4), calls=%async_computation | async-start | bytes 1048576 | tf_op jit(solution)/shard_map/all_to_all | solution.py:154
  53.1 6.3 %copy-start.7 = (bf16[128,1024]{1,0:T(8,128)(2,1)S(1)}, bf16[128,1024]{1,0:T(8,128)(2,1)}, u32[]{:S(2)}) copy-start(bf16[128,1024]{1,0:T(8,128)(2,1)} %param.14) | copy-start | bytes 786436
  53.1 6.2 %copy-start.2 = (bf16[16,16,1024]{2,1,0:T(8,128)(2,1)}, bf16[16,16,1024]{2,1,0:T(8,128)(2,1)S(1)}, u32[]{:S(2)}) copy-start(bf16[16,16,1024]{2,1,0:T(8,128)(2,1)S(1)} %all-to-all-done) | copy-start | bytes 1572868
  53.1 156.9 %all-to-all-start.2 = ((bf16[256,64,256]{2,1,0:T(8,128)(2,1)}), bf16[256,64,256]{2,1,0:T(8,128)(2,1)}, u32[]{:S(2)}, u32[]{:S(2)}) async-start(bf16[256,64,256]{2,1,0:T(8,128)(2,1)} %scatter_fusion), calls=%async_computation.2 | async-start | bytes 16777216 | tf_op jit(solution)/shard_map/all_to_all | solution.py:155
  59.3 30.9 %all-gather.3.cloned.1.call-start = ((), (), s32[]{:S(2)}) async-start(), calls=%async_computation.6 | async-start | bytes 2359296 | tf_op jit(solution)/shard_map/all_gather | solution.py:92
  59.3 32.8 %copy-start.16 = (f32[2048]{0:T(1024)S(1)}, f32[2048]{0:T(1024)}, u32[]{:S(2)}) copy-start(f32[2048]{0:T(1024)} %param.20) | copy-start | bytes 24580
  60.3 294.6 %reduce-scatter.3.cloned.1.call-start = ((), (), s32[]{:S(2)}) async-start(), calls=%async_computation.7 | async-start | bytes 2359296 | tf_op jit(solution)/shard_map/reduce_scatter | solution.py:98
  90.2 5.2 %copy-start.6 = (bf16[384,2048]{1,0:T(8,128)(2,1)S(1)}, bf16[384,2048]{1,0:T(8,128)(2,1)}, u32[]{:S(2)}) copy-start(bf16[384,2048]{1,0:T(8,128)(2,1)} %all-gather.3.cloned.1.call-done) | copy-start | bytes 4718596
  90.2 5.2 %copy-start.15 = (bf16[2048,512]{1,0:T(8,128)(2,1)S(1)}, bf16[2048,512]{1,0:T(8,128)(2,1)}, u32[]{:S(2)}) copy-start(bf16[2048,512]{1,0:T(8,128)(2,1)} %param.21) | copy-start | bytes 6291460
  104.3 4.1 copy-start.11
  229.1 13.0 %copy-start.9 = (pred[256,64]{1,0:T(8,128)(4,1)S(1)}, pred[256,64]{1,0:T(8,128)(4,1)}, u32[]{:S(2)}) copy-start(pred[256,64]{1,0:T(8,128)(4,1)} %iota_compare_fusion.1) | copy-start | bytes 49156
  264.7 7.6 %copy-start.4 = (f32[256,2,4,64]{3,2,1,0:T(4,128)S(1)}, f32[256,2,4,64]{3,2,1,0:T(4,128)}, u32[]{:S(2)}) copy-start(f32[256,2,4,64]{3,2,1,0:T(4,128)} %get-tuple-element.13) | copy-start | bytes 1572868
  277.1 9.5 %copy-start.10 = (f32[256,2,64]{0,2,1:T(8,128)S(1)}, f32[256,2,64]{0,2,1:T(8,128)}, u32[]{:S(2)}) copy-start(f32[256,2,64]{0,2,1:T(8,128)} %get-tuple-element.8) | copy-start | bytes 393220
  286.6 8.1 %copy-start.18 = (bf16[2,64,128,4]{2,1,3,0:T(8,128)(2,1)S(1)}, bf16[2,64,128,4]{2,1,3,0:T(8,128)(2,1)}, u32[]{:S(2)}) copy-start(bf16[2,64,128,4]{2,1,3,0:T(8,128)(2,1)} %fusion.29) | copy-start | bytes 393220
  294.7 60.2 %copy-start.3 = (bf16[16,16,1024]{2,1,0:T(8,128)(2,1)S(1)}, bf16[16,16,1024]{2,1,0:T(8,128)(2,1)}, u32[]{:S(2)}) copy-start(bf16[16,16,1024]{2,1,0:T(8,128)(2,1)} %copy-done.2) | copy-start | bytes 1572868
  294.7 60.2 %copy-start.8 = (bf16[128,1024]{1,0:T(8,128)(2,1)S(1)}, bf16[128,1024]{1,0:T(8,128)(2,1)}, u32[]{:S(2)}) copy-start(bf16[128,1024]{1,0:T(8,128)(2,1)} %param.14) | copy-start | bytes 786436
  296.9 89.6 %copy-start.17 = (f32[2048]{0:T(1024)S(1)}, f32[2048]{0:T(1024)}, u32[]{:S(2)}) copy-start(f32[2048]{0:T(1024)} %param.24) | copy-start | bytes 24580
  296.9 87.7 %all-gather.5.cloned.1.call-start = ((), (), s32[]{:S(2)}) async-start(), calls=%async_computation.8 | async-start | bytes 2359296 | tf_op jit(solution)/shard_map/all_gather | solution.py:102
  357.3 73.1 %reduce-scatter.5.cloned.1.call-start = ((), (), s32[]{:S(2)}) async-start(), calls=%async_computation.9 | async-start | bytes 2359296 | tf_op jit(solution)/shard_map/reduce_scatter | solution.py:108
  393.0 37.4 %copy-start.1 = (bf16[384,1024]{1,0:T(8,128)(2,1)S(1)}, bf16[384,1024]{1,0:T(8,128)(2,1)}, u32[]{:S(2)}) copy-start(bf16[384,1024]{1,0:T(8,128)(2,1)} %add_convert_fusion.1) | copy-start | bytes 2359300
  404.2 35.0 %copy-start.13 = (s32[128,1]{0,1:T(1,128)S(1)}, s32[128,1]{0,1:T(1,128)}, u32[]{:S(2)}) copy-start(s32[128,1]{0,1:T(1,128)} %copy-done.12) | copy-start | bytes 1540
  404.2 50.3 %copy-start.14 = (pred[128]{0:T(512)(128)(4,1)S(1)}, pred[128]{0:T(512)(128)(4,1)}, u32[]{:S(2)}) copy-start(pred[128]{0:T(512)(128)(4,1)} %get-tuple-element.2) | copy-start | bytes 388
  431.9 0.9 copy-start.5
  433.6 20.1 %all-to-all-start.3 = ((bf16[16,16,1024]{2,1,0:T(8,128)(2,1)}), bf16[16,16,1024]{2,1,0:T(8,128)(2,1)S(1)}, u32[]{:S(2)}, u32[]{:S(2)}) async-start(bf16[16,16,1024]{2,1,0:T(8,128)(2,1)} %bitcast.37), calls=%async_computation.5 | async-start | bytes 1048576 | tf_op jit(solution)/shard_map/all_to_all | solution.py:181
Sparse Core Ops, SparseCore 0:
  61.6 28.4 all-gather.2
  297.1 57.8 reduce-scatter.2
  357.4 27.1 all-gather.4
  404.3 26.0 reduce-scatter.4
where the time goes:
time: 468 us; the launch traced here: 462 us
  waiting for transfers between devices  241 us (51%)
  local copies, waits for them, and re-layouts  89.5 us (19%)
  matrix products  66.2 us (14%)
  other arithmetic  28.4 us (6%)
  starting transfers between devices  22.9 us (5%)
  between operations  14.5 us (3%)
    all_to_all x1, waiting for transfers between devices, body(): lax.all_to_all(send_cache, 'replica', split_axis=0, concat_axis=0, tiled=...  87.4 us
    reduce_scatter x1, waiting for transfers between devices, tensor_layer(): lax.psum_scatter(head_terms.astype(jnp.bfloat16), 'tensor', scatter_dimen...  58 us
    unnamed x41, local copies, waits for them, and re-layouts  28.5 us
    all_gather x1, waiting for transfers between devices, tensor_layer(): whole_mid = lax.all_gather(residual, 'tensor', axis=1, tiled=True)  27.3 us
    reduce_scatter x1, waiting for transfers between devices, tensor_layer(): lax.psum_scatter(unit_terms.astype(jnp.bfloat16), 'tensor', scatter_dimen...  26.2 us
    all_gather x1, waiting for transfers between devices, tensor_layer(): whole_rows = lax.all_gather(row_block, 'tensor', axis=1, tiled=True)  25 us
    scatter x1, local copies, waits for them, and re-layouts, body(): send_cache = jnp.zeros((slot_count,) + request_keyval_cache.shape[1:], jn...  19.4 us
    all_to_all x1, local copies, waits for them, and re-layouts, body(): lax.all_to_all(send_cache, 'replica', split_axis=0, concat_axis=0, tiled=...  13.1 us
  transfers between devices with their start and end apart: 8, of which 7 were waited for; matrix products, arithmetic and copies ran while one was open for 14% of the time, Pallas kernels for 0%

commit v1 on v0

v1 whole, which is shorter than its diff:
```python
import functools
import math

import jax
import jax.numpy as jnp
from jax import lax
from jax.experimental import pallas as pl
from jax.experimental.pallas import tpu as pltpu
from jax.sharding import PartitionSpec as P

HEAD_SIZE = 64
QUERIES_PER_KEY = 4
PAIR = 2 * HEAD_SIZE
GROUP = 16
EPS = 1e-05
FACTOR = HEAD_SIZE ** (-0.5) * math.log2(math.e)
F32 = jnp.float32
BF16 = jnp.bfloat16
VMEM_BYTES = 48 * 1024 * 1024
WHOLE = pl.BlockSpec(memory_space=pltpu.VMEM)
SCALAR = pl.BlockSpec(memory_space=pltpu.SMEM)


def params():
    return pltpu.CompilerParams(vmem_limit_bytes=VMEM_BYTES)


def cost(flops, read, exps=0):
    return pl.CostEstimate(flops=int(flops), bytes_accessed=int(read), transcendentals=int(exps))


def lane_ids(shape):
    return lax.broadcasted_iota(jnp.int32, shape, len(shape) - 1)


def rms_norm(values, gain_row):
    inv_scale = lax.rsqrt(jnp.mean(values * values, axis=1, keepdims=True) + EPS)
    return (values * inv_scale * gain_row).astype(BF16)


def in_order(place_ref, parts):
    if len(parts) == 2:
        first = place_ref[0] == 0
        own, other = parts
        parts = (jnp.where(first, own, other), jnp.where(first, other, own))
    return jnp.concatenate(parts, axis=1)


def head_query(queries, head):
    pair = head // 2
    block = queries[:, pair * PAIR : (pair + 1) * PAIR].astype(F32)
    if head % 2:
        block = pltpu.roll(block, HEAD_SIZE, 1)
    return jnp.where(lane_ids(block.shape) < HEAD_SIZE, block, 0.0).astype(BF16)


def ones_for_keys(keyval):
    key_half = lane_ids(keyval.shape) % PAIR < HEAD_SIZE
    return jnp.where(key_half, 1.0, keyval.astype(F32)).astype(BF16)


def scores_of(query_rows, key_rows):
    return lax.dot_general(
        query_rows, key_rows, (((1,), (1,)), ((), ())), preferred_element_type=F32
    )


def pack_pair(even, odd):
    even = even / pltpu.roll(even, HEAD_SIZE, 1)
    odd = odd / pltpu.roll(odd, HEAD_SIZE, 1)
    return jnp.where(
        lane_ids(even.shape) < HEAD_SIZE, pltpu.roll(even, HEAD_SIZE, 1), odd
    )


def project(rows, gain_ref, w_query_ref, keyval_weight_ref):
    normed = rms_norm(rows.astype(F32), gain_ref[...])
    queries = jnp.dot(normed, w_query_ref[...], preferred_element_type=F32).astype(BF16)
    keyval = jnp.dot(normed, keyval_weight_ref[...], preferred_element_type=F32).astype(BF16)
    return queries, keyval


def request_project_kernel(count, place_ref, *refs):
    parts, refs = refs[:count], refs[count:]
    gain_ref, w_query_ref, keyval_weight_ref, spread_ref, q_ref, kv_ref, send_ref = refs
    rows = in_order(place_ref, [ref[...] for ref in parts])
    queries, keyval = project(rows, gain_ref, w_query_ref, keyval_weight_ref)
    q_ref[...] = queries
    kv_ref[...] = keyval
    send_ref[...] = jnp.dot(spread_ref[...], queries, preferred_element_type=F32).astype(BF16)


def prompt_kernel(count, place_ref, *refs):
    parts, refs = refs[:count], refs[count:]
    gain_ref, w_query_ref, keyval_weight_ref, prefix_ref, w_out_ref, mixed_ref, q_scr, kvx_scr, att_scr = refs
    rows = in_order(place_ref, [ref[...] for ref in parts])
    queries, keyval = project(rows, gain_ref, w_query_ref, keyval_weight_ref)
    heads = queries.shape[1] // HEAD_SIZE
    row_count = queries.shape[0]
    for head in range(heads):
        q_scr[head] = head_query(queries, head)
    kvx_scr[...] = ones_for_keys(prefix_ref[...])
    own_ones = ones_for_keys(keyval)
    row_ids = lax.broadcasted_iota(jnp.int32, (2 * row_count, row_count), 0) % row_count
    visible = lax.broadcasted_iota(jnp.int32, (2 * row_count, row_count), 1) <= row_ids
    for kv in range(heads // QUERIES_PER_KEY):
        columns = slice(kv * PAIR, (kv + 1) * PAIR)
        own_keys = keyval[:, columns]
        own_values = own_ones[:, columns]
        for half in range(QUERIES_PER_KEY // 2):
            pair = kv * (QUERIES_PER_KEY // 2) + half
            query_rows = q_scr[pl.ds(2 * pair, 2)].reshape(2 * row_count, PAIR)
            past = scores_of(query_rows, prefix_ref[:, columns])
            own = jnp.where(visible, scores_of(query_rows, own_keys), -jnp.inf)
            row_max = jnp.maximum(
                jnp.max(past, axis=1, keepdims=True), jnp.max(own, axis=1, keepdims=True)
            )
            past_exp = jnp.exp2((past - row_max) * FACTOR).astype(BF16)
            own_exp = jnp.exp2((own - row_max) * FACTOR).astype(BF16)
            total = jnp.dot(past_exp, kvx_scr[:, columns], preferred_element_type=F32)
            total = total + jnp.dot(own_exp, own_values, preferred_element_type=F32)
            att_scr[:, pair * PAIR : (pair + 1) * PAIR] = pack_pair(
                total[:row_count], total[row_count:]
            ).astype(BF16)
    mixed_ref[...] = jnp.dot(
        att_scr[...], w_out_ref[...], preferred_element_type=F32
    ).astype(BF16)


def slot_kernel(q_ref, prefix_ref, out_ref, q_scr, kvx_scr):
    slots, width = q_ref.shape
    heads = width // HEAD_SIZE
    queries = q_ref[...]
    for head in range(heads):
        q_scr[head] = head_query(queries, head)
    kvx_scr[...] = ones_for_keys(prefix_ref[...])
    lanes = lane_ids((slots, PAIR))
    sums = jnp.zeros((slots, PAIR), F32)
    for kv in range(heads // QUERIES_PER_KEY):
        columns = slice(kv * PAIR, (kv + 1) * PAIR)
        for half in range(QUERIES_PER_KEY // 2):
            pair = kv * (QUERIES_PER_KEY // 2) + half
            totals = []
            for head in (2 * pair, 2 * pair + 1):
                scores = scores_of(q_scr[head], prefix_ref[:, columns])
                row_max = jnp.max(scores, axis=1, keepdims=True)
                exp_vals = jnp.exp2((scores - row_max) * FACTOR).astype(BF16)
                total = jnp.dot(exp_vals, kvx_scr[:, columns], preferred_element_type=F32)
                totals.append(total)
                log_sum = row_max * FACTOR + jnp.log2(total)
                high = log_sum.astype(BF16).astype(F32)
                middle = (log_sum - high).astype(BF16).astype(F32)
                low = log_sum - high - middle
                for place, part in enumerate((high, middle, low)):
                    sums = jnp.where(lanes == 3 * head + place, part, sums)
            out_ref[:, pair * PAIR : (pair + 1) * PAIR] = pack_pair(*totals).astype(BF16)
    out_ref[:, width:] = sums.astype(BF16)


def past_kernel(q_ref, kv_ref, len_ref, cache_ref, out_ref, sum_ref):
    group, width = q_ref.shape
    heads = width // HEAD_SIZE
    cached = cache_ref.shape[1]
    kv_width = kv_ref.shape[1]
    queries = q_ref[...]
    own = kv_ref[...].astype(F32)
    own_ones = jnp.where(lane_ids(own.shape) % PAIR < HEAD_SIZE, 1.0, own)
    keys = cache_ref[...].reshape(group * cached, kv_width)
    padded, own_scores = [], []
    for head in range(heads):
        kv = head // QUERIES_PER_KEY
        query = head_query(queries, head)
        blocks = [jnp.zeros_like(query)] * (kv_width // PAIR)
        blocks[kv] = query
        padded.append(jnp.concatenate(blocks, axis=1) if len(blocks) > 1 else query)
        own_scores.append(
            jnp.sum(query.astype(F32) * own[:, kv * PAIR : (kv + 1) * PAIR], axis=1, keepdims=True)
        )
    query_rows = jnp.concatenate(padded, axis=0)
    own_scores = jnp.concatenate(own_scores, axis=0)
    lengths = jnp.concatenate([len_ref[...]] * heads, axis=0)
    shape = (heads * group, group * cached)
    columns = lane_ids(shape)
    owner = lax.broadcasted_iota(jnp.int32, shape, 0) % group
    visible = (columns // cached == owner) & (columns % cached < lengths)
    scores = jnp.where(visible, scores_of(query_rows, keys), -jnp.inf)
    row_max = jnp.maximum(jnp.max(scores, axis=1, keepdims=True), own_scores)
    exp_vals = jnp.exp2((scores - row_max) * FACTOR).astype(BF16)
    own_exp = jnp.exp2((own_scores - row_max) * FACTOR).astype(BF16).astype(F32)
    totals = jnp.dot(exp_vals, ones_for_keys(keys), preferred_element_type=F32)
    lanes = lane_ids((group, PAIR))
    sums = jnp.zeros((group, PAIR), F32)
    done = []
    for head in range(heads):
        kv = head // QUERIES_PER_KEY
        at = slice(head * group, (head + 1) * group)
        block = slice(kv * PAIR, (kv + 1) * PAIR)
        total = totals[at, block] + own_exp[at] * own_ones[:, block]
        log_sum = row_max[at] * FACTOR + jnp.log2(total)
        sums = jnp.where(lanes == head, log_sum, sums)
        done.append(total)
    for pair in range(heads // 2):
        out_ref[:, pair * PAIR : (pair + 1) * PAIR] = pack_pair(done[2 * pair], done[2 * pair + 1])
    sum_ref[...] = sums


def merge_kernel(gather_ref, back_ref, past_ref, sum_ref, w_out_ref, mixed_ref):
    width = past_ref.shape[1]
    heads = width // HEAD_SIZE
    prefix = jnp.dot(gather_ref[...], back_ref[...], preferred_element_type=F32)
    prefix_sums = prefix[:, width:]
    past_sums = sum_ref[...]
    lanes = lane_ids(past_sums.shape)
    shares = []
    for head in range(heads):
        prefix_log = jnp.sum(
            jnp.where(lanes // 3 == head, prefix_sums, 0.0), axis=1, keepdims=True
        )
        past_log = jnp.sum(jnp.where(lanes == head, past_sums, 0.0), axis=1, keepdims=True)
        top = jnp.maximum(prefix_log, past_log)
        prefix_part = jnp.exp2(prefix_log - top)
        past_part = jnp.exp2(past_log - top)
        both = prefix_part + past_part
        shares.append((prefix_part / both, past_part / both))
    attended = []
    for pair in range(heads // 2):
        at = slice(pair * PAIR, (pair + 1) * PAIR)
        key_half = lanes < HEAD_SIZE
        prefix_share = jnp.where(key_half, shares[2 * pair][0], shares[2 * pair + 1][0])
        past_share = jnp.where(key_half, shares[2 * pair][1], shares[2 * pair + 1][1])
        attended.append((prefix_share * prefix[:, at] + past_share * past_ref[:, at]).astype(BF16))
    mixed_ref[...] = jnp.dot(
        jnp.concatenate(attended, axis=1), w_out_ref[...], preferred_element_type=F32
    ).astype(BF16)


def mlp_kernel(count, steps, place_ref, *refs):
    parts, refs = refs[:count], refs[count:]
    mixed, refs = refs[:count], refs[count:]
    gain_ref, w_gate_ref, w_up_ref, w_down_ref, *refs = refs
    *out_refs, normed_scr, total_scr = refs
    step = pl.program_id(0)
    total_width = total_scr.shape[1]
    width = total_width // count

    @pl.when(step == 0)
    def _():
        rows = in_order(place_ref, [ref[...] for ref in parts]).astype(F32)
        summed = mixed[0][...].astype(F32)
        for ref in mixed[1:]:
            summed = summed + ref[...].astype(F32)
        residual = (rows + summed).astype(BF16)
        normed_scr[...] = rms_norm(residual.astype(F32), gain_ref[...])
        if count == 2:
            first = place_ref[0] == 0
            out_refs[2][...] = jnp.where(first, residual[:, :width], residual[:, width:])
        else:
            out_refs[1][...] = residual

    normed = normed_scr[...]
    gate_act = jnp.dot(normed, w_gate_ref[...], preferred_element_type=F32)
    up_act = jnp.dot(normed, w_up_ref[...], preferred_element_type=F32)
    hidden = (gate_act / (1.0 + jnp.exp(-gate_act)) * up_act).astype(BF16)
    product = jnp.dot(hidden, w_down_ref[...], preferred_element_type=F32)

    @pl.when(step == 0)
    def _():
        total_scr[...] = product

    @pl.when(step > 0)
    def _():
        total_scr[...] += product

    @pl.when(step == steps - 1)
    def _():
        terms = total_scr[...].astype(BF16)
        if count == 2:
            first = place_ref[0] == 0
            out_refs[0][...] = jnp.where(first, terms[:, :width], terms[:, width:])
            out_refs[1][...] = jnp.where(first, terms[:, width:], terms[:, :width])
        else:
            out_refs[0][...] = terms


def swap(block, count):
    if count == 2:
        return [block, lax.ppermute(block, "tensor", [(0, 1), (1, 0)])]
    if count == 1:
        return [block]
    gathered = lax.all_gather(block, "tensor", axis=0, tiled=False)
    return [gathered[i] for i in range(count)]


def mlp(place, parts, mixed, gain, w_gate, w_up, w_down):
    count = len(parts)
    rows = parts[0].shape[0]
    model = sum(part.shape[1] for part in parts)
    hidden = w_gate.shape[1]
    steps = 5 if hidden % (5 * 128) == 0 else 1
    chunk = hidden // steps
    width = model // count
    if count == 2:
        outs = [jax.ShapeDtypeStruct((rows, width), BF16)] * 3
    else:
        outs = [jax.ShapeDtypeStruct((rows, model), BF16)] * 2
    return pl.pallas_call(
        functools.partial(mlp_kernel, count, steps),
        grid=(steps,),
        in_specs=[SCALAR]
        + [pl.BlockSpec((rows, width), lambda i: (0, 0))] * count
        + [pl.BlockSpec((rows, model), lambda i: (0, 0))] * count
        + [
            pl.BlockSpec((1, model), lambda i: (0, 0)),
            pl.BlockSpec((model, chunk), lambda i: (0, i)),
            pl.BlockSpec((model, chunk), lambda i: (0, i)),
            pl.BlockSpec((chunk, model), lambda i: (i, 0)),
        ],
        out_specs=[pl.BlockSpec(out.shape, lambda i: (0, 0)) for out in outs],
        out_shape=outs,
        scratch_shapes=[pltpu.VMEM((rows, model), BF16), pltpu.VMEM((rows, model), F32)],
        compiler_params=params(),
        cost_estimate=cost(6 * rows * model * hidden, 6 * model * hidden, rows * hidden),
        name="mlp",
    )(place, *parts, *mixed, gain, w_gate, w_up, w_down)


def finish(place, parts, mixed, layer_params):
    count = len(parts)
    mlp_gain, w_gate, w_up, w_down = layer_params
    outs = mlp(place, parts, mixed, mlp_gain, w_gate, w_up, w_down)
    if count == 2:
        keep, send, residual = outs
        other = lax.ppermute(send, "tensor", [(0, 1), (1, 0)])
        summed = keep.astype(F32) + other.astype(F32)
        return (residual.astype(F32) + summed).astype(BF16)
    terms, residual = outs
    width = terms.shape[1] // count
    summed = lax.psum_scatter(terms.astype(F32), "tensor", scatter_dimension=1, tiled=True)
    own = lax.dynamic_slice_in_dim(residual, lax.axis_index("tensor") * width, width, axis=1)
    return (own.astype(F32) + summed).astype(BF16)


def body(
    prompt_rows,
    request_rows,
    request_keyval_cache,
    cache_len,
    destination,
    prefix_cache,
    attn_gain,
    w_query,
    keyval_weight,
    w_out,
    mlp_gain,
    w_gate,
    w_up,
    w_down,
):
    count = lax.axis_size("tensor")
    replicas = lax.axis_size("replica")
    place = lax.axis_index("tensor").astype(jnp.int32).reshape(1)
    requests = request_rows.shape[0]
    prompts = prompt_rows.shape[0]
    model = w_query.shape[0]
    width = w_query.shape[1]
    kv_width = keyval_weight.shape[1]
    heads = width // HEAD_SIZE
    prefix_len = prefix_cache.shape[0]
    attn_gain = attn_gain.reshape(1, model)
    mlp_gain = mlp_gain.reshape(1, model)
    mlp_params = (mlp_gain, w_gate, w_up, w_down)

    request_parts = swap(request_rows, count)
    prompt_parts = swap(prompt_rows, count)

    per_peer = 2 * requests // replicas
    slots = replicas * per_peer
    target = destination[:, 0]
    earlier = lax.broadcasted_iota(jnp.int32, (requests, requests), 1) < lax.broadcasted_iota(
        jnp.int32, (requests, requests), 0
    )
    peer_rank = jnp.sum(((target[:, None] == target[None, :]) & earlier).astype(jnp.int32), axis=1)
    slot_place = target * per_peer + peer_rank
    gather = (
        lax.broadcasted_iota(jnp.int32, (requests, slots), 1) == slot_place[:, None]
    ).astype(BF16)
    spread = (
        lax.broadcasted_iota(jnp.int32, (slots, requests), 0) == slot_place[None, :]
    ).astype(BF16)

    queries, keyval, send = pl.pallas_call(
        functools.partial(request_project_kernel, count),
        in_specs=[SCALAR] + [WHOLE] * (count + 4),
        out_specs=[WHOLE] * 3,
        out_shape=[
            jax.ShapeDtypeStruct((requests, width), BF16),
            jax.ShapeDtypeStruct((requests, kv_width), BF16),
            jax.ShapeDtypeStruct((slots, width), BF16),
        ],
        compiler_params=params(),
        cost_estimate=cost(
            2 * requests * model * (width + kv_width), 2 * model * (width + kv_width)
        ),
        name="request_project",
    )(place, *request_parts, attn_gain, w_query, keyval_weight, spread)

    slot_queries = lax.all_to_all(send, "replica", split_axis=0, concat_axis=0, tiled=True)

    prompt_mixed = pl.pallas_call(
        functools.partial(prompt_kernel, count),
        in_specs=[SCALAR] + [WHOLE] * (count + 5),
        out_specs=WHOLE,
        out_shape=jax.ShapeDtypeStruct((prompts, model), BF16),
        scratch_shapes=[
            pltpu.VMEM((heads, prompts, PAIR), BF16),
            pltpu.VMEM((prefix_len, kv_width), BF16),
            pltpu.VMEM((prompts, width), BF16),
        ],
        compiler_params=params(),
        cost_estimate=cost(
            2 * prompts * model * (2 * width + kv_width) + 4 * prompts * heads * prefix_len * PAIR,
            2 * model * (2 * width + kv_width) + 2 * prefix_len * kv_width,
            prompts * heads * prefix_len,
        ),
        name="prompt_attention",
    )(place, *prompt_parts, attn_gain, w_query, keyval_weight, prefix_cache, w_out)

    cached = request_keyval_cache.shape[1]
    past, past_sums = pl.pallas_call(
        past_kernel,
        grid=(requests // GROUP,),
        in_specs=[
            pl.BlockSpec((GROUP, width), lambda i: (i, 0)),
            pl.BlockSpec((GROUP, kv_width), lambda i: (i, 0)),
            pl.BlockSpec((GROUP, 1), lambda i: (i, 0)),
            pl.BlockSpec((GROUP, cached, kv_width), lambda i: (i, 0, 0)),
        ],
        out_specs=[
            pl.BlockSpec((GROUP, width), lambda i: (i, 0)),
            pl.BlockSpec((GROUP, PAIR), lambda i: (i, 0)),
        ],
        out_shape=[
            jax.ShapeDtypeStruct((requests, width), F32),
            jax.ShapeDtypeStruct((requests, PAIR), F32),
        ],
        compiler_params=params(),
        cost_estimate=cost(
            4 * requests * heads * GROUP * cached * kv_width,
            2 * requests * cached * kv_width,
            requests * heads * GROUP * cached,
        ),
        name="past_attention",
    )(queries, keyval, cache_len.reshape(requests, 1), request_keyval_cache)

    slot_out = pl.pallas_call(
        slot_kernel,
        in_specs=[WHOLE] * 2,
        out_specs=WHOLE,
        out_shape=jax.ShapeDtypeStruct((slots, width + PAIR), BF16),
        scratch_shapes=[
            pltpu.VMEM((heads, slots, PAIR), BF16),
            pltpu.VMEM((prefix_len, kv_width), BF16),
        ],
        compiler_params=params(),
        cost_estimate=cost(
            4 * slots * heads * prefix_len * PAIR,
            2 * prefix_len * kv_width,
            slots * heads * prefix_len,
        ),
        name="slot_attention",
    )(slot_queries, prefix_cache)

    back = lax.all_to_all(slot_out, "replica", split_axis=0, concat_axis=0, tiled=True)

    prompt_out = finish(place, prompt_parts, swap(prompt_mixed, count), mlp_params)

    request_mixed = pl.pallas_call(
        merge_kernel,
        in_specs=[WHOLE] * 5,
        out_specs=WHOLE,
        out_shape=jax.ShapeDtypeStruct((requests, model), BF16),
        compiler_params=params(),
        cost_estimate=cost(2 * requests * width * model, 2 * width * model),
        name="merge",
    )(gather, back, past, past_sums, w_out)

    request_out = finish(place, request_parts, swap(request_mixed, count), mlp_params)
    return (prompt_out, request_out)


def solution(mesh):
    return jax.shard_map(
        body,
        mesh=mesh,
        in_specs=(
            P("replica", "tensor"),
            P("replica", "tensor"),
            P("replica", None, "tensor"),
            P("replica"),
            P("replica", None),
            P("replica", "tensor"),
            P(),
            P(None, "tensor"),
            P(None, "tensor"),
            P("tensor", None),
            P(),
            P(None, "tensor"),
            P(None, "tensor"),
            P("tensor", None),
        ),
        out_specs=(P("replica", "tensor"), P("replica", "tensor")),
        check_vma=False,
    )
```

time: 468 us -> 99.6 us (0.21); the launches traced: 462 us -> 99 us
  waiting for transfers between devices: 241 us -> 21.7 us
  local copies, waits for them, and re-layouts: 89.5 us -> 13.9 us
  matrix products: 66.2 us -> 0 us
  Pallas kernels: 0 us -> 39.7 us
  other arithmetic: 28.4 us -> 3.33 us
  between operations: 14.5 us -> 0.85 us
    all_to_all x4 -> x2, waiting for transfers between devices: 104 us -> 7.73 us  [the longest x1 7.73 us: body(): lax.all_to_all(send, 'replica', split_axis=0, concat_axis=0, tiled=True)]
    reduce_scatter x2 -> x0, waiting for transfers between devices: 84.2 us -> none  [the longest x1 58 us: tensor_layer(): lax.psum_scatter(head_terms.astype(jnp.bfloat16), 'tensor', scatter_dimen...]
    dot_general x10 -> x0, matrix products: 62.1 us -> none  [the longest x1 11.2 us: tensor_layer(): unit_terms = jnp.dot(hidden, w_down, preferred_element_type=jnp.float32)]
    all_gather x2 -> x0, waiting for transfers between devices: 52.3 us -> none  [the longest x1 27.3 us: tensor_layer(): whole_mid = lax.all_gather(residual, 'tensor', axis=1, tiled=True)]
    pallas_call x0 -> x7, Pallas kernels: none -> 39.7 us  [the longest x2 18 us: mlp(): pl.pallas_call(functools.partial(mlp_kernel, count, steps), grid=(steps,)...]
    scatter x3 -> x0, local copies, waits for them, and re-layouts: 23.1 us -> none  [the longest x1 19.4 us: body(): send_cache = jnp.zeros((slot_count,) + request_keyval_cache.shape[1:], jn...]
    unnamed x41 -> x48, local copies, waits for them, and re-layouts: 28.5 us -> 13.2 us
    ppermute x0 -> x6, waiting for transfers between devices: none -> 14 us  [the longest x4 8.84 us: swap(): return [block, lax.ppermute(block, 'tensor', [(0, 1), (1, 0)])]]
  transfers between devices with their start and end apart: 8 -> 8, of which waited for: 7 -> 4; matrix products, arithmetic and copies ran while one was open for 14% -> 3% of each run, Pallas kernels for 0% -> 39%
where the time goes in v1:
time: 99.6 us; the launch traced here: 99 us
  Pallas kernels  39.7 us (40%)
  waiting for transfers between devices  21.7 us (22%)
  starting transfers between devices  19.5 us (20%)
  local copies, waits for them, and re-layouts  13.9 us (14%)
  other arithmetic  3.33 us (3%)
    pallas_call x2, Pallas kernels, mlp(): pl.pallas_call(functools.partial(mlp_kernel, count, steps), grid=(steps,)...  18 us
    unnamed x48, local copies, waits for them, and re-layouts  13.2 us
    ppermute x4, waiting for transfers between devices, swap(): return [block, lax.ppermute(block, 'tensor', [(0, 1), (1, 0)])]  8.84 us
    all_to_all x1, waiting for transfers between devices, body(): lax.all_to_all(send, 'replica', split_axis=0, concat_axis=0, tiled=True)  7.73 us
    pallas_call x1, Pallas kernels, body(): pl.pallas_call(functools.partial(prompt_kernel, count), in_specs=[SCALAR]...  7.24 us
    ppermute x4, starting transfers between devices, swap(): return [block, lax.ppermute(block, 'tensor', [(0, 1), (1, 0)])]  6.65 us
    all_to_all x1, starting transfers between devices, body(): lax.all_to_all(send, 'replica', split_axis=0, concat_axis=0, tiled=True)  6.45 us
    pallas_call x1, Pallas kernels, body(): pl.pallas_call(slot_kernel, in_specs=[WHOLE] * 2, out_specs=WHOLE, out_sh...  6.41 us
  transfers between devices with their start and end apart: 8, of which 4 were waited for; matrix products, arithmetic and copies ran while one was open for 3% of the time, Pallas kernels for 39%

profile of v1, /device:TPU:0, one launch (start us, length us, event | category | flops | bytes accessed | tf_op | source)
XLA Modules:
  0.0 99.0 jit_solution(4081282561891658041)
XLA Ops:
  0.6 3.0 %collective-permute-start.3 = (bf16[128,1024]{1,0:T(8,128)(2,1)}, bf16[128,1024]{1,0:T(8,128)(2,1)S(1)}, u32[]{:S(2)}, u32[]{:S(2)}) collective-permute-start(bf16[128,1024]{1,0:T(8,128)(2,1)} %refs_0_.7), channel_id=1, source_target_pairs={{0,1},{1,0},{2,3},{3,2},{4,5},{5,4},{6,7},{7,6},{8,9},{9,8},{10,11... | collective-permute-start | bytes 786440 | tf_op jit(solution)/shard_map/ppermute | solution.py:287
  3.6 0.9 convert_reduce_fusion
  5.2 4.9 %collective-permute-done.3.refs_1_ = bf16[128,1024]{1,0:T(8,128)(2,1)S(1)} collective-permute-done((bf16[128,1024]{1,0:T(8,128)(2,1)}, bf16[128,1024]{1,0:T(8,128)(2,1)S(1)}, u32[]{:S(2)}, u32[]{:S(2)}) %collective-permute-start.3) | collective-permute-done | bytes 262176 | tf_op jit(solution)/shard_map/ppermute | solution.py:287
  10.2 1.6 %copy-done = bf16[2048,512]{1,0:T(8,128)(2,1)S(1)} copy-done((bf16[2048,512]{1,0:T(8,128)(2,1)S(1)}, bf16[2048,512]{1,0:T(8,128)(2,1)}, u32[]{:S(2)}) %copy-start) | copy-done | bytes 2097176
  11.7 1.2 %copy-done.4 = bf16[2048,256]{1,0:T(8,128)(2,1)S(1)} copy-done((bf16[2048,256]{1,0:T(8,128)(2,1)S(1)}, bf16[2048,256]{1,0:T(8,128)(2,1)}, u32[]{:S(2)}) %copy-start.4) | copy-done | bytes 1048600
  13.0 0.9 copy-done.8
  13.9 0.7 copy-done.20
  14.6 0.8 request_project.1
  16.2 0.7 copy-done.15
  18.1 6.4 %all-to-all-start = ((bf16[16,16,512]{2,1,0:T(8,128)(2,1)}), bf16[16,16,512]{2,1,0:T(8,128)(2,1)S(1)}, u32[]{:S(2)}, u32[]{:S(2)}) async-start(bf16[16,16,512]{2,1,0:T(8,128)(2,1)} %bitcast.19), calls=%async_computation | async-start | bytes 524288 | tf_op jit(solution)/shard_map/all_to_all | solution.py:407
  24.6 1.6 %collective-permute-start = (bf16[128,1024]{1,0:T(8,128)(2,1)}, bf16[128,1024]{1,0:T(8,128)(2,1)}, u32[]{:S(2)}, u32[]{:S(2)}) collective-permute-start(bf16[128,1024]{1,0:T(8,128)(2,1)} %refs_0_.5), channel_id=1, source_target_pairs={{0,1},{1,0},{2,3},{3,2},{4,5},{5,4},{6,7},{7,6},{8,9},{9,8},{10,11... | collective-permute-start | bytes 786440 | tf_op jit(solution)/shard_map/ppermute | solution.py:287
  26.1 0.8 copy.17.len_ref
  26.9 7.7 %all-to-all-done = bf16[16,16,512]{2,1,0:T(8,128)(2,1)S(1)} async-done(((bf16[16,16,512]{2,1,0:T(8,128)(2,1)}), bf16[16,16,512]{2,1,0:T(8,128)(2,1)S(1)}, u32[]{:S(2)}, u32[]{:S(2)}) %all-to-all-start) | async-done | bytes 262176 | tf_op jit(solution)/shard_map/all_to_all | solution.py:407
  34.6 1.2 %copy-done.12 = bf16[2048,256]{1,0:T(8,128)(2,1)S(1)} copy-done((bf16[2048,256]{1,0:T(8,128)(2,1)S(1)}, bf16[2048,256]{1,0:T(8,128)(2,1)}, u32[]{:S(2)}) %copy-start.12) | copy-done | bytes 1048600
  35.9 6.4 %slot_attention.1 = bf16[256,640]{1,0:T(8,128)(2,1)S(1)} custom-call(bf16[256,512]{1,0:T(8,128)(2,1)S(1)} %bitcast.18, bf16[2048,256]{1,0:T(8,128)(2,1)S(1)} %copy-done.12), custom_call_target="tpu_custom_call" | custom-call | flops 2147483648 | bytes 1048576 | tf_op jit(solution)/shard_map/slot_attention/pallas_call | solution.py:455
  42.3 0.7 copy-done.14
  43.0 3.7 %all-to-all-start.1 = ((bf16[16,16,640]{2,1,0:T(8,128)(2,1)}), bf16[16,16,640]{2,1,0:T(8,128)(2,1)S(1)}, u32[]{:S(2)}, u32[]{:S(2)}) async-start(bf16[16,16,640]{2,1,0:T(8,128)(2,1)} %bitcast.17), calls=%async_computation.1 | async-start | bytes 655360 | tf_op jit(solution)/shard_map/all_to_all | solution.py:473
  46.8 1.1 %copy-done.6 = bf16[128,1024]{1,0:T(8,128)(2,1)S(1)} copy-done((bf16[128,1024]{1,0:T(8,128)(2,1)S(1)}, bf16[128,1024]{1,0:T(8,128)(2,1)}, u32[]{:S(2)}) %copy-start.6) | copy-done | bytes 262168
  47.9 1.4 %copy-done.13 = bf16[2048,256]{1,0:T(8,128)(2,1)S(1)} copy-done((bf16[2048,256]{1,0:T(8,128)(2,1)S(1)}, bf16[2048,256]{1,0:T(8,128)(2,1)}, u32[]{:S(2)}) %copy-start.13) | copy-done | bytes 1048600
  49.3 7.2 %prompt_attention.1.refs_2_ = bf16[128,2048]{1,0:T(8,128)(2,1)} custom-call(s32[1]{0:T(128)} %bitcast.place_ref, bf16[128,1024]{1,0:T(8,128)(2,1)S(1)} %copy-done.6, bf16[128,1024]{1,0:T(8,128)(2,1)} %collective-permute-done.refs_1_, f32[1,2048]{1,0:T(1,128)S(1)} %bitcast.21, bf16[2048,512]{1,0:T(8,128)(2,1)S(1)} %copy-done.1, ...), custom_call_target="tpu_custom_call" | custom-call | flops 1744830464 | bytes 6291456 | tf_op jit(solution)/shard_map/prompt_attention/pallas_call | solution.py:409
  56.6 1.5 %collective-permute-start.1 = (bf16[128,2048]{1,0:T(8,128)(2,1)}, bf16[128,2048]{1,0:T(8,128)(2,1)S(1)}, u32[]{:S(2)}, u32[]{:S(2)}) collective-permute-start(bf16[128,2048]{1,0:T(8,128)(2,1)} %prompt_attention.1.refs_2_), channel_id=1, source_target_pairs={{0,1},{1,0},{2,3},{3,2},{4,5},{5,4},{6,7},{7,6},{8,9},{9,8},{10,11... | collective-permute-start | bytes 1572872 | tf_op jit(solution)/shard_map/ppermute | solution.py:287
  58.2 6.4 %past_attention.1 = (f32[128,512]{1,0:T(8,128)S(1)}, f32[128,128]{1,0:T(8,128)S(1)}) custom-call(bf16[128,512]{1,0:T(8,128)(2,1)S(1)} %copy-done.17, bf16[128,256]{1,0:T(8,128)(2,1)S(1)} %copy-done.19, s32[128,1]{1,0:T(8,128)S(1)} %copy.17.len_ref, bf16[128,64,256]{2,1,0:T(8,128)(2,1)S(1)} %copy-done.3), custom_call_target="tpu_custom_call" | custom-call | flops 1073741824 | bytes 4194304 | tf_op jit(solution)/shard_map/past_attention/pallas_call | solution.py:429
  64.6 1.6 %copy-done.2 = bf16[512,2048]{1,0:T(8,128)(2,1)S(1)} copy-done((bf16[512,2048]{1,0:T(8,128)(2,1)S(1)}, bf16[512,2048]{1,0:T(8,128)(2,1)}, u32[]{:S(2)}) %copy-start.2) | copy-done | bytes 2097176
  66.1 0.9 merge.1.refs_2_
  67.6 3.9 %collective-permute-done.1.refs_3_ = bf16[128,2048]{1,0:T(8,128)(2,1)S(1)} collective-permute-done((bf16[128,2048]{1,0:T(8,128)(2,1)}, bf16[128,2048]{1,0:T(8,128)(2,1)S(1)}, u32[]{:S(2)}, u32[]{:S(2)}) %collective-permute-start.1) | collective-permute-done | bytes 524320 | tf_op jit(solution)/shard_map/ppermute | solution.py:287
  71.6 9.3 %mlp.2 = (bf16[128,1024]{1,0:T(8,128)(2,1)S(1)}, bf16[128,1024]{1,0:T(8,128)(2,1)S(1)}, bf16[128,1024]{1,0:T(8,128)(2,1)S(1)}) custom-call(s32[1]{0:T(128)} %bitcast.place_ref, bf16[128,1024]{1,0:T(8,128)(2,1)S(1)} %copy-done.7, bf16[128,1024]{1,0:T(8,128)(2,1)} %collective-permute-done.refs_1_, bf16[128,2048]{1,0:T(8,128)(2,1)} %prompt_attention.1.refs_2_, ...), custom_call_target="tpu_custom_call" | custom-call | flops 2013265920 | bytes 15728640 | tf_op jit(solution)/shard_map/mlp/pallas_call | solution.py:306
  80.8 1.6 %collective-permute-start.2 = (bf16[128,1024]{1,0:T(8,128)(2,1)S(1)}, bf16[128,1024]{1,0:T(8,128)(2,1)S(1)}, u32[]{:S(2)}, u32[]{:S(2)}) collective-permute-start(bf16[128,1024]{1,0:T(8,128)(2,1)S(1)} %get-tuple-element.15), channel_id=1, source_target_pairs={{0,1},{1,0},{2,3},{3,2},{4,5},{5,4},{6,7},{7,6},{8,9},{9,8},{10,11... | collective-permute-start | bytes 786440 | tf_op jit(solution)/shard_map/ppermute | solution.py:333
  82.4 8.7 %mlp.3 = (bf16[128,1024]{1,0:T(8,128)(2,1)S(1)}, bf16[128,1024]{1,0:T(8,128)(2,1)S(1)}, bf16[128,1024]{1,0:T(8,128)(2,1)S(1)}) custom-call(s32[1]{0:T(128)} %bitcast.place_ref, bf16[128,1024]{1,0:T(8,128)(2,1)S(1)} %copy-done.9, bf16[128,1024]{1,0:T(8,128)(2,1)S(1)} %copy-done.11, bf16[128,2048]{1,0:T(8,128)(2,1)S(1)} %merge.1.refs_2_, ...), custom_call_target="tpu_custom_call" | custom-call | flops 2013265920 | bytes 15728640 | tf_op jit(solution)/shard_map/mlp/pallas_call | solution.py:306
  91.1 1.1 %collective-permute-start.5 = (bf16[128,1024]{1,0:T(8,128)(2,1)S(1)}, bf16[128,1024]{1,0:T(8,128)(2,1)S(1)}, u32[]{:S(2)}, u32[]{:S(2)}) collective-permute-start(bf16[128,1024]{1,0:T(8,128)(2,1)S(1)} %get-tuple-element.23), channel_id=1, source_target_pairs={{0,1},{1,0},{2,3},{3,2},{4,5},{5,4},{6,7},{7,6},{8,9},{9,8},{10,11... | collective-permute-start | bytes 786440 | tf_op jit(solution)/shard_map/ppermute | solution.py:333
  92.2 0.8 add_convert_fusion.1
  93.0 5.2 %collective-permute-done.5 = bf16[128,1024]{1,0:T(8,128)(2,1)S(1)} collective-permute-done((bf16[128,1024]{1,0:T(8,128)(2,1)S(1)}, bf16[128,1024]{1,0:T(8,128)(2,1)S(1)}, u32[]{:S(2)}, u32[]{:S(2)}) %collective-permute-start.5) | collective-permute-done | bytes 262176 | tf_op jit(solution)/shard_map/ppermute | solution.py:333
  98.2 0.8 add_convert_fusion
  (47 shorter events, 3.4 us)
Async XLA Ops:
  0.6 9.5 %collective-permute-start.3 = (bf16[128,1024]{1,0:T(8,128)(2,1)}, bf16[128,1024]{1,0:T(8,128)(2,1)S(1)}, u32[]{:S(2)}, u32[]{:S(2)}) collective-permute-start(bf16[128,1024]{1,0:T(8,128)(2,1)} %refs_0_.7), channel_id=1, source_target_pairs={{0,1},{1,0},{2,3},{3,2},{4,5},{5,4},{6,7},{7,6},{8,9},{9,8},{10,11... | collective-permute-start | bytes 786440 | tf_op jit(solution)/shard_map/ppermute | solution.py:287
  10.2 1.6 %copy-start = (bf16[2048,512]{1,0:T(8,128)(2,1)S(1)}, bf16[2048,512]{1,0:T(8,128)(2,1)}, u32[]{:S(2)}) copy-start(bf16[2048,512]{1,0:T(8,128)(2,1)} %refs_3_.3) | copy-start | bytes 6291460
  11.7 1.2 %copy-start.4 = (bf16[2048,256]{1,0:T(8,128)(2,1)S(1)}, bf16[2048,256]{1,0:T(8,128)(2,1)}, u32[]{:S(2)}) copy-start(bf16[2048,256]{1,0:T(8,128)(2,1)} %refs_4_.3) | copy-start | bytes 3145732
  13.0 0.9 copy-start.8
  13.9 0.7 copy-start.20
  14.6 32.1 %copy-start.23 = (s32[128,1]{0,1:T(1,128)S(1)}, s32[128,1]{0,1:T(1,128)}, u32[]{:S(2)}) copy-start(s32[128,1]{0,1:T(1,128)} %param.18) | copy-start | bytes 1540
  14.6 32.1 %copy-start.21 = (f32[2048]{0:T(1024)S(1)}, f32[2048]{0:T(1024)}, u32[]{:S(2)}) copy-start(f32[2048]{0:T(1024)} %param.20) | copy-start | bytes 24580
  15.4 0.7 copy-start.10
  16.1 0.7 copy-start.15
  16.9 0.6 copy-start.16
  17.5 0.6 copy-start.18
  18.1 28.7 %copy-start.1 = (bf16[2048,512]{1,0:T(8,128)(2,1)S(1)}, bf16[2048,512]{1,0:T(8,128)(2,1)}, u32[]{:S(2)}) copy-start(bf16[2048,512]{1,0:T(8,128)(2,1)} %refs_3_.3) | copy-start | bytes 6291460
  18.1 28.7 %copy-start.5 = (bf16[2048,256]{1,0:T(8,128)(2,1)S(1)}, bf16[2048,256]{1,0:T(8,128)(2,1)}, u32[]{:S(2)}) copy-start(bf16[2048,256]{1,0:T(8,128)(2,1)} %refs_4_.3) | copy-start | bytes 3145732
  18.1 16.5 %all-to-all-start = ((bf16[16,16,512]{2,1,0:T(8,128)(2,1)}), bf16[16,16,512]{2,1,0:T(8,128)(2,1)S(1)}, u32[]{:S(2)}, u32[]{:S(2)}) async-start(bf16[16,16,512]{2,1,0:T(8,128)(2,1)} %bitcast.19), calls=%async_computation | async-start | bytes 524288 | tf_op jit(solution)/shard_map/all_to_all | solution.py:407
  24.6 22.2 %collective-permute-start = (bf16[128,1024]{1,0:T(8,128)(2,1)}, bf16[128,1024]{1,0:T(8,128)(2,1)}, u32[]{:S(2)}, u32[]{:S(2)}) collective-permute-start(bf16[128,1024]{1,0:T(8,128)(2,1)} %refs_0_.5), channel_id=1, source_target_pairs={{0,1},{1,0},{2,3},{3,2},{4,5},{5,4},{6,7},{7,6},{8,9},{9,8},{10,11... | collective-permute-start | bytes 786440 | tf_op jit(solution)/shard_map/ppermute | solution.py:287
  34.6 1.2 %copy-start.12 = (bf16[2048,256]{1,0:T(8,128)(2,1)S(1)}, bf16[2048,256]{1,0:T(8,128)(2,1)}, u32[]{:S(2)}) copy-start(bf16[2048,256]{1,0:T(8,128)(2,1)} %prefix_ref.1) | copy-start | bytes 3145732
  42.3 0.7 copy-start.14
  43.0 21.6 %all-to-all-start.1 = ((bf16[16,16,640]{2,1,0:T(8,128)(2,1)}), bf16[16,16,640]{2,1,0:T(8,128)(2,1)S(1)}, u32[]{:S(2)}, u32[]{:S(2)}) async-start(bf16[16,16,640]{2,1,0:T(8,128)(2,1)} %bitcast.17), calls=%async_computation.1 | async-start | bytes 655360 | tf_op jit(solution)/shard_map/all_to_all | solution.py:473
  46.7 11.4 %copy-start.3 = (bf16[128,64,256]{2,1,0:T(8,128)(2,1)S(1)}, bf16[128,64,256]{2,1,0:T(8,128)(2,1)}, u32[]{:S(2)}) copy-start(bf16[128,64,256]{2,1,0:T(8,128)(2,1)} %cache_ref.1) | copy-start | bytes 12582916
  46.8 1.1 %copy-start.6 = (bf16[128,1024]{1,0:T(8,128)(2,1)S(1)}, bf16[128,1024]{1,0:T(8,128)(2,1)}, u32[]{:S(2)}) copy-start(bf16[128,1024]{1,0:T(8,128)(2,1)} %refs_0_.5) | copy-start | bytes 786436
  47.9 1.4 %copy-start.13 = (bf16[2048,256]{1,0:T(8,128)(2,1)S(1)}, bf16[2048,256]{1,0:T(8,128)(2,1)}, u32[]{:S(2)}) copy-start(bf16[2048,256]{1,0:T(8,128)(2,1)} %prefix_ref.1) | copy-start | bytes 3145732
  49.3 8.9 %copy-start.17 = (bf16[128,512]{1,0:T(8,128)(2,1)S(1)}, bf16[128,512]{1,0:T(8,128)(2,1)}, u32[]{:S(2)}) copy-start(bf16[128,512]{1,0:T(8,128)(2,1)} %copy-done.16) | copy-start | bytes 393220
  49.3 8.9 %copy-start.19 = (bf16[128,256]{1,0:T(8,128)(2,1)S(1)}, bf16[128,256]{1,0:T(8,128)(2,1)}, u32[]{:S(2)}) copy-start(bf16[128,256]{1,0:T(8,128)(2,1)} %copy-done.18) | copy-start | bytes 196612
  56.5 15.0 %copy-start.7 = (bf16[128,1024]{1,0:T(8,128)(2,1)S(1)}, bf16[128,1024]{1,0:T(8,128)(2,1)}, u32[]{:S(2)}) copy-start(bf16[128,1024]{1,0:T(8,128)(2,1)} %refs_0_.5) | copy-start | bytes 786436
  56.5 15.0 %copy-start.22 = (f32[2048]{0:T(1024)S(1)}, f32[2048]{0:T(1024)}, u32[]{:S(2)}) copy-start(f32[2048]{0:T(1024)} %param.24) | copy-start | bytes 24580
  56.6 15.0 %collective-permute-start.1 = (bf16[128,2048]{1,0:T(8,128)(2,1)}, bf16[128,2048]{1,0:T(8,128)(2,1)S(1)}, u32[]{:S(2)}, u32[]{:S(2)}) collective-permute-start(bf16[128,2048]{1,0:T(8,128)(2,1)} %prompt_attention.1.refs_2_), channel_id=1, source_target_pairs={{0,1},{1,0},{2,3},{3,2},{4,5},{5,4},{6,7},{7,6},{8,9},{9,8},{10,11... | collective-permute-start | bytes 1572872 | tf_op jit(solution)/shard_map/ppermute | solution.py:287
  64.6 1.6 %copy-start.2 = (bf16[512,2048]{1,0:T(8,128)(2,1)S(1)}, bf16[512,2048]{1,0:T(8,128)(2,1)}, u32[]{:S(2)}) copy-start(bf16[512,2048]{1,0:T(8,128)(2,1)} %w_out_ref.1) | copy-start | bytes 6291460
  67.0 15.4 %collective-permute-start.4 = (bf16[128,2048]{1,0:T(8,128)(2,1)S(1)}, bf16[128,2048]{1,0:T(8,128)(2,1)S(1)}, u32[]{:S(2)}, u32[]{:S(2)}) collective-permute-start(bf16[128,2048]{1,0:T(8,128)(2,1)S(1)} %merge.1.refs_2_), channel_id=1, source_target_pairs={{0,1},{1,0},{2,3},{3,2},{4,5},{5,4},{6,7},{7,6},{8,9},{9,8},{10,11... | collective-permute-start | bytes 1572872 | tf_op jit(solution)/shard_map/ppermute | solution.py:287
  71.5 10.9 %copy-start.9 = (bf16[128,1024]{1,0:T(8,128)(2,1)S(1)}, bf16[128,1024]{1,0:T(8,128)(2,1)}, u32[]{:S(2)}) copy-start(bf16[128,1024]{1,0:T(8,128)(2,1)} %refs_0_.7) | copy-start | bytes 786436
  71.5 10.9 %copy-start.11 = (bf16[128,1024]{1,0:T(8,128)(2,1)S(1)}, bf16[128,1024]{1,0:T(8,128)(2,1)}, u32[]{:S(2)}) copy-start(bf16[128,1024]{1,0:T(8,128)(2,1)} %copy-done.10) | copy-start | bytes 786436
  80.8 11.4 %collective-permute-start.2 = (bf16[128,1024]{1,0:T(8,128)(2,1)S(1)}, bf16[128,1024]{1,0:T(8,128)(2,1)S(1)}, u32[]{:S(2)}, u32[]{:S(2)}) collective-permute-start(bf16[128,1024]{1,0:T(8,128)(2,1)S(1)} %get-tuple-element.15), channel_id=1, source_target_pairs={{0,1},{1,0},{2,3},{3,2},{4,5},{5,4},{6,7},{7,6},{8,9},{9,8},{10,11... | collective-permute-start | bytes 786440 | tf_op jit(solution)/shard_map/ppermute | solution.py:333
  91.1 7.0 %collective-permute-start.5 = (bf16[128,1024]{1,0:T(8,128)(2,1)S(1)}, bf16[128,1024]{1,0:T(8,128)(2,1)S(1)}, u32[]{:S(2)}, u32[]{:S(2)}) collective-permute-start(bf16[128,1024]{1,0:T(8,128)(2,1)S(1)} %get-tuple-element.23), channel_id=1, source_target_pairs={{0,1},{1,0},{2,3},{3,2},{4,5},{5,4},{6,7},{7,6},{8,9},{9,8},{10,11... | collective-permute-start | bytes 786440 | tf_op jit(solution)/shard_map/ppermute | solution.py:333

commit v2 on v1

v2 whole, which is shorter than its diff:
```python
import functools
import math

import jax
import jax.numpy as jnp
from jax import lax
from jax.experimental import pallas as pl
from jax.experimental.pallas import tpu as pltpu
from jax.sharding import PartitionSpec as P

HEAD_SIZE = 64
QUERIES_PER_KEY = 4
PAIR = 2 * HEAD_SIZE
GROUP = 8
CHUNK = 256
EPS = 1e-05
FACTOR = HEAD_SIZE ** (-0.5) * math.log2(math.e)
F32 = jnp.float32
BF16 = jnp.bfloat16
MIB = 1024 * 1024
MOST_VMEM = 62 * MIB
ANY = pl.BlockSpec(memory_space=pl.ANY)
HBM = pl.BlockSpec(memory_space=pltpu.HBM)
SCALAR = pl.BlockSpec(memory_space=pltpu.SMEM)


def params(limit=MOST_VMEM):
    return pltpu.CompilerParams(vmem_limit_bytes=limit)


def cost(flops, read, exps=0):
    return pl.CostEstimate(flops=int(flops), bytes_accessed=int(read), transcendentals=int(exps))


def lane_ids(shape):
    return lax.broadcasted_iota(jnp.int32, shape, len(shape) - 1)


def rms_norm(values, gain_row):
    inv_scale = lax.rsqrt(jnp.mean(values * values, axis=1, keepdims=True) + EPS)
    return (values * inv_scale * gain_row).astype(BF16)


def in_order(place_ref, parts):
    if len(parts) == 2:
        first = place_ref[0] == 0
        own, other = parts
        parts = (jnp.where(first, own, other), jnp.where(first, other, own))
    return jnp.concatenate(parts, axis=1)


def column_of(row):
    shape = (row.shape[1], row.shape[1])
    rows = lax.broadcasted_iota(jnp.int32, shape, 0)
    return jnp.sum(
        jnp.where(rows == lane_ids(shape), jnp.broadcast_to(row, shape), 0), axis=1, keepdims=True
    )


def slot_places(target_row, per_peer):
    count = target_row.shape[1]
    target_column = column_of(target_row)
    shape = (count, count)
    rows, columns = lax.broadcasted_iota(jnp.int32, shape, 0), lane_ids(shape)
    same = (target_column == target_row).astype(jnp.int32)
    column = target_column * per_peer + jnp.sum(
        jnp.where(columns < rows, same, 0), axis=1, keepdims=True
    )
    row = target_row * per_peer + jnp.sum(
        jnp.where(rows < columns, same, 0), axis=0, keepdims=True
    )
    return column, row


def head_query(queries, head):
    pair = head // 2
    block = queries[:, pair * PAIR : (pair + 1) * PAIR].astype(F32)
    if head % 2:
        block = pltpu.roll(block, HEAD_SIZE, 1)
    return jnp.where(lane_ids(block.shape) < HEAD_SIZE, block, 0.0).astype(BF16)


def ones_for_keys(keyval):
    key_half = lane_ids(keyval.shape) % PAIR < HEAD_SIZE
    return jnp.where(key_half, 1.0, keyval.astype(F32)).astype(BF16)


def scores_of(query_rows, key_rows):
    return lax.dot_general(
        query_rows, key_rows, (((1,), (1,)), ((), ())), preferred_element_type=F32
    )


def pack_pair(even, odd):
    even = even / pltpu.roll(even, HEAD_SIZE, 1)
    odd = odd / pltpu.roll(odd, HEAD_SIZE, 1)
    return jnp.where(
        lane_ids(even.shape) < HEAD_SIZE, pltpu.roll(even, HEAD_SIZE, 1), odd
    )


class Copies:
    def __init__(self, sems):
        self.sems = sems
        self.used = 0
        self.flying = []

    def start(self, source, target):
        copy = pltpu.make_async_copy(source, target, self.sems.at[self.used])
        copy.start()
        self.used += 1
        self.flying.append(copy)
        return copy

    def wait(self):
        for copy in self.flying:
            copy.wait()
        self.flying = []


def fetch(refs, targets, sems):
    copies = Copies(sems)
    for ref, target in zip(refs, targets):
        copies.start(ref, target)
    started, copies.flying = copies.flying, []
    return copies, started


def scratch_like(*arrays):
    return [pltpu.VMEM(x.shape, x.dtype) for x in arrays]


def request_kernel(count, per_peer, place_ref, *refs):
    inputs = count + 6
    sources, (send_ref, past_ref, sum_ref), refs = refs[:inputs], refs[inputs : inputs + 3], refs[inputs + 3 :]
    held, (send_scr, past_scr, sum_scr), refs = refs[:inputs], refs[inputs : inputs + 3], refs[inputs + 3 :]
    q_scr, score_scr, weight_scr, mixed_scr, sems = refs
    copies, started = fetch(sources, held, sems)
    gain_ref, target_ref, w_query_ref, len_ref, keyval_weight_ref, cache_ref = held[count:]
    requests, cached, kv_width = cache_ref.shape
    groups = requests // GROUP
    keys = GROUP * cached
    for copy in started[: count + 2]:
        copy.wait()
    _, slot_row = slot_places(target_ref[...], per_peer)
    spread = lax.broadcasted_iota(jnp.int32, (send_scr.shape[0], requests), 0) == slot_row
    rows = in_order(place_ref, [ref[...] for ref in held[:count]])
    normed = rms_norm(rows.astype(F32), gain_ref[...])
    started[count + 2].wait()
    queries = jnp.dot(normed, w_query_ref[...], preferred_element_type=F32).astype(BF16)
    send_scr[...] = jnp.dot(
        spread.astype(BF16), queries, preferred_element_type=F32
    ).astype(BF16)
    copies.start(send_scr, send_ref)
    started[count + 3].wait()
    started[count + 4].wait()
    keyval = jnp.dot(normed, keyval_weight_ref[...], preferred_element_type=F32).astype(BF16)
    heads = queries.shape[1] // HEAD_SIZE
    block_rows = heads * GROUP
    q_scr[...] = jnp.zeros_like(q_scr)
    for head in range(heads):
        at = head // QUERIES_PER_KEY * PAIR
        q_scr[:, head * GROUP : (head + 1) * GROUP, at : at + PAIR] = (
            head_query(queries, head).astype(F32).reshape(groups, GROUP, PAIR)
        )
    own = jnp.broadcast_to(
        keyval.astype(F32).reshape(groups, 1, GROUP, kv_width), (groups, heads, GROUP, kv_width)
    ).reshape(groups * block_rows, kv_width)
    own_scores = jnp.sum(
        q_scr[...].reshape(groups * block_rows, kv_width) * own, axis=1, keepdims=True
    )
    owner = lax.broadcasted_iota(jnp.int32, (block_rows, keys), 0) % GROUP
    columns = lane_ids((block_rows, keys))
    position = jnp.where(columns // cached == owner, columns % cached, cached)
    lengths = column_of(len_ref[...])
    started[count + 5].wait()
    for group in range(groups):
        block = cache_ref[group * GROUP : (group + 1) * GROUP].reshape(keys, kv_width)
        live = position < jnp.concatenate(
            [lengths[group * GROUP : (group + 1) * GROUP]] * heads, axis=0
        )
        score_scr[group] = jnp.where(
            live, scores_of(q_scr[group].astype(BF16), block), -jnp.inf
        )
    scores = score_scr[...].reshape(groups * block_rows, keys)
    row_max = jnp.maximum(jnp.max(scores, axis=1, keepdims=True), own_scores)
    exp_vals = jnp.exp2((scores - row_max) * FACTOR)
    own_exp = jnp.exp2((own_scores - row_max) * FACTOR)
    weight_scr[...] = exp_vals.astype(BF16).reshape(groups, block_rows, keys)
    total = jnp.sum(exp_vals, axis=1, keepdims=True) + own_exp
    log_sum = (row_max * FACTOR + jnp.log2(total)).reshape(groups, block_rows, 1)
    for group in range(groups):
        block = cache_ref[group * GROUP : (group + 1) * GROUP].reshape(keys, kv_width)
        mixed_scr[group] = jnp.dot(weight_scr[group], block, preferred_element_type=F32)
    mixed = mixed_scr[...].reshape(groups * block_rows, kv_width)
    mixed = (mixed + own_exp.astype(BF16).astype(F32) * own) * (1.0 / total)
    mixed = mixed.reshape(groups, block_rows, kv_width)
    lanes = lane_ids((requests, PAIR))
    sums = jnp.zeros((requests, PAIR), F32)
    done = []
    for head in range(heads):
        at = head // QUERIES_PER_KEY * PAIR
        rows_of = slice(head * GROUP, (head + 1) * GROUP)
        done.append(mixed[:, rows_of, at : at + PAIR].reshape(requests, PAIR))
        sums = jnp.where(lanes == head, log_sum[:, rows_of].reshape(requests, 1), sums)
    for pair in range(heads // 2):
        past_scr[:, pair * PAIR : (pair + 1) * PAIR] = jnp.where(
            lanes < HEAD_SIZE, pltpu.roll(done[2 * pair], HEAD_SIZE, 1), done[2 * pair + 1]
        )
    sum_scr[...] = sums
    copies.start(past_scr, past_ref)
    copies.start(sum_scr, sum_ref)
    copies.wait()


def prompt_kernel(count, place_ref, *refs):
    inputs = count + 4
    sources, att_ref, refs = refs[:inputs], refs[inputs], refs[inputs + 1 :]
    held, (q_scr, kvx_scr, att_scr, sems) = refs[:inputs], refs[inputs:]
    copies, started = fetch(sources, held, sems)
    for copy in started[: count + 1]:
        copy.wait()
    gain_ref, w_query_ref, keyval_weight_ref, prefix_ref = held[count:]
    rows = in_order(place_ref, [ref[...] for ref in held[:count]])
    normed = rms_norm(rows.astype(F32), gain_ref[...])
    started[count + 1].wait()
    queries = jnp.dot(normed, w_query_ref[...], preferred_element_type=F32).astype(BF16)
    started[count + 2].wait()
    keyval = jnp.dot(normed, keyval_weight_ref[...], preferred_element_type=F32).astype(BF16)
    started[count + 3].wait()
    heads = queries.shape[1] // HEAD_SIZE
    row_count = queries.shape[0]
    for head in range(heads):
        q_scr[head] = head_query(queries, head)
    kvx_scr[...] = ones_for_keys(prefix_ref[...])
    own_ones = ones_for_keys(keyval)
    row_ids = lax.broadcasted_iota(jnp.int32, (2 * row_count, row_count), 0) % row_count
    visible = lax.broadcasted_iota(jnp.int32, (2 * row_count, row_count), 1) <= row_ids
    for kv in range(heads // QUERIES_PER_KEY):
        columns = slice(kv * PAIR, (kv + 1) * PAIR)
        own_keys = keyval[:, columns]
        own_values = own_ones[:, columns]
        for half in range(QUERIES_PER_KEY // 2):
            pair = kv * (QUERIES_PER_KEY // 2) + half
            query_rows = q_scr[pl.ds(2 * pair, 2)].reshape(2 * row_count, PAIR)
            past = scores_of(query_rows, prefix_ref[:, columns])
            own = jnp.where(visible, scores_of(query_rows, own_keys), -jnp.inf)
            row_max = jnp.maximum(
                jnp.max(past, axis=1, keepdims=True), jnp.max(own, axis=1, keepdims=True)
            )
            past_exp = jnp.exp2((past - row_max) * FACTOR).astype(BF16)
            own_exp = jnp.exp2((own - row_max) * FACTOR).astype(BF16)
            total = jnp.dot(past_exp, kvx_scr[:, columns], preferred_element_type=F32)
            total = total + jnp.dot(own_exp, own_values, preferred_element_type=F32)
            att_scr[:, pair * PAIR : (pair + 1) * PAIR] = pack_pair(
                total[:row_count], total[row_count:]
            ).astype(BF16)
    copies.start(att_scr, att_ref)
    copies.wait()


def slot_kernel(q_hbm, prefix_hbm, out_hbm, q_ref, prefix_ref, out_ref, q_scr, kvx_scr, sems):
    copies, started = fetch((q_hbm, prefix_hbm), (q_ref, prefix_ref), sems)
    started[0].wait()
    slots, width = q_ref.shape
    heads = width // HEAD_SIZE
    queries = q_ref[...]
    for head in range(heads):
        q_scr[head] = head_query(queries, head)
    started[1].wait()
    kvx_scr[...] = ones_for_keys(prefix_ref[...])
    lanes = lane_ids((slots, PAIR))
    sums = jnp.zeros((slots, PAIR), F32)
    for kv in range(heads // QUERIES_PER_KEY):
        columns = slice(kv * PAIR, (kv + 1) * PAIR)
        for half in range(QUERIES_PER_KEY // 2):
            pair = kv * (QUERIES_PER_KEY // 2) + half
            totals = []
            for head in (2 * pair, 2 * pair + 1):
                scores = scores_of(q_scr[head], prefix_ref[:, columns])
                row_max = jnp.max(scores, axis=1, keepdims=True)
                exp_vals = jnp.exp2((scores - row_max) * FACTOR).astype(BF16)
                total = jnp.dot(exp_vals, kvx_scr[:, columns], preferred_element_type=F32)
                totals.append(total)
                log_sum = row_max * FACTOR + jnp.log2(total)
                high = log_sum.astype(BF16).astype(F32)
                middle = (log_sum - high).astype(BF16).astype(F32)
                low = log_sum - high - middle
                for place, part in enumerate((high, middle, low)):
                    sums = jnp.where(lanes == 3 * head + place, part, sums)
            out_ref[:, pair * PAIR : (pair + 1) * PAIR] = pack_pair(*totals).astype(BF16)
    out_ref[:, width:] = sums.astype(BF16)
    copies.start(out_ref, out_hbm)
    copies.wait()


def merge_kernel(per_peer, *refs):
    sources, att_ref, held, (att_scr, sems) = refs[:4], refs[4], refs[5:9], refs[9:]
    copies, started = fetch(sources, held, sems)
    target_ref, back_ref, past_ref, sum_ref = held
    for copy in started:
        copy.wait()
    slot_column, _ = slot_places(target_ref[...], per_peer)
    gather = lane_ids((slot_column.shape[0], back_ref.shape[0])) == slot_column
    width = past_ref.shape[1]
    heads = width // HEAD_SIZE
    prefix = jnp.dot(gather.astype(BF16), back_ref[...], preferred_element_type=F32)
    prefix_sums = prefix[:, width:]
    past_sums = sum_ref[...]
    lanes = lane_ids(past_sums.shape)
    shares = []
    for head in range(heads):
        prefix_log = jnp.sum(
            jnp.where(lanes // 3 == head, prefix_sums, 0.0), axis=1, keepdims=True
        )
        past_log = jnp.sum(jnp.where(lanes == head, past_sums, 0.0), axis=1, keepdims=True)
        top = jnp.maximum(prefix_log, past_log)
        prefix_part = jnp.exp2(prefix_log - top)
        past_part = jnp.exp2(past_log - top)
        both = prefix_part + past_part
        shares.append((prefix_part / both, past_part / both))
    for pair in range(heads // 2):
        at = slice(pair * PAIR, (pair + 1) * PAIR)
        key_half = lanes < HEAD_SIZE
        prefix_share = jnp.where(key_half, shares[2 * pair][0], shares[2 * pair + 1][0])
        past_share = jnp.where(key_half, shares[2 * pair][1], shares[2 * pair + 1][1])
        att_scr[:, at] = (prefix_share * prefix[:, at] + past_share * past_ref[:, at]).astype(BF16)
    copies.start(att_scr, att_ref)
    copies.wait()


def mlp_kernel(count, blocks, place_ref, *refs):
    inputs = 2 * count + 1
    groups = count
    weight_count = groups + 3
    sources, refs = refs[:inputs], refs[inputs:]
    weight_refs, refs = refs[: blocks + 3], refs[blocks + 3 :]
    outs = 3 if count == 2 else 2
    out_refs, held_refs, refs = refs[:outs], refs[outs : outs + weight_count], refs[outs + weight_count :]
    held, out_scr, sems = refs[:inputs], refs[inputs : inputs + outs], refs[inputs + outs]
    copies, started = fetch(sources, held, sems)
    w_outs, (w_gate, w_up, w_down) = held_refs[:groups], held_refs[groups:]
    hidden_width = w_gate.shape[1]
    chunks = [
        pl.ds(start, min(CHUNK, hidden_width - start)) for start in range(0, hidden_width, CHUNK)
    ]
    if blocks == groups:
        outs_in = [[copies.start(weight_refs[i], w_outs[i])] for i in range(groups)]
    else:
        half = weight_refs[1].shape[0]
        odd = place_ref[1]
        outs_in = [
            [copies.start(weight_refs[0], w_outs[0])],
            [
                copies.start(weight_refs[1 + i], w_outs[1].at[pl.ds(start, half)])
                for i, start in enumerate(
                    (
                        2 * odd * half,
                        (2 * odd + 1) * half,
                        2 * (1 - odd) * half,
                        (2 * (1 - odd) + 1) * half,
                    )
                )
            ],
        ]
    weight_refs = weight_refs[blocks:]
    columns = [
        [
            copies.start(weight_refs[i].at[:, at], (w_gate, w_up)[i].at[:, at])
            for i in range(2)
        ]
        for at in chunks
    ]
    downs = [copies.start(weight_refs[2].at[at], w_down.at[at]) for at in chunks]
    copies.flying = []
    for copy in started:
        copy.wait()
    rows = in_order(place_ref, [ref[...] for ref in held[:count]]).astype(F32)
    width = rows.shape[1] // count
    mixed = None
    for i in range(groups):
        for copy in outs_in[i]:
            copy.wait()
        term = jnp.dot(held[count + i][...], w_outs[i][...], preferred_element_type=F32)
        term = term.astype(BF16).astype(F32)
        mixed = term if mixed is None else mixed + term
    residual = (rows + mixed).astype(BF16)
    normed = rms_norm(residual.astype(F32), held[2 * count][...])
    if count == 2:
        first = place_ref[0] == 0
        out_scr[2][...] = jnp.where(first, residual[:, :width], residual[:, width:])
        copies.start(out_scr[2], out_refs[2])
    else:
        out_scr[1][...] = residual
        copies.start(out_scr[1], out_refs[1])
    hidden = []
    for i, at in enumerate(chunks):
        columns[i][0].wait()
        columns[i][1].wait()
        gate_act = jnp.dot(normed, w_gate[:, at], preferred_element_type=F32)
        up_act = jnp.dot(normed, w_up[:, at], preferred_element_type=F32)
        hidden.append((gate_act / (1.0 + jnp.exp(-gate_act)) * up_act).astype(BF16))
    for copy in downs:
        copy.wait()
    hidden = jnp.concatenate(hidden, axis=1)
    terms = jnp.dot(hidden, w_down[...], preferred_element_type=F32).astype(BF16)
    if count == 2:
        out_scr[0][...] = jnp.where(first, terms[:, :width], terms[:, width:])
        out_scr[1][...] = jnp.where(first, terms[:, width:], terms[:, :width])
        copies.start(out_scr[0], out_refs[0])
        copies.start(out_scr[1], out_refs[1])
    else:
        out_scr[0][...] = terms
        copies.start(out_scr[0], out_refs[0])
    copies.wait()


def swap(block, count):
    if count == 2:
        return [block, lax.ppermute(block, "tensor", [(0, 1), (1, 0)])]
    if count == 1:
        return [block]
    gathered = lax.all_gather(block, "tensor", axis=0, tiled=False)
    return [gathered[i] for i in range(count)]


def share_rows(block, count, replicas, after):
    if count != 2 or replicas % 2:
        return swap(block, count), after
    half = block.shape[0] // 2
    odd = lax.axis_index("replica") % 2
    mine = lax.dynamic_slice_in_dim(block, odd * half, half, axis=0)
    pieces = (mine[: half // 2], mine[half // 2 :])
    pieces, after = lax.optimization_barrier((pieces, after))
    return [lax.ppermute(piece, "tensor", [(0, 1), (1, 0)]) for piece in pieces], after


def pass_rows(fetched, replicas):
    return lax.ppermute(fetched, "replica", [(i, i ^ 1) for i in range(replicas)])


def finish(place, parts, attended, gain, w_outs, *weights):
    count = len(parts)
    rows = parts[0].shape[0]
    model = sum(part.shape[1] for part in parts)
    hidden = weights[-1].shape[0]
    width = model // count
    if count == 2:
        outs = [jax.ShapeDtypeStruct((rows, width), BF16)] * 3
    else:
        outs = [jax.ShapeDtypeStruct((rows, model), BF16)] * 2
    operands = (*parts, *attended, gain)
    copies = len(operands) + len(w_outs) + 3 * (-(-hidden // CHUNK)) + len(outs)
    held = [pltpu.VMEM(w.shape, w.dtype) for w in [w_outs[0]] * count + list(weights)]
    return pl.pallas_call(
        functools.partial(mlp_kernel, count, len(w_outs)),
        in_specs=[SCALAR] + [ANY] * (len(operands) + len(w_outs) + len(weights)),
        out_specs=[HBM] * len(outs),
        out_shape=outs,
        scratch_shapes=held
        + scratch_like(*operands, *outs)
        + [pltpu.SemaphoreType.DMA((copies,))],
        compiler_params=params(),
        cost_estimate=cost(6 * rows * model * hidden, 6 * model * hidden, rows * hidden),
        name="mlp",
    )(place, *operands, *w_outs, *weights)


def exchange(terms, count):
    if count == 2:
        keep, send, residual = terms
        other = lax.ppermute(send, "tensor", [(0, 1), (1, 0)])
        summed = keep.astype(F32) + other.astype(F32)
        return (residual.astype(F32) + summed).astype(BF16)
    terms, residual = terms
    width = terms.shape[1] // count
    summed = lax.psum_scatter(terms.astype(F32), "tensor", scatter_dimension=1, tiled=True)
    own = lax.dynamic_slice_in_dim(residual, lax.axis_index("tensor") * width, width, axis=1)
    return (own.astype(F32) + summed).astype(BF16)


def body(
    prompt_rows,
    request_rows,
    request_keyval_cache,
    cache_len,
    destination,
    prefix_cache,
    attn_gain,
    w_query,
    keyval_weight,
    w_out,
    mlp_gain,
    w_gate,
    w_up,
    w_down,
):
    count = lax.axis_size("tensor")
    replicas = lax.axis_size("replica")
    place = jnp.stack((lax.axis_index("tensor"), lax.axis_index("replica") % 2)).astype(jnp.int32)
    requests = request_rows.shape[0]
    prompts = prompt_rows.shape[0]
    model = w_query.shape[0]
    width = w_query.shape[1]
    kv_width = keyval_weight.shape[1]
    heads = width // HEAD_SIZE
    prefix_len = prefix_cache.shape[0]
    attn_gain = attn_gain.reshape(1, model)
    mlp_gain = mlp_gain.reshape(1, model)

    request_parts = swap(request_rows, count)

    per_peer = 2 * requests // replicas
    slots = replicas * per_peer
    target = destination.reshape(1, requests)
    cached = request_keyval_cache.shape[1]
    w_outs, prompt_rows = share_rows(w_out, count, replicas, prompt_rows)
    prompt_parts = swap(prompt_rows, count)
    outs = [
        jax.ShapeDtypeStruct((slots, width), BF16),
        jax.ShapeDtypeStruct((requests, width), F32),
        jax.ShapeDtypeStruct((requests, PAIR), F32),
    ]
    operands = (
        *request_parts,
        attn_gain,
        target,
        w_query,
        cache_len.reshape(1, requests),
        keyval_weight,
        request_keyval_cache,
    )
    blocks = (requests // GROUP, heads * GROUP)
    send, past, past_sums = pl.pallas_call(
        functools.partial(request_kernel, count, per_peer),
        in_specs=[SCALAR] + [ANY] * len(operands),
        out_specs=[HBM] * 3,
        out_shape=outs,
        scratch_shapes=scratch_like(*operands, *outs)
        + [
            pltpu.VMEM((*blocks, kv_width), F32),
            pltpu.VMEM((*blocks, GROUP * cached), F32),
            pltpu.VMEM((*blocks, GROUP * cached), BF16),
            pltpu.VMEM((*blocks, kv_width), F32),
            pltpu.SemaphoreType.DMA((len(operands) + 3,)),
        ],
        compiler_params=params(),
        cost_estimate=cost(
            2 * requests * model * (width + kv_width), 2 * model * (width + kv_width)
        ),
        name="request_project",
    )(place, *operands)

    send, prompt_parts[-1], past, past_sums = lax.optimization_barrier(
        (send, prompt_parts[-1], past, past_sums)
    )
    slot_queries = lax.all_to_all(send, "replica", split_axis=0, concat_axis=0, tiled=True)

    operands = (*prompt_parts, attn_gain, w_query, keyval_weight, prefix_cache)
    prompt_attended = pl.pallas_call(
        functools.partial(prompt_kernel, count),
        in_specs=[SCALAR] + [ANY] * count + [HBM] * 4,
        out_specs=HBM,
        out_shape=jax.ShapeDtypeStruct((prompts, width), BF16),
        scratch_shapes=scratch_like(*operands)
        + [
            pltpu.VMEM((heads, prompts, PAIR), BF16),
            pltpu.VMEM((prefix_len, kv_width), BF16),
            pltpu.VMEM((prompts, width), BF16),
            pltpu.SemaphoreType.DMA((len(operands) + 1,)),
        ],
        compiler_params=params(),
        cost_estimate=cost(
            2 * prompts * model * (width + kv_width) + 4 * prompts * heads * prefix_len * PAIR,
            2 * model * (width + kv_width) + 2 * prefix_len * kv_width,
            prompts * heads * prefix_len,
        ),
        name="prompt_attention",
    )(place, *operands)

    prompt_attended = swap(prompt_attended, count)
    slot_queries, prompt_attended[0], w_outs[0] = lax.optimization_barrier(
        (slot_queries, prompt_attended[0], w_outs[0])
    )
    passed = [pass_rows(w_outs[0], replicas)] if count == 2 else []
    slot_out = pl.pallas_call(
        slot_kernel,
        in_specs=[ANY, HBM],
        out_specs=HBM,
        out_shape=jax.ShapeDtypeStruct((slots, width + PAIR), BF16),
        scratch_shapes=scratch_like(slot_queries, prefix_cache)
        + [
            pltpu.VMEM((slots, width + PAIR), BF16),
            pltpu.VMEM((heads, slots, PAIR), BF16),
            pltpu.VMEM((prefix_len, kv_width), BF16),
            pltpu.SemaphoreType.DMA((3,)),
        ],
        compiler_params=params(),
        cost_estimate=cost(
            4 * slots * heads * prefix_len * PAIR,
            2 * prefix_len * kv_width,
            slots * heads * prefix_len,
        ),
        name="slot_attention",
    )(slot_queries, prefix_cache)

    slot_out, w_outs, prompt_attended = lax.optimization_barrier(
        (slot_out, w_outs, prompt_attended)
    )
    if count == 2:
        w_outs = [w_out, *w_outs, *passed, pass_rows(w_outs[1], replicas)]
    back = lax.all_to_all(slot_out, "replica", split_axis=0, concat_axis=0, tiled=True)

    weights = (mlp_gain, w_outs, w_gate, w_up, w_down)
    prompt_terms = finish(place, prompt_parts, prompt_attended, *weights)
    back, prompt_terms = lax.optimization_barrier((back, prompt_terms))
    operands = (target, back, past, past_sums)
    request_attended = pl.pallas_call(
        functools.partial(merge_kernel, per_peer),
        in_specs=[ANY] * len(operands),
        out_specs=HBM,
        out_shape=jax.ShapeDtypeStruct((requests, width), BF16),
        scratch_shapes=scratch_like(*operands)
        + [pltpu.VMEM((requests, width), BF16), pltpu.SemaphoreType.DMA((5,))],
        compiler_params=params(),
        cost_estimate=cost(4 * requests * slots * width, 4 * slots * width),
        name="merge",
    )(*operands)

    request_terms = finish(place, request_parts, swap(request_attended, count), *weights)
    return (exchange(prompt_terms, count), exchange(request_terms, count))


def solution(mesh):
    return jax.shard_map(
        body,
        mesh=mesh,
        in_specs=(
            P("replica", "tensor"),
            P("replica", "tensor"),
            P("replica", None, "tensor"),
            P("replica"),
            P("replica", None),
            P("replica", "tensor"),
            P(),
            P(None, "tensor"),
            P(None, "tensor"),
            P("tensor", None),
            P(),
            P(None, "tensor"),
            P(None, "tensor"),
            P("tensor", None),
        ),
        out_specs=(P("replica", "tensor"), P("replica", "tensor")),
        check_vma=False,
    )
```

time: 99.6 us -> 91.3 us (0.917)
  waiting for transfers between devices: 21.7 us -> 12 us
  local copies, waits for them, and re-layouts: 13.9 us -> 5.21 us
  Pallas kernels: 39.7 us -> 45.6 us
  starting transfers between devices: 19.5 us -> 23.9 us
    unnamed x48 -> x22, local copies, waits for them, and re-layouts: 13.2 us -> 3.09 us
    all_to_all x1, waiting for transfers between devices: 7.73 us -> 0.03 us  [body(): lax.all_to_all(send, 'replica', split_axis=0, concat_axis=0, tiled=True)]
    pallas_call x6 -> x5, Pallas kernels: 32.5 us -> 37.8 us  [the longest x2 19.5 us: finish(): pl.pallas_call(functools.partial(mlp_kernel, count, len(w_outs)), in_spec...]
    ppermute x2 -> x6, starting transfers between devices: 2.64 us -> 6.13 us  [the longest x2 3.54 us: share_rows(): lax.ppermute(piece, 'tensor', [(0, 1), (1, 0)])]
    all_to_all x1, starting transfers between devices: 3.72 us -> 5.94 us  [body(): lax.all_to_all(slot_out, 'replica', split_axis=0, concat_axis=0, tiled=True)]
    slice x0 -> x1, local copies, waits for them, and re-layouts: none -> 2.12 us  [share_rows(): pieces = (mine[:half // 2], mine[half // 2:])]
    ppermute x4, waiting for transfers between devices: 8.84 us -> 7.08 us  [swap(): return [block, lax.ppermute(block, 'tensor', [(0, 1), (1, 0)])]]
    ppermute x4, starting transfers between devices: 6.65 us -> 5.22 us  [swap(): return [block, lax.ppermute(block, 'tensor', [(0, 1), (1, 0)])]]
  transfers between devices with their start and end apart: 8 -> 12, of which waited for: 4 -> 4; matrix products, arithmetic and copies ran while one was open for 3% -> 4% of each run, Pallas kernels for 39% -> 48%
where the time goes in v2:
time: 91.3 us; the launch traced here: 90.8 us
  Pallas kernels  45.6 us (50%)
  starting transfers between devices  23.9 us (26%)
  waiting for transfers between devices  12 us (13%)
  local copies, waits for them, and re-layouts  5.21 us (6%)
  other arithmetic  3.34 us (4%)
    pallas_call x2, Pallas kernels, finish(): pl.pallas_call(functools.partial(mlp_kernel, count, len(w_outs)), in_spec...  19.5 us
    pallas_call x1, Pallas kernels, body(): pl.pallas_call(slot_kernel, in_specs=[ANY, HBM], out_specs=HBM, out_shape...  8.58 us
    pallas_call x1, Pallas kernels, body(): pl.pallas_call(functools.partial(prompt_kernel, count), in_specs=[SCALAR]...  7.88 us
    pallas_call x1, Pallas kernels, body(): pl.pallas_call(functools.partial(request_kernel, count, per_peer), in_spe...  7.25 us
    ppermute x4, waiting for transfers between devices, swap(): return [block, lax.ppermute(block, 'tensor', [(0, 1), (1, 0)])]  7.08 us
    all_to_all x1, starting transfers between devices, body(): lax.all_to_all(send, 'replica', split_axis=0, concat_axis=0, tiled=True)  6.58 us
    all_to_all x1, starting transfers between devices, body(): lax.all_to_all(slot_out, 'replica', split_axis=0, concat_axis=0, tiled=True)  5.94 us
    ppermute x4, starting transfers between devices, swap(): return [block, lax.ppermute(block, 'tensor', [(0, 1), (1, 0)])]  5.22 us
  transfers between devices with their start and end apart: 12, of which 4 were waited for; matrix products, arithmetic and copies ran while one was open for 4% of the time, Pallas kernels for 48%

profile of v2, /device:TPU:0, one launch (start us, length us, event | category | flops | bytes accessed | tf_op | source)
XLA Modules:
  0.0 90.8 jit_solution(9699793748817420115)
XLA Ops:
  0.6 3.0 %collective-permute-start = (bf16[128,1024]{1,0:T(8,128)(2,1)}, bf16[128,1024]{1,0:T(8,128)(2,1)S(1)}, u32[]{:S(2)}, u32[]{:S(2)}) collective-permute-start(bf16[128,1024]{1,0:T(8,128)(2,1)} %refs_0_.5), channel_id=1, source_target_pairs={{0,1},{1,0},{2,3},{3,2},{4,5},{5,4},{6,7},{7,6},{8,9},{9,8},{10,11... | collective-permute-start | bytes 786440 | tf_op jit(solution)/shard_map/ppermute | solution.py:420
  3.6 2.1 %constant_dynamic-slice_fusion.1 = (bf16[128,2048]{1,0:T(8,128)(2,1)}, bf16[128,2048]{1,0:T(8,128)(2,1)S(1)}) fusion(bf16[512,2048]{1,0:T(8,128)(2,1)} %refs_5_.5, s32[]{:T(128)S(6)} %add.27, s32[]{:T(128)S(6)} %select_n.13), kind=kLoop, calls=%fused_computation.4 | loop fusion | bytes 2097160 | tf_op jit(solution)/shard_map/slice | solution.py:433
  5.8 0.0 collective-permute-start.1
  5.8 2.0 %collective-permute-start.2 = (bf16[128,2048]{1,0:T(8,128)(2,1)S(1)}, bf16[128,2048]{1,0:T(8,128)(2,1)S(1)}, u32[]{:S(2)}, u32[]{:S(2)}) collective-permute-start(bf16[128,2048]{1,0:T(8,128)(2,1)S(1)} %get-tuple-element.36), channel_id=1, source_target_pairs={{0,1},{1,0},{2,3},{3,2},{4,5},{5,4},{6,7},{7,6},{8,9},{9,8},{10,11... | collective-permute-start | bytes 1572872 | tf_op jit(solution)/shard_map/ppermute | solution.py:435
  7.8 0.7 pad_add_fusion.place_ref
  8.4 2.5 %collective-permute-done.refs_1_ = bf16[128,1024]{1,0:T(8,128)(2,1)S(1)} collective-permute-done((bf16[128,1024]{1,0:T(8,128)(2,1)}, bf16[128,1024]{1,0:T(8,128)(2,1)S(1)}, u32[]{:S(2)}, u32[]{:S(2)}) %collective-permute-start) | collective-permute-done | bytes 262176 | tf_op jit(solution)/shard_map/ppermute | solution.py:420
  11.0 0.7 copy-done.5
  11.7 7.2 %request_project.1 = (bf16[256,512]{1,0:T(8,128)(2,1)}, f32[128,512]{1,0:T(8,128)}, f32[128,128]{1,0:T(8,128)}) custom-call(s32[2]{0:T(128)} %pad_add_fusion.place_ref, bf16[128,1024]{1,0:T(8,128)(2,1)} %refs_0_.5, bf16[128,1024]{1,0:T(8,128)(2,1)} %copy-done.5, f32[1,2048]{1,0:T(1,128)} %bitcast.15, s32[1,128]{1,0:T(1,128)} %bitcast.17, ...), custom_call_target="tpu_custom_call" | custom-call | flops 402653184 | bytes 3145728 | tf_op jit(solution)/shard_map/request_project/pallas_call | solution.py:534
  19.0 6.6 %all-to-all-start = ((bf16[16,16,512]{2,1,0:T(8,128)(2,1)}), bf16[16,16,512]{2,1,0:T(8,128)(2,1)}, u32[]{:S(2)}, u32[]{:S(2)}) async-start(bf16[16,16,512]{2,1,0:T(8,128)(2,1)} %bitcast.12), calls=%async_computation | async-start | bytes 524288 | tf_op jit(solution)/shard_map/all_to_all | solution.py:557
  25.6 1.6 %collective-permute-start.3 = (bf16[128,2048]{1,0:T(8,128)(2,1)}, bf16[128,2048]{1,0:T(8,128)(2,1)S(1)}, u32[]{:S(2)}, u32[]{:S(2)}) collective-permute-start(bf16[128,2048]{1,0:T(8,128)(2,1)} %get-tuple-element.39), channel_id=1, source_target_pairs={{0,1},{1,0},{2,3},{3,2},{4,5},{5,4},{6,7},{7,6},{8,9},{9,8},{10,11... | collective-permute-start | bytes 1572872 | tf_op jit(solution)/shard_map/ppermute | solution.py:435
  27.1 7.9 %prompt_attention.1.refs_2_ = bf16[128,512]{1,0:T(8,128)(2,1)} custom-call(s32[2]{0:T(128)} %pad_add_fusion.place_ref, bf16[128,1024]{1,0:T(8,128)(2,1)} %refs_0_.4, bf16[128,1024]{1,0:T(8,128)(2,1)} %copy-done.6, f32[1,2048]{1,0:T(1,128)} %bitcast.16, bf16[2048,512]{1,0:T(8,128)(2,1)} %refs_3_.1, bf16[2048,256]{1,0:T(8,128)(2,1)} %refs_4_.3, ...), custom_call_target="tpu_custom_call" | custom-call | flops 1476395008 | bytes 4194304 | tf_op jit(solution)/shard_map/prompt_attention/pallas_call | solution.py:560
  35.0 0.6 collective-permute-start.4
  35.6 0.0 all-to-all-done
  35.7 0.0 collective-permute-start.5
  35.7 8.6 %slot_attention.1 = bf16[256,640]{1,0:T(8,128)(2,1)} custom-call(bf16[256,512]{1,0:T(8,128)(2,1)} %bitcast.6.q_hbm, bf16[2048,256]{1,0:T(8,128)(2,1)} %prefix_hbm.1), custom_call_target="tpu_custom_call" | custom-call | flops 2147483648 | bytes 1048576 | tf_op jit(solution)/shard_map/slot_attention/pallas_call | solution.py:586
  44.3 0.4 collective-permute-start.6
  44.8 5.9 %all-to-all-start.1 = ((bf16[16,16,640]{2,1,0:T(8,128)(2,1)}), bf16[16,16,640]{2,1,0:T(8,128)(2,1)S(1)}, u32[]{:S(2)}, u32[]{:S(2)}) async-start(bf16[16,16,640]{2,1,0:T(8,128)(2,1)} %bitcast.11), calls=%async_computation.1 | async-start | bytes 655360 | tf_op jit(solution)/shard_map/all_to_all | solution.py:612
  50.8 0.8 copy-done.3
  51.6 0.1 copy-done.2
  51.7 9.8 %mlp.2 = (bf16[128,1024]{1,0:T(8,128)(2,1)}, bf16[128,1024]{1,0:T(8,128)(2,1)}, bf16[128,1024]{1,0:T(8,128)(2,1)}) custom-call(s32[2]{0:T(128)} %pad_add_fusion.place_ref, bf16[128,1024]{1,0:T(8,128)(2,1)} %refs_0_.4, bf16[128,1024]{1,0:T(8,128)(2,1)} %copy-done.6, bf16[128,512]{1,0:T(8,128)(2,1)} %prompt_attention.1.refs_2_, bf16[128,512]{1,0:T(8,128)(2,1)} %copy-done.9, ...), custom_call_target="tpu_custom_call" | custom-call | flops 2013265920 | bytes 15728640 | tf_op jit(solution)/shard_map/mlp/pallas_call | solution.py:455
  61.5 0.3 all-to-all-done.1
  61.8 0.7 copy-done.4
  62.6 2.4 %merge.1.refs_2_ = bf16[128,512]{1,0:T(8,128)(2,1)} custom-call(s32[1,128]{1,0:T(1,128)} %bitcast.18, bf16[256,640]{1,0:T(8,128)(2,1)} %bitcast.10, f32[128,512]{1,0:T(8,128)} %get-tuple-element.53.refs_2_, f32[128,128]{1,0:T(8,128)} %get-tuple-element.54.refs_3_), custom_call_target="tpu_custom_call" | custom-call | flops 67108864 | bytes 524288 | tf_op jit(solution)/shard_map/merge/pallas_call | solution.py:618
  65.0 1.6 %collective-permute-start.8 = (bf16[128,512]{1,0:T(8,128)(2,1)}, bf16[128,512]{1,0:T(8,128)(2,1)S(1)}, u32[]{:S(2)}, u32[]{:S(2)}) collective-permute-start(bf16[128,512]{1,0:T(8,128)(2,1)} %merge.1.refs_2_), channel_id=1, source_target_pairs={{0,1},{1,0},{2,3},{3,2},{4,5},{5,4},{6,7},{7,6},{8,9},{9,8},{10,11... | collective-permute-start | bytes 393224 | tf_op jit(solution)/shard_map/ppermute | solution.py:420
  66.6 0.5 collective-permute-start.7
  67.1 4.5 %collective-permute-done.8.refs_3_ = bf16[128,512]{1,0:T(8,128)(2,1)S(1)} collective-permute-done((bf16[128,512]{1,0:T(8,128)(2,1)}, bf16[128,512]{1,0:T(8,128)(2,1)S(1)}, u32[]{:S(2)}, u32[]{:S(2)}) %collective-permute-start.8) | collective-permute-done | bytes 131104 | tf_op jit(solution)/shard_map/ppermute | solution.py:420
  71.6 0.7 copy-done.10
  72.3 9.8 %mlp.3 = (bf16[128,1024]{1,0:T(8,128)(2,1)}, bf16[128,1024]{1,0:T(8,128)(2,1)}, bf16[128,1024]{1,0:T(8,128)(2,1)}) custom-call(s32[2]{0:T(128)} %pad_add_fusion.place_ref, bf16[128,1024]{1,0:T(8,128)(2,1)} %refs_0_.5, bf16[128,1024]{1,0:T(8,128)(2,1)} %copy-done.5, bf16[128,512]{1,0:T(8,128)(2,1)} %merge.1.refs_2_, bf16[128,512]{1,0:T(8,128)(2,1)} %copy-done.10, ...), custom_call_target="tpu_custom_call" | custom-call | flops 2013265920 | bytes 15728640 | tf_op jit(solution)/shard_map/mlp/pallas_call | solution.py:455
  82.0 1.6 %collective-permute-start.9 = (bf16[128,1024]{1,0:T(8,128)(2,1)}, bf16[128,1024]{1,0:T(8,128)(2,1)S(1)}, u32[]{:S(2)}, u32[]{:S(2)}) collective-permute-start(bf16[128,1024]{1,0:T(8,128)(2,1)} %get-tuple-element.57), channel_id=1, source_target_pairs={{0,1},{1,0},{2,3},{3,2},{4,5},{5,4},{6,7},{7,6},{8,9},{9,8},{10,11... | collective-permute-start | bytes 786440 | tf_op jit(solution)/shard_map/ppermute | solution.py:472
  83.6 0.8 add_convert_fusion.1
  84.5 4.5 %collective-permute-done.9 = bf16[128,1024]{1,0:T(8,128)(2,1)S(1)} collective-permute-done((bf16[128,1024]{1,0:T(8,128)(2,1)}, bf16[128,1024]{1,0:T(8,128)(2,1)S(1)}, u32[]{:S(2)}, u32[]{:S(2)}) %collective-permute-start.9) | collective-permute-done | bytes 262176 | tf_op jit(solution)/shard_map/ppermute | solution.py:472
  89.0 1.9 %add_convert_fusion = bf16[128,1024]{1,0:T(8,128)(2,1)} fusion(bf16[128,1024]{1,0:T(8,128)(2,1)S(1)} %collective-permute-done.9, bf16[128,1024]{1,0:T(8,128)(2,1)} %get-tuple-element.56, bf16[128,1024]{1,0:T(8,128)(2,1)} %get-tuple-element.55), kind=kLoop, calls=%fused_computation | loop fusion | flops 786432 | bytes 1048576 | tf_op jit(solution)/shard_map/convert_element_type | solution.py:474
  (24 shorter events, 0.1 us)
Async XLA Ops:
  0.6 10.4 %collective-permute-start = (bf16[128,1024]{1,0:T(8,128)(2,1)}, bf16[128,1024]{1,0:T(8,128)(2,1)S(1)}, u32[]{:S(2)}, u32[]{:S(2)}) collective-permute-start(bf16[128,1024]{1,0:T(8,128)(2,1)} %refs_0_.5), channel_id=1, source_target_pairs={{0,1},{1,0},{2,3},{3,2},{4,5},{5,4},{6,7},{7,6},{8,9},{9,8},{10,11... | collective-permute-start | bytes 786440 | tf_op jit(solution)/shard_map/ppermute | solution.py:420
  5.8 13.2 %collective-permute-start.1 = (bf16[128,1024]{1,0:T(8,128)(2,1)}, bf16[128,1024]{1,0:T(8,128)(2,1)S(1)}, u32[]{:S(2)}, u32[]{:S(2)}) collective-permute-start(bf16[128,1024]{1,0:T(8,128)(2,1)} %refs_0_.4), channel_id=1, source_target_pairs={{0,1},{1,0},{2,3},{3,2},{4,5},{5,4},{6,7},{7,6},{8,9},{9,8},{10,11... | collective-permute-start | bytes 786440 | tf_op jit(solution)/shard_map/ppermute | solution.py:420
  5.8 29.8 %collective-permute-start.2 = (bf16[128,2048]{1,0:T(8,128)(2,1)S(1)}, bf16[128,2048]{1,0:T(8,128)(2,1)S(1)}, u32[]{:S(2)}, u32[]{:S(2)}) collective-permute-start(bf16[128,2048]{1,0:T(8,128)(2,1)S(1)} %get-tuple-element.36), channel_id=1, source_target_pairs={{0,1},{1,0},{2,3},{3,2},{4,5},{5,4},{6,7},{7,6},{8,9},{9,8},{10,11... | collective-permute-start | bytes 1572872 | tf_op jit(solution)/shard_map/ppermute | solution.py:435
  11.0 0.7 copy-start.5
  19.0 8.2 %copy-start.6 = (bf16[128,1024]{1,0:T(8,128)(2,1)}, bf16[128,1024]{1,0:T(8,128)(2,1)S(1)}, u32[]{:S(2)}) copy-start(bf16[128,1024]{1,0:T(8,128)(2,1)S(1)} %collective-permute-done.1.refs_1_) | copy-start | bytes 786436
  19.0 16.7 %all-to-all-start = ((bf16[16,16,512]{2,1,0:T(8,128)(2,1)}), bf16[16,16,512]{2,1,0:T(8,128)(2,1)}, u32[]{:S(2)}, u32[]{:S(2)}) async-start(bf16[16,16,512]{2,1,0:T(8,128)(2,1)} %bitcast.12), calls=%async_computation | async-start | bytes 524288 | tf_op jit(solution)/shard_map/all_to_all | solution.py:557
  25.6 18.8 %collective-permute-start.3 = (bf16[128,2048]{1,0:T(8,128)(2,1)}, bf16[128,2048]{1,0:T(8,128)(2,1)S(1)}, u32[]{:S(2)}, u32[]{:S(2)}) collective-permute-start(bf16[128,2048]{1,0:T(8,128)(2,1)} %get-tuple-element.39), channel_id=1, source_target_pairs={{0,1},{1,0},{2,3},{3,2},{4,5},{5,4},{6,7},{7,6},{8,9},{9,8},{10,11... | collective-permute-start | bytes 1572872 | tf_op jit(solution)/shard_map/ppermute | solution.py:435
  35.0 9.3 %collective-permute-start.4 = (bf16[128,512]{1,0:T(8,128)(2,1)}, bf16[128,512]{1,0:T(8,128)(2,1)S(1)}, u32[]{:S(2)}, u32[]{:S(2)}) collective-permute-start(bf16[128,512]{1,0:T(8,128)(2,1)} %prompt_attention.1.refs_2_), channel_id=1, source_target_pairs={{0,1},{1,0},{2,3},{3,2},{4,5},{5,4},{6,7},{7,6},{8,9},{9,8},{10,11... | collective-permute-start | bytes 393224 | tf_op jit(solution)/shard_map/ppermute | solution.py:420
  35.6 9.2 %copy-start = (bf16[128,2048]{1,0:T(8,128)(2,1)}, bf16[128,2048]{1,0:T(8,128)(2,1)S(1)}, u32[]{:S(2)}) copy-start(bf16[128,2048]{1,0:T(8,128)(2,1)S(1)} %collective-permute-done.2.refs_6_) | copy-start | bytes 1572868
  35.7 15.1 %collective-permute-start.5 = (bf16[128,2048]{1,0:T(8,128)(2,1)S(1)}, bf16[128,2048]{1,0:T(8,128)(2,1)S(1)}, u32[]{:S(2)}, u32[]{:S(2)}) collective-permute-start(bf16[128,2048]{1,0:T(8,128)(2,1)S(1)} %collective-permute-done.2.refs_6_), channel_id=1, source_target_pairs={{0,2},{2,0},{4,6},{6,4},{8,10},{10,8},{12,14},{14,12},{16,18},{18,... | collective-permute-start | bytes 1572872 | tf_op jit(solution)/shard_map/ppermute | solution.py:439
  44.3 7.3 %copy-start.9 = (bf16[128,512]{1,0:T(8,128)(2,1)}, bf16[128,512]{1,0:T(8,128)(2,1)S(1)}, u32[]{:S(2)}) copy-start(bf16[128,512]{1,0:T(8,128)(2,1)S(1)} %collective-permute-done.4.refs_3_) | copy-start | bytes 393220
  44.3 7.3 %copy-start.1 = (bf16[128,2048]{1,0:T(8,128)(2,1)}, bf16[128,2048]{1,0:T(8,128)(2,1)S(1)}, u32[]{:S(2)}) copy-start(bf16[128,2048]{1,0:T(8,128)(2,1)S(1)} %collective-permute-done.3.refs_7_) | copy-start | bytes 1572868
  44.3 6.4 %collective-permute-start.6 = (bf16[128,2048]{1,0:T(8,128)(2,1)S(1)}, bf16[128,2048]{1,0:T(8,128)(2,1)S(1)}, u32[]{:S(2)}, u32[]{:S(2)}) collective-permute-start(bf16[128,2048]{1,0:T(8,128)(2,1)S(1)} %collective-permute-done.3.refs_7_), channel_id=1, source_target_pairs={{0,2},{2,0},{4,6},{6,4},{8,10},{10,8},{12,14},{14,12},{16,18},{18,... | collective-permute-start | bytes 1572872 | tf_op jit(solution)/shard_map/ppermute | solution.py:439
  44.8 17.0 %all-to-all-start.1 = ((bf16[16,16,640]{2,1,0:T(8,128)(2,1)}), bf16[16,16,640]{2,1,0:T(8,128)(2,1)S(1)}, u32[]{:S(2)}, u32[]{:S(2)}) async-start(bf16[16,16,640]{2,1,0:T(8,128)(2,1)} %bitcast.11), calls=%async_computation.1 | async-start | bytes 655360 | tf_op jit(solution)/shard_map/all_to_all | solution.py:612
  50.8 1.0 %copy-start.2 = (bf16[128,2048]{1,0:T(8,128)(2,1)}, bf16[128,2048]{1,0:T(8,128)(2,1)S(1)}, u32[]{:S(2)}) copy-start(bf16[128,2048]{1,0:T(8,128)(2,1)S(1)} %collective-permute-done.5.refs_8_) | copy-start | bytes 1572868
  50.8 0.8 copy-start.3
  61.8 0.7 copy-start.4
  65.0 18.6 %copy-start.7 = (bf16[128,1024]{1,0:T(8,128)(2,1)S(1)}, bf16[128,1024]{1,0:T(8,128)(2,1)}, u32[]{:S(2)}) copy-start(bf16[128,1024]{1,0:T(8,128)(2,1)} %get-tuple-element.50) | copy-start | bytes 786436
  65.0 18.6 %copy-start.8 = (bf16[128,1024]{1,0:T(8,128)(2,1)S(1)}, bf16[128,1024]{1,0:T(8,128)(2,1)}, u32[]{:S(2)}) copy-start(bf16[128,1024]{1,0:T(8,128)(2,1)} %get-tuple-element.49) | copy-start | bytes 786436
  65.0 6.6 %collective-permute-start.8 = (bf16[128,512]{1,0:T(8,128)(2,1)}, bf16[128,512]{1,0:T(8,128)(2,1)S(1)}, u32[]{:S(2)}, u32[]{:S(2)}) collective-permute-start(bf16[128,512]{1,0:T(8,128)(2,1)} %merge.1.refs_2_), channel_id=1, source_target_pairs={{0,1},{1,0},{2,3},{3,2},{4,5},{5,4},{6,7},{7,6},{8,9},{9,8},{10,11... | collective-permute-start | bytes 393224 | tf_op jit(solution)/shard_map/ppermute | solution.py:420
  66.6 17.0 %collective-permute-start.7 = (bf16[128,1024]{1,0:T(8,128)(2,1)}, bf16[128,1024]{1,0:T(8,128)(2,1)S(1)}, u32[]{:S(2)}, u32[]{:S(2)}) collective-permute-start(bf16[128,1024]{1,0:T(8,128)(2,1)} %get-tuple-element.51), channel_id=1, source_target_pairs={{0,1},{1,0},{2,3},{3,2},{4,5},{5,4},{6,7},{7,6},{8,9},{9,8},{10,11... | collective-permute-start | bytes 786440 | tf_op jit(solution)/shard_map/ppermute | solution.py:472
  71.6 0.7 copy-start.10
  82.0 6.9 %collective-permute-start.9 = (bf16[128,1024]{1,0:T(8,128)(2,1)}, bf16[128,1024]{1,0:T(8,128)(2,1)S(1)}, u32[]{:S(2)}, u32[]{:S(2)}) collective-permute-start(bf16[128,1024]{1,0:T(8,128)(2,1)} %get-tuple-element.57), channel_id=1, source_target_pairs={{0,1},{1,0},{2,3},{3,2},{4,5},{5,4},{6,7},{7,6},{8,9},{9,8},{10,11... | collective-permute-start | bytes 786440 | tf_op jit(solution)/shard_map/ppermute | solution.py:472

commit v3 on v2

--- a/solution.py
+++ b/solution.py
@@ -19,8 +19,10 @@
 BF16 = jnp.bfloat16
 MIB = 1024 * 1024
 MOST_VMEM = 62 * MIB
+TAIL_VMEM = 36 * MIB
 ANY = pl.BlockSpec(memory_space=pl.ANY)
 HBM = pl.BlockSpec(memory_space=pltpu.HBM)
+HELD = pl.BlockSpec(memory_space=pltpu.VMEM)
 SCALAR = pl.BlockSpec(memory_space=pltpu.SMEM)
 
 
@@ -131,19 +133,15 @@
 
 
 def request_kernel(count, per_peer, place_ref, *refs):
-    inputs = count + 6
-    sources, (send_ref, past_ref, sum_ref), refs = refs[:inputs], refs[inputs : inputs + 3], refs[inputs + 3 :]
-    held, (send_scr, past_scr, sum_scr), refs = refs[:inputs], refs[inputs : inputs + 3], refs[inputs + 3 :]
-    q_scr, score_scr, weight_scr, mixed_scr, sems = refs
+    inputs = count + 4
+    sources, (send_ref, q_ref, kv_ref), refs = refs[:inputs], refs[inputs : inputs + 3], refs[inputs + 3 :]
+    held, (send_scr, q_scr, kv_scr, sems) = refs[:inputs], refs[inputs:]
     copies, started = fetch(sources, held, sems)
-    gain_ref, target_ref, w_query_ref, len_ref, keyval_weight_ref, cache_ref = held[count:]
-    requests, cached, kv_width = cache_ref.shape
-    groups = requests // GROUP
-    keys = GROUP * cached
+    gain_ref, target_ref, w_query_ref, keyval_weight_ref = held[count:]
     for copy in started[: count + 2]:
         copy.wait()
     _, slot_row = slot_places(target_ref[...], per_peer)
-    spread = lax.broadcasted_iota(jnp.int32, (send_scr.shape[0], requests), 0) == slot_row
+    spread = lax.broadcasted_iota(jnp.int32, (send_scr.shape[0], slot_row.shape[1]), 0) == slot_row
     rows = in_order(place_ref, [ref[...] for ref in held[:count]])
     normed = rms_norm(rows.astype(F32), gain_ref[...])
     started[count + 2].wait()
@@ -152,9 +150,18 @@
         spread.astype(BF16), queries, preferred_element_type=F32
     ).astype(BF16)
     copies.start(send_scr, send_ref)
+    q_scr[...] = queries
+    copies.start(q_scr, q_ref)
     started[count + 3].wait()
-    started[count + 4].wait()
-    keyval = jnp.dot(normed, keyval_weight_ref[...], preferred_element_type=F32).astype(BF16)
+    kv_scr[...] = jnp.dot(normed, keyval_weight_ref[...], preferred_element_type=F32).astype(BF16)
+    copies.start(kv_scr, kv_ref)
+    copies.wait()
+
+
+def past_attention(queries, keyval, lengths, cache_ref, past_scr, q_scr, score_scr, weight_scr, mixed_scr):
+    requests, cached, kv_width = cache_ref.shape
+    groups = requests // GROUP
+    keys = GROUP * cached
     heads = queries.shape[1] // HEAD_SIZE
     block_rows = heads * GROUP
     q_scr[...] = jnp.zeros_like(q_scr)
@@ -172,8 +179,6 @@
     owner = lax.broadcasted_iota(jnp.int32, (block_rows, keys), 0) % GROUP
     columns = lane_ids((block_rows, keys))
     position = jnp.where(columns // cached == owner, columns % cached, cached)
-    lengths = column_of(len_ref[...])
-    started[count + 5].wait()
     for group in range(groups):
         block = cache_ref[group * GROUP : (group + 1) * GROUP].reshape(keys, kv_width)
         live = position < jnp.concatenate(
@@ -207,20 +212,29 @@
         past_scr[:, pair * PAIR : (pair + 1) * PAIR] = jnp.where(
             lanes < HEAD_SIZE, pltpu.roll(done[2 * pair], HEAD_SIZE, 1), done[2 * pair + 1]
         )
-    sum_scr[...] = sums
-    copies.start(past_scr, past_ref)
-    copies.start(sum_scr, sum_ref)
-    copies.wait()
+    past_scr[:, heads * HEAD_SIZE :] = sums
+
+
+def pipelined(count, score, soften, settle):
+    scores, pending = score(0), None
+    for i in range(count):
+        following = score(i + 1) if i + 1 < count else None
+        weights = soften(i, scores)
+        if pending is not None:
+            settle(i - 1, pending)
+        scores, pending = following, weights
+    settle(count - 1, pending)
 
 
 def prompt_kernel(count, place_ref, *refs):
-    inputs = count + 4
-    sources, att_ref, refs = refs[:inputs], refs[inputs], refs[inputs + 1 :]
-    held, (q_scr, kvx_scr, att_scr, sems) = refs[:inputs], refs[inputs:]
+    inputs = count + 8
+    sources, (att_ref, past_ref), refs = refs[:inputs], refs[inputs : inputs + 2], refs[inputs + 2 :]
+    held, (q_scr, kvx_scr, att_scr, past_scr, *past_scrs, sems) = refs[:inputs], refs[inputs:]
     copies, started = fetch(sources, held, sems)
     for copy in started[: count + 1]:
         copy.wait()
-    gain_ref, w_query_ref, keyval_weight_ref, prefix_ref = held[count:]
+    gain_ref, w_query_ref, keyval_weight_ref, prefix_ref = held[count : count + 4]
+    request_q_ref, request_kv_ref, len_ref, cache_ref = held[count + 4 :]
     rows = in_order(place_ref, [ref[...] for ref in held[:count]])
     normed = rms_norm(rows.astype(F32), gain_ref[...])
     started[count + 1].wait()
@@ -236,26 +250,46 @@
     own_ones = ones_for_keys(keyval)
     row_ids = lax.broadcasted_iota(jnp.int32, (2 * row_count, row_count), 0) % row_count
     visible = lax.broadcasted_iota(jnp.int32, (2 * row_count, row_count), 1) <= row_ids
-    for kv in range(heads // QUERIES_PER_KEY):
-        columns = slice(kv * PAIR, (kv + 1) * PAIR)
-        own_keys = keyval[:, columns]
-        own_values = own_ones[:, columns]
-        for half in range(QUERIES_PER_KEY // 2):
-            pair = kv * (QUERIES_PER_KEY // 2) + half
-            query_rows = q_scr[pl.ds(2 * pair, 2)].reshape(2 * row_count, PAIR)
-            past = scores_of(query_rows, prefix_ref[:, columns])
-            own = jnp.where(visible, scores_of(query_rows, own_keys), -jnp.inf)
-            row_max = jnp.maximum(
-                jnp.max(past, axis=1, keepdims=True), jnp.max(own, axis=1, keepdims=True)
-            )
-            past_exp = jnp.exp2((past - row_max) * FACTOR).astype(BF16)
-            own_exp = jnp.exp2((own - row_max) * FACTOR).astype(BF16)
-            total = jnp.dot(past_exp, kvx_scr[:, columns], preferred_element_type=F32)
-            total = total + jnp.dot(own_exp, own_values, preferred_element_type=F32)
-            att_scr[:, pair * PAIR : (pair + 1) * PAIR] = pack_pair(
-                total[:row_count], total[row_count:]
-            ).astype(BF16)
+
+    def columns_of(pair):
+        kv = 2 * pair // QUERIES_PER_KEY
+        return slice(kv * PAIR, (kv + 1) * PAIR)
+
+    def score(pair):
+        query_rows = q_scr[pl.ds(2 * pair, 2)].reshape(2 * row_count, PAIR)
+        past = scores_of(query_rows, prefix_ref[:, columns_of(pair)])
+        own = scores_of(query_rows, keyval[:, columns_of(pair)])
+        return past, jnp.where(visible, own, -jnp.inf)
+
+    def soften(pair, scores):
+        past, own = scores
+        row_max = jnp.maximum(
+            jnp.max(past, axis=1, keepdims=True), jnp.max(own, axis=1, keepdims=True)
+        )
+        return [jnp.exp2((part - row_max) * FACTOR).astype(BF16) for part in (past, own)]
+
+    def settle(pair, weights):
+        total = jnp.dot(weights[0], kvx_scr[:, columns_of(pair)], preferred_element_type=F32)
+        total = total + jnp.dot(
+            weights[1], own_ones[:, columns_of(pair)], preferred_element_type=F32
+        )
+        att_scr[:, pair * PAIR : (pair + 1) * PAIR] = pack_pair(
+            total[:row_count], total[row_count:]
+        ).astype(BF16)
+
+    pipelined(heads // 2, score, soften, settle)
     copies.start(att_scr, att_ref)
+    for copy in started[count + 4 :]:
+        copy.wait()
+    past_attention(
+        request_q_ref[...],
+        request_kv_ref[...],
+        column_of(len_ref[...]),
+        cache_ref,
+        past_scr,
+        *past_scrs,
+    )
+    copies.start(past_scr, past_ref)
     copies.wait()
 
 
@@ -270,43 +304,55 @@
     started[1].wait()
     kvx_scr[...] = ones_for_keys(prefix_ref[...])
     lanes = lane_ids((slots, PAIR))
-    sums = jnp.zeros((slots, PAIR), F32)
-    for kv in range(heads // QUERIES_PER_KEY):
-        columns = slice(kv * PAIR, (kv + 1) * PAIR)
-        for half in range(QUERIES_PER_KEY // 2):
-            pair = kv * (QUERIES_PER_KEY // 2) + half
-            totals = []
-            for head in (2 * pair, 2 * pair + 1):
-                scores = scores_of(q_scr[head], prefix_ref[:, columns])
-                row_max = jnp.max(scores, axis=1, keepdims=True)
-                exp_vals = jnp.exp2((scores - row_max) * FACTOR).astype(BF16)
-                total = jnp.dot(exp_vals, kvx_scr[:, columns], preferred_element_type=F32)
-                totals.append(total)
-                log_sum = row_max * FACTOR + jnp.log2(total)
-                high = log_sum.astype(BF16).astype(F32)
-                middle = (log_sum - high).astype(BF16).astype(F32)
-                low = log_sum - high - middle
-                for place, part in enumerate((high, middle, low)):
-                    sums = jnp.where(lanes == 3 * head + place, part, sums)
-            out_ref[:, pair * PAIR : (pair + 1) * PAIR] = pack_pair(*totals).astype(BF16)
-    out_ref[:, width:] = sums.astype(BF16)
-    copies.start(out_ref, out_hbm)
+    sums = [jnp.zeros((slots, PAIR), F32)]
+    even = []
+
+    def columns_of(head):
+        kv = head // QUERIES_PER_KEY
+        return slice(kv * PAIR, (kv + 1) * PAIR)
+
+    def score(head):
+        return scores_of(q_scr[head], prefix_ref[:, columns_of(head)])
+
+    def soften(head, scores):
+        row_max = jnp.max(scores, axis=1, keepdims=True)
+        return row_max, jnp.exp2((scores - row_max) * FACTOR).astype(BF16)
+
+    def settle(head, pending):
+        row_max, weights = pending
+        total = jnp.dot(weights, kvx_scr[:, columns_of(head)], preferred_element_type=F32)
+        log_sum = row_max * FACTOR + jnp.log2(total)
+        high = log_sum.astype(BF16).astype(F32)
+        middle = (log_sum - high).astype(BF16).astype(F32)
+        low = log_sum - high - middle
+        for place, part in enumerate((high, middle, low)):
+            sums[0] = jnp.where(lanes == 3 * head + place, part, sums[0])
+        if head % 2 == 0:
+            even.append(total)
+            return
+        at = slice((head - 1) * HEAD_SIZE, (head + 1) * HEAD_SIZE)
+        out_ref[:, at] = pack_pair(even[-1], total).astype(BF16)
+        copies.start(out_ref.at[:, at], out_hbm.at[:, at])
+
+    pipelined(heads, score, soften, settle)
+    out_ref[:, width:] = sums[0].astype(BF16)
+    copies.start(out_ref.at[:, width:], out_hbm.at[:, width:])
     copies.wait()
 
 
 def merge_kernel(per_peer, *refs):
-    sources, att_ref, held, (att_scr, sems) = refs[:4], refs[4], refs[5:9], refs[9:]
+    sources, att_ref, held, (att_scr, sems) = refs[:3], refs[3], refs[4:7], refs[7:]
     copies, started = fetch(sources, held, sems)
-    target_ref, back_ref, past_ref, sum_ref = held
+    target_ref, back_ref, past_ref = held
     for copy in started:
         copy.wait()
     slot_column, _ = slot_places(target_ref[...], per_peer)
     gather = lane_ids((slot_column.shape[0], back_ref.shape[0])) == slot_column
-    width = past_ref.shape[1]
+    width = past_ref.shape[1] - PAIR
     heads = width // HEAD_SIZE
     prefix = jnp.dot(gather.astype(BF16), back_ref[...], preferred_element_type=F32)
     prefix_sums = prefix[:, width:]
-    past_sums = sum_ref[...]
+    past_sums = past_ref[:, width:]
     lanes = lane_ids(past_sums.shape)
     shares = []
     for head in range(heads):
@@ -347,21 +393,9 @@
     if blocks == groups:
         outs_in = [[copies.start(weight_refs[i], w_outs[i])] for i in range(groups)]
     else:
-        half = weight_refs[1].shape[0]
-        odd = place_ref[1]
         outs_in = [
             [copies.start(weight_refs[0], w_outs[0])],
-            [
-                copies.start(weight_refs[1 + i], w_outs[1].at[pl.ds(start, half)])
-                for i, start in enumerate(
-                    (
-                        2 * odd * half,
-                        (2 * odd + 1) * half,
-                        2 * (1 - odd) * half,
-                        (2 * (1 - odd) + 1) * half,
-                    )
-                )
-            ],
+            start_pieces(copies, place_ref, weight_refs[1:blocks], w_outs[1]),
         ]
     weight_refs = weight_refs[blocks:]
     columns = [
@@ -415,6 +449,117 @@
     copies.wait()
 
 
+def load_kernel(*refs):
+    count = len(refs) // 2
+    _, started = fetch(refs[:count], refs[count : 2 * count], refs[-1])
+    for copy in started:
+        copy.wait()
+
+
+def load(limit, *arrays):
+    return pl.pallas_call(
+        load_kernel,
+        in_specs=[ANY] * len(arrays),
+        out_specs=[HELD] * len(arrays),
+        out_shape=[jax.ShapeDtypeStruct(x.shape, x.dtype) for x in arrays],
+        scratch_shapes=[pltpu.SemaphoreType.DMA((len(arrays),))],
+        compiler_params=params(limit),
+        cost_estimate=cost(0, sum(2 * x.size for x in arrays)),
+        name="load",
+    )(*arrays)
+
+
+def start_pieces(copies, place_ref, pieces, target):
+    rows = pieces[0].shape[0]
+    odd = place_ref[1]
+    starts = (2 * odd, 2 * odd + 1, 2 * (1 - odd), 2 * (1 - odd) + 1)
+    return [
+        copies.start(piece, target.at[pl.ds(start * rows, rows)])
+        for piece, start in zip(pieces, starts)
+    ]
+
+
+def tail_kernel(place_ref, *refs):
+    w_gate, w_up, sources, pieces, w_down_hbm = refs[0], refs[1], refs[2:8], refs[8:12], refs[12]
+    send_ref, hidden_ref, residual_ref = refs[13:16]
+    held, (w_out_other, w_down, send_scr, sems) = refs[16:22], refs[22:]
+    own_ref, other_ref, gain_ref, att_ref, att_other_ref, w_out_ref = held
+    width = send_scr.shape[1]
+    hidden_width = w_gate.shape[1]
+    away = pl.ds(pl.multiple_of((1 - place_ref[0]) * width, width), width)
+    copies, started = fetch(sources, held, sems)
+    arriving = start_pieces(copies, place_ref, pieces, w_out_other)
+    down = copies.start(w_down_hbm.at[:, away], w_down)
+    copies.flying = []
+    for copy in started:
+        copy.wait()
+    rows = in_order(place_ref, [own_ref[...], other_ref[...]]).astype(F32)
+    mixed = jnp.dot(att_ref[...], w_out_ref[...], preferred_element_type=F32)
+    for copy in arriving:
+        copy.wait()
+    mixed_other = jnp.dot(att_other_ref[...], w_out_other[...], preferred_element_type=F32)
+    mixed = mixed.astype(BF16).astype(F32) + mixed_other.astype(BF16).astype(F32)
+    residual = (rows + mixed).astype(BF16)
+    normed = rms_norm(residual.astype(F32), gain_ref[...])
+    residual_ref[...] = jnp.where(place_ref[0] == 0, residual[:, :width], residual[:, width:])
+    hidden = []
+    for start in range(0, hidden_width, CHUNK):
+        at = slice(start, min(start + CHUNK, hidden_width))
+        gate_act = jnp.dot(normed, w_gate[:, at], preferred_element_type=F32)
+        up_act = jnp.dot(normed, w_up[:, at], preferred_element_type=F32)
+        hidden.append((gate_act / (1.0 + jnp.exp(-gate_act)) * up_act).astype(BF16))
+    hidden = jnp.concatenate(hidden, axis=1)
+    down.wait()
+    send_scr[...] = jnp.dot(hidden, w_down[...], preferred_element_type=F32).astype(BF16)
+    copies.start(send_scr, send_ref)
+    hidden_ref[...] = hidden
+    copies.wait()
+
+
+def keep_kernel(place_ref, hidden_ref, residual_ref, w_down_hbm, out_ref, w_down, sems):
+    width = out_ref.shape[1]
+    own = pl.ds(pl.multiple_of(place_ref[0] * width, width), width)
+    copies = Copies(sems)
+    copies.start(w_down_hbm.at[:, own], w_down)
+    copies.wait()
+    term = jnp.dot(hidden_ref[...], w_down[...], preferred_element_type=F32).astype(BF16)
+    out_ref[...] = residual_ref[...].astype(F32) + term.astype(F32)
+
+
+def tail(place, parts, attended, gain, w_outs, w_gate, w_up, w_down):
+    attended, w_gate, w_up = lax.optimization_barrier((attended, w_gate, w_up))
+    rows, width = parts[0].shape
+    hidden = w_up.shape[1]
+    held = load(TAIL_VMEM, w_gate, w_up)
+    sources = (*parts, gain, *swap(attended, 2), w_outs[0])
+    half = jax.ShapeDtypeStruct((rows, width), BF16)
+    units = jax.ShapeDtypeStruct((rows, hidden), BF16)
+    half_down = pltpu.VMEM((hidden, width), BF16)
+    send, units, residual = pl.pallas_call(
+        tail_kernel,
+        in_specs=[SCALAR] + [HELD] * 2 + [ANY] * 11,
+        out_specs=[HBM, HELD, HELD],
+        out_shape=[half, units, half],
+        scratch_shapes=scratch_like(*sources, w_outs[0])
+        + [half_down, pltpu.VMEM((rows, width), BF16), pltpu.SemaphoreType.DMA((12,))],
+        compiler_params=params(TAIL_VMEM),
+        cost_estimate=cost(10 * rows * width * hidden, 6 * width * hidden, rows * hidden),
+        name="tail",
+    )(place, *held, *sources, *w_outs[1:], w_down)
+    kept = pl.pallas_call(
+        keep_kernel,
+        in_specs=[SCALAR] + [HELD] * 2 + [ANY],
+        out_specs=HELD,
+        out_shape=jax.ShapeDtypeStruct((rows, width), F32),
+        scratch_shapes=[half_down, pltpu.SemaphoreType.DMA((1,))],
+        compiler_params=params(TAIL_VMEM),
+        cost_estimate=cost(2 * rows * width * hidden, 2 * width * hidden),
+        name="keep",
+    )(place, units, residual, w_down)
+    other = lax.ppermute(send, "tensor", [(0, 1), (1, 0)])
+    return (kept + other.astype(F32)).astype(BF16)
+
+
 def swap(block, count):
     if count == 2:
         return [block, lax.ppermute(block, "tensor", [(0, 1), (1, 0)])]
@@ -516,34 +661,19 @@
     cached = request_keyval_cache.shape[1]
     w_outs, prompt_rows = share_rows(w_out, count, replicas, prompt_rows)
     prompt_parts = swap(prompt_rows, count)
+    operands = (*request_parts, attn_gain, target, w_query, keyval_weight)
     outs = [
         jax.ShapeDtypeStruct((slots, width), BF16),
-        jax.ShapeDtypeStruct((requests, width), F32),
-        jax.ShapeDtypeStruct((requests, PAIR), F32),
+        jax.ShapeDtypeStruct((requests, width), BF16),
+        jax.ShapeDtypeStruct((requests, kv_width), BF16),
     ]
-    operands = (
-        *request_parts,
-        attn_gain,
-        target,
-        w_query,
-        cache_len.reshape(1, requests),
-        keyval_weight,
-        request_keyval_cache,
-    )
-    blocks = (requests // GROUP, heads * GROUP)
-    send, past, past_sums = pl.pallas_call(
+    send, queries, keyval = pl.pallas_call(
         functools.partial(request_kernel, count, per_peer),
         in_specs=[SCALAR] + [ANY] * len(operands),
         out_specs=[HBM] * 3,
         out_shape=outs,
         scratch_shapes=scratch_like(*operands, *outs)
-        + [
-            pltpu.VMEM((*blocks, kv_width), F32),
-            pltpu.VMEM((*blocks, GROUP * cached), F32),
-            pltpu.VMEM((*blocks, GROUP * cached), BF16),
-            pltpu.VMEM((*blocks, kv_width), F32),
-            pltpu.SemaphoreType.DMA((len(operands) + 3,)),
-        ],
+        + [pltpu.SemaphoreType.DMA((len(operands) + 3,))],
         compiler_params=params(),
         cost_estimate=cost(
             2 * requests * model * (width + kv_width), 2 * model * (width + kv_width)
@@ -551,23 +681,42 @@
         name="request_project",
     )(place, *operands)
 
-    send, prompt_parts[-1], past, past_sums = lax.optimization_barrier(
-        (send, prompt_parts[-1], past, past_sums)
-    )
+    send, prompt_parts[-1] = lax.optimization_barrier((send, prompt_parts[-1]))
     slot_queries = lax.all_to_all(send, "replica", split_axis=0, concat_axis=0, tiled=True)
 
-    operands = (*prompt_parts, attn_gain, w_query, keyval_weight, prefix_cache)
-    prompt_attended = pl.pallas_call(
+    operands = (
+        *prompt_parts,
+        attn_gain,
+        w_query,
+        keyval_weight,
+        prefix_cache,
+        queries,
+        keyval,
+        cache_len.reshape(1, requests),
+        request_keyval_cache,
+    )
+    outs = [
+        jax.ShapeDtypeStruct((prompts, width), BF16),
+        jax.ShapeDtypeStruct((requests, width + PAIR), F32),
+    ]
+    blocks = (requests // GROUP, heads * GROUP)
+    prompt_attended, past = pl.pallas_call(
         functools.partial(prompt_kernel, count),
-        in_specs=[SCALAR] + [ANY] * count + [HBM] * 4,
-        out_specs=HBM,
-        out_shape=jax.ShapeDtypeStruct((prompts, width), BF16),
+        in_specs=[SCALAR] + [ANY] * len(operands),
+        out_specs=[HBM] * 2,
+        out_shape=outs,
         scratch_shapes=scratch_like(*operands)
         + [
             pltpu.VMEM((heads, prompts, PAIR), BF16),
             pltpu.VMEM((prefix_len, kv_width), BF16),
-            pltpu.VMEM((prompts, width), BF16),
-            pltpu.SemaphoreType.DMA((len(operands) + 1,)),
+        ]
+        + scratch_like(*outs)
+        + [
+            pltpu.VMEM((*blocks, kv_width), F32),
+            pltpu.VMEM((*blocks, GROUP * cached), F32),
+            pltpu.VMEM((*blocks, GROUP * cached), BF16),
+            pltpu.VMEM((*blocks, kv_width), F32),
+            pltpu.SemaphoreType.DMA((len(operands) + 2,)),
         ],
         compiler_params=params(),
         cost_estimate=cost(
@@ -593,7 +742,7 @@
             pltpu.VMEM((slots, width + PAIR), BF16),
             pltpu.VMEM((heads, slots, PAIR), BF16),
             pltpu.VMEM((prefix_len, kv_width), BF16),
-            pltpu.SemaphoreType.DMA((3,)),
+            pltpu.SemaphoreType.DMA((3 + heads // 2,)),
         ],
         compiler_params=params(),
         cost_estimate=cost(
@@ -614,21 +763,26 @@
     weights = (mlp_gain, w_outs, w_gate, w_up, w_down)
     prompt_terms = finish(place, prompt_parts, prompt_attended, *weights)
     back, prompt_terms = lax.optimization_barrier((back, prompt_terms))
-    operands = (target, back, past, past_sums)
+    operands = (target, back, past)
     request_attended = pl.pallas_call(
         functools.partial(merge_kernel, per_peer),
         in_specs=[ANY] * len(operands),
         out_specs=HBM,
         out_shape=jax.ShapeDtypeStruct((requests, width), BF16),
         scratch_shapes=scratch_like(*operands)
-        + [pltpu.VMEM((requests, width), BF16), pltpu.SemaphoreType.DMA((5,))],
+        + [pltpu.VMEM((requests, width), BF16), pltpu.SemaphoreType.DMA((4,))],
         compiler_params=params(),
         cost_estimate=cost(4 * requests * slots * width, 4 * slots * width),
         name="merge",
     )(*operands)
 
-    request_terms = finish(place, request_parts, swap(request_attended, count), *weights)
-    return (exchange(prompt_terms, count), exchange(request_terms, count))
+    if count == 2:
+        request_out = tail(place, request_parts, request_attended, *weights)
+    else:
+        request_out = exchange(
+            finish(place, request_parts, swap(request_attended, count), *weights), count
+        )
+    return (exchange(prompt_terms, count), request_out)
 
 
 def solution(mesh):

time: 91.3 us -> 85.5 us (0.936)
  waiting for transfers between devices: 12 us -> 7.29 us
  Pallas kernels: 45.6 us -> 43 us
  local copies, waits for them, and re-layouts: 5.21 us -> 7.68 us
  other arithmetic: 3.34 us -> 2.24 us
    pallas_call x2 -> x1, Pallas kernels: 19.5 us -> 9.76 us  [finish(): pl.pallas_call(functools.partial(mlp_kernel, count, len(w_outs)), in_spec...]
    pallas_call x0 -> x3, Pallas kernels: none -> 9.25 us  [the longest x1 4.61 us: tail(): pl.pallas_call(tail_kernel, in_specs=[SCALAR] + [HELD] * 2 + [ANY] * 11,...]
    ppermute x2 -> x1, waiting for transfers between devices: 4.52 us -> 0.01 us  [exchange(): other = lax.ppermute(send, 'tensor', [(0, 1), (1, 0)])]
    ppermute x4, waiting for transfers between devices: 7.08 us -> 3.17 us  [swap(): return [block, lax.ppermute(block, 'tensor', [(0, 1), (1, 0)])]]
    ppermute x0 -> x1, waiting for transfers between devices: none -> 3.78 us  [tail(): other = lax.ppermute(send, 'tensor', [(0, 1), (1, 0)])]
    pallas_call x1, Pallas kernels: 7.25 us -> 4.29 us  [body(): pl.pallas_call(functools.partial(request_kernel, count, per_peer), in_spe...]
    unnamed x22 -> x46, local copies, waits for them, and re-layouts: 3.09 us -> 5.56 us
    convert_element_type x2 -> x1, other arithmetic: 2.69 us -> 0.83 us  [exchange(): return (residual.astype(F32) + summed).astype(BF16)]
where the time goes in v3:
time: 85.5 us; the launch traced here: 85 us
  Pallas kernels  43 us (50%)
  starting transfers between devices  23.8 us (28%)
  local copies, waits for them, and re-layouts  7.68 us (9%)
  waiting for transfers between devices  7.29 us (9%)
  other arithmetic  2.24 us (3%)
  between operations  0.92 us (1%)
    pallas_call x1, Pallas kernels, finish(): pl.pallas_call(functools.partial(mlp_kernel, count, len(w_outs)), in_spec...  9.76 us
    pallas_call x1, Pallas kernels, body(): pl.pallas_call(functools.partial(prompt_kernel, count), in_specs=[SCALAR]...  9.66 us
    pallas_call x1, Pallas kernels, body(): pl.pallas_call(slot_kernel, in_specs=[ANY, HBM], out_specs=HBM, out_shape...  7.61 us
    all_to_all x1, starting transfers between devices, body(): lax.all_to_all(send, 'replica', split_axis=0, concat_axis=0, tiled=True)  6.55 us
    all_to_all x1, starting transfers between devices, body(): lax.all_to_all(slot_out, 'replica', split_axis=0, concat_axis=0, tiled=True)  5.89 us
    unnamed x46, local copies, waits for them, and re-layouts  5.56 us
    ppermute x4, starting transfers between devices, swap(): return [block, lax.ppermute(block, 'tensor', [(0, 1), (1, 0)])]  5.23 us
    pallas_call x1, Pallas kernels, tail(): pl.pallas_call(tail_kernel, in_specs=[SCALAR] + [HELD] * 2 + [ANY] * 11,...  4.61 us
  transfers between devices with their start and end apart: 12, of which 4 were waited for; matrix products, arithmetic and copies ran while one was open for 4% of the time, Pallas kernels for 48%

profile of v3, /device:TPU:0, one launch (start us, length us, event | category | flops | bytes accessed | tf_op | source)
XLA Modules:
  0.0 85.0 jit_solution(7608836182205375649)
XLA Ops:
  0.6 3.0 %collective-permute-start = (bf16[128,1024]{1,0:T(8,128)(2,1)}, bf16[128,1024]{1,0:T(8,128)(2,1)S(1)}, u32[]{:S(2)}, u32[]{:S(2)}) collective-permute-start(bf16[128,1024]{1,0:T(8,128)(2,1)} %refs_2_.1), channel_id=1, source_target_pairs={{0,1},{1,0},{2,3},{3,2},{4,5},{5,4},{6,7},{7,6},{8,9},{9,8},{10,11... | collective-permute-start | bytes 786440 | tf_op jit(solution)/shard_map/ppermute | solution.py:565
  3.6 2.1 %constant_dynamic-slice_fusion.1 = (bf16[128,2048]{1,0:T(8,128)(2,1)}, bf16[128,2048]{1,0:T(8,128)(2,1)S(1)}) fusion(bf16[512,2048]{1,0:T(8,128)(2,1)} %refs_7_.1, s32[]{:T(128)S(6)} %add.23, s32[]{:T(128)S(6)} %select_n.13), kind=kLoop, calls=%fused_computation.4 | loop fusion | bytes 2097160 | tf_op jit(solution)/shard_map/slice | solution.py:578
  5.8 2.0 %collective-permute-start.2 = (bf16[128,2048]{1,0:T(8,128)(2,1)S(1)}, bf16[128,2048]{1,0:T(8,128)(2,1)S(1)}, u32[]{:S(2)}, u32[]{:S(2)}) collective-permute-start(bf16[128,2048]{1,0:T(8,128)(2,1)S(1)} %get-tuple-element.42), channel_id=1, source_target_pairs={{0,1},{1,0},{2,3},{3,2},{4,5},{5,4},{6,7},{7,6},{8,9},{9,8},{10,11... | collective-permute-start | bytes 1572872 | tf_op jit(solution)/shard_map/ppermute | solution.py:580
  7.8 0.7 pad_add_fusion.place_ref
  8.4 2.5 %collective-permute-done.refs_1_.refs_3_ = bf16[128,1024]{1,0:T(8,128)(2,1)S(1)} collective-permute-done((bf16[128,1024]{1,0:T(8,128)(2,1)}, bf16[128,1024]{1,0:T(8,128)(2,1)S(1)}, u32[]{:S(2)}, u32[]{:S(2)}) %collective-permute-start) | collective-permute-done | bytes 262176 | tf_op jit(solution)/shard_map/ppermute | solution.py:565
  11.0 0.7 copy-done.11
  11.7 4.3 %request_project.1 = (bf16[256,512]{1,0:T(8,128)(2,1)}, bf16[128,512]{1,0:T(8,128)(2,1)}, bf16[128,256]{1,0:T(8,128)(2,1)}) custom-call(s32[2]{0:T(128)} %pad_add_fusion.place_ref, bf16[128,1024]{1,0:T(8,128)(2,1)} %refs_2_.1, bf16[128,1024]{1,0:T(8,128)(2,1)} %copy-done.11, f32[1,2048]{1,0:T(1,128)} %bitcast.17, s32[1,128]{1,0:T(1,128)} %bitcast.19, ...), custom_call_target="tpu_custom_call" | custom-call | flops 402653184 | bytes 3145728 | tf_op jit(solution)/shard_map/request_project/pallas_call | solution.py:670
  16.0 0.6 collective-permute-done.1.refs_1_
  16.6 6.6 %all-to-all-start = ((bf16[16,16,512]{2,1,0:T(8,128)(2,1)}), bf16[16,16,512]{2,1,0:T(8,128)(2,1)}, u32[]{:S(2)}, u32[]{:S(2)}) async-start(bf16[16,16,512]{2,1,0:T(8,128)(2,1)} %bitcast.16), calls=%async_computation | async-start | bytes 524288 | tf_op jit(solution)/shard_map/all_to_all | solution.py:685
  23.2 1.6 %collective-permute-start.3 = (bf16[128,2048]{1,0:T(8,128)(2,1)}, bf16[128,2048]{1,0:T(8,128)(2,1)S(1)}, u32[]{:S(2)}, u32[]{:S(2)}) collective-permute-start(bf16[128,2048]{1,0:T(8,128)(2,1)} %get-tuple-element.45), channel_id=1, source_target_pairs={{0,1},{1,0},{2,3},{3,2},{4,5},{5,4},{6,7},{7,6},{8,9},{9,8},{10,11... | collective-permute-start | bytes 1572872 | tf_op jit(solution)/shard_map/ppermute | solution.py:580
  24.7 9.7 %prompt_attention.1 = (bf16[128,512]{1,0:T(8,128)(2,1)}, f32[128,640]{1,0:T(8,128)}) custom-call(s32[2]{0:T(128)} %pad_add_fusion.place_ref, bf16[128,1024]{1,0:T(8,128)(2,1)} %refs_0_.3, bf16[128,1024]{1,0:T(8,128)(2,1)} %copy-done.17, f32[1,2048]{1,0:T(1,128)} %bitcast.18, bf16[2048,512]{1,0:T(8,128)(2,1)} %refs_3_.1, bf16[2048,256]{1,0:T(8,128)(2,1)} %refs_4_.3, ...), custom_call_target="tpu_custom_call" | custom-call | flops 1476395008 | bytes 4194304 | tf_op jit(solution)/shard_map/prompt_attention/pallas_call | solution.py:703
  34.4 0.6 collective-permute-start.4
  35.1 7.6 %slot_attention.1 = bf16[256,640]{1,0:T(8,128)(2,1)} custom-call(bf16[256,512]{1,0:T(8,128)(2,1)} %bitcast.5.q_hbm, bf16[2048,256]{1,0:T(8,128)(2,1)} %prefix_hbm.1), custom_call_target="tpu_custom_call" | custom-call | flops 2147483648 | bytes 1048576 | tf_op jit(solution)/shard_map/slot_attention/pallas_call | solution.py:735
  42.7 0.5 collective-permute-start.6
  43.2 5.9 %all-to-all-start.1 = ((bf16[16,16,640]{2,1,0:T(8,128)(2,1)}), bf16[16,16,640]{2,1,0:T(8,128)(2,1)S(1)}, u32[]{:S(2)}, u32[]{:S(2)}) async-start(bf16[16,16,640]{2,1,0:T(8,128)(2,1)} %bitcast.15), calls=%async_computation.1 | async-start | bytes 655360 | tf_op jit(solution)/shard_map/all_to_all | solution.py:761
  49.1 0.8 copy-done.8
  50.1 9.8 %mlp.1 = (bf16[128,1024]{1,0:T(8,128)(2,1)}, bf16[128,1024]{1,0:T(8,128)(2,1)}, bf16[128,1024]{1,0:T(8,128)(2,1)}) custom-call(s32[2]{0:T(128)} %pad_add_fusion.place_ref, bf16[128,1024]{1,0:T(8,128)(2,1)} %refs_0_.3, bf16[128,1024]{1,0:T(8,128)(2,1)} %copy-done.17, bf16[128,512]{1,0:T(8,128)(2,1)} %get-tuple-element.48.refs_2_, ...), custom_call_target="tpu_custom_call" | custom-call | flops 2013265920 | bytes 15728640 | tf_op jit(solution)/shard_map/mlp/pallas_call | solution.py:600
  59.9 0.3 all-to-all-done.1
  60.2 0.7 copy-done.16
  60.9 2.5 %merge.1.refs_5_ = bf16[128,512]{1,0:T(8,128)(2,1)} custom-call(s32[1,128]{1,0:T(1,128)} %bitcast.20, bf16[256,640]{1,0:T(8,128)(2,1)} %bitcast.14, f32[128,640]{1,0:T(8,128)} %get-tuple-element.59.refs_2_), custom_call_target="tpu_custom_call" | custom-call | flops 67108864 | bytes 524288 | tf_op jit(solution)/shard_map/merge/pallas_call | solution.py:767
  63.4 1.6 %collective-permute-start.8 = (bf16[128,512]{1,0:T(8,128)(2,1)}, bf16[128,512]{1,0:T(8,128)(2,1)S(1)}, u32[]{:S(2)}, u32[]{:S(2)}) collective-permute-start(bf16[128,512]{1,0:T(8,128)(2,1)} %merge.1.refs_5_), channel_id=1, source_target_pairs={{0,1},{1,0},{2,3},{3,2},{4,5},{5,4},{6,7},{7,6},{8,9},{9,8},{10,11... | collective-permute-start | bytes 393224 | tf_op jit(solution)/shard_map/ppermute | solution.py:565
  65.0 0.5 collective-permute-start.7
  65.5 2.5 %copy-done = bf16[2048,1280]{1,0:T(8,128)(2,1)S(1)} copy-done((bf16[2048,1280]{1,0:T(8,128)(2,1)S(1)}, bf16[2048,1280]{1,0:T(8,128)(2,1)}, u32[]{:S(2)}) %copy-start) | copy-done | bytes 5242904
  68.0 3.1 %load.1 = (bf16[2048,1280]{1,0:T(8,128)(2,1)S(1)}, bf16[2048,1280]{1,0:T(8,128)(2,1)S(1)}) custom-call(bf16[2048,1280]{1,0:T(8,128)(2,1)S(1)} %copy-done, bf16[2048,1280]{1,0:T(8,128)(2,1)} %refs_1_), custom_call_target="tpu_custom_call" | custom-call | bytes 10485760 | tf_op jit(solution)/shard_map/load/pallas_call | solution.py:460
  71.2 0.2 copy-done.5
  71.5 0.2 copy-done.9
  71.8 4.6 %tail.1 = (bf16[128,1024]{1,0:T(8,128)(2,1)S(1)}, bf16[128,1280]{1,0:T(8,128)(2,1)S(1)}, bf16[128,1024]{1,0:T(8,128)(2,1)S(1)}) custom-call(s32[2]{0:T(128)S(1)} %copy-done.15, bf16[2048,1280]{1,0:T(8,128)(2,1)S(1)} %get-tuple-element.62.refs_0_, bf16[2048,1280]{1,0:T(8,128)(2,1)S(1)} %get-tuple-element.63.refs_1_, bf16[128,1024]{1,0:T(8,128)(2,1)S(1)} %copy-done.10, ...), custom_call_target="tpu_custom_call" | custom-call | flops 1677721600 | bytes 7864320 | tf_op jit(solution)/shard_map/tail/pallas_call | solution.py:538
  76.4 1.6 %collective-permute-start.9 = (bf16[128,1024]{1,0:T(8,128)(2,1)S(1)}, bf16[128,1024]{1,0:T(8,128)(2,1)S(1)}, u32[]{:S(2)}, u32[]{:S(2)}) collective-permute-start(bf16[128,1024]{1,0:T(8,128)(2,1)S(1)} %get-tuple-element.67), channel_id=1, source_target_pairs={{0,1},{1,0},{2,3},{3,2},{4,5},{5,4},{6,7},{7,6},{8,9},{9,8},{10,11... | collective-permute-start | bytes 786440 | tf_op jit(solution)/shard_map/ppermute | solution.py:559
  78.0 1.6 %keep.1 = f32[128,1024]{1,0:T(8,128)S(1)} custom-call(s32[2]{0:T(128)S(1)} %copy-done.15, bf16[128,1280]{1,0:T(8,128)(2,1)S(1)} %get-tuple-element.65.hidden_ref, bf16[128,1024]{1,0:T(8,128)(2,1)S(1)} %get-tuple-element.66.residual_ref, bf16[1280,2048]{1,0:T(8,128)(2,1)S(1)} %bitcast.11), custom_call_target="tpu_custom_call" | custom-call | flops 335544320 | bytes 2621440 | tf_op jit(solution)/shard_map/keep/pallas_call | solution.py:549
  79.6 0.8 add_convert_fusion.1
  80.5 3.8 %collective-permute-done.9 = bf16[128,1024]{1,0:T(8,128)(2,1)S(1)} collective-permute-done((bf16[128,1024]{1,0:T(8,128)(2,1)S(1)}, bf16[128,1024]{1,0:T(8,128)(2,1)S(1)}, u32[]{:S(2)}, u32[]{:S(2)}) %collective-permute-start.9) | collective-permute-done | bytes 262176 | tf_op jit(solution)/shard_map/ppermute | solution.py:559
  84.3 0.8 add_convert_fusion
  (51 shorter events, 0.6 us)
Async XLA Ops:
  0.6 10.4 %collective-permute-start = (bf16[128,1024]{1,0:T(8,128)(2,1)}, bf16[128,1024]{1,0:T(8,128)(2,1)S(1)}, u32[]{:S(2)}, u32[]{:S(2)}) collective-permute-start(bf16[128,1024]{1,0:T(8,128)(2,1)} %refs_2_.1), channel_id=1, source_target_pairs={{0,1},{1,0},{2,3},{3,2},{4,5},{5,4},{6,7},{7,6},{8,9},{9,8},{10,11... | collective-permute-start | bytes 786440 | tf_op jit(solution)/shard_map/ppermute | solution.py:565
  5.8 10.8 %collective-permute-start.1 = (bf16[128,1024]{1,0:T(8,128)(2,1)}, bf16[128,1024]{1,0:T(8,128)(2,1)S(1)}, u32[]{:S(2)}, u32[]{:S(2)}) collective-permute-start(bf16[128,1024]{1,0:T(8,128)(2,1)} %refs_0_.3), channel_id=1, source_target_pairs={{0,1},{1,0},{2,3},{3,2},{4,5},{5,4},{6,7},{7,6},{8,9},{9,8},{10,11... | collective-permute-start | bytes 786440 | tf_op jit(solution)/shard_map/ppermute | solution.py:565
  5.8 29.2 %collective-permute-start.2 = (bf16[128,2048]{1,0:T(8,128)(2,1)S(1)}, bf16[128,2048]{1,0:T(8,128)(2,1)S(1)}, u32[]{:S(2)}, u32[]{:S(2)}) collective-permute-start(bf16[128,2048]{1,0:T(8,128)(2,1)S(1)} %get-tuple-element.42), channel_id=1, source_target_pairs={{0,1},{1,0},{2,3},{3,2},{4,5},{5,4},{6,7},{7,6},{8,9},{9,8},{10,11... | collective-permute-start | bytes 1572872 | tf_op jit(solution)/shard_map/ppermute | solution.py:580
  16.6 8.1 %copy-start.17 = (bf16[128,1024]{1,0:T(8,128)(2,1)}, bf16[128,1024]{1,0:T(8,128)(2,1)S(1)}, u32[]{:S(2)}) copy-start(bf16[128,1024]{1,0:T(8,128)(2,1)S(1)} %collective-permute-done.1.refs_1_) | copy-start | bytes 786436
  16.6 18.4 %all-to-all-start = ((bf16[16,16,512]{2,1,0:T(8,128)(2,1)}), bf16[16,16,512]{2,1,0:T(8,128)(2,1)}, u32[]{:S(2)}, u32[]{:S(2)}) async-start(bf16[16,16,512]{2,1,0:T(8,128)(2,1)} %bitcast.16), calls=%async_computation | async-start | bytes 524288 | tf_op jit(solution)/shard_map/all_to_all | solution.py:685
  23.2 19.6 %collective-permute-start.3 = (bf16[128,2048]{1,0:T(8,128)(2,1)}, bf16[128,2048]{1,0:T(8,128)(2,1)S(1)}, u32[]{:S(2)}, u32[]{:S(2)}) collective-permute-start(bf16[128,2048]{1,0:T(8,128)(2,1)} %get-tuple-element.45), channel_id=1, source_target_pairs={{0,1},{1,0},{2,3},{3,2},{4,5},{5,4},{6,7},{7,6},{8,9},{9,8},{10,11... | collective-permute-start | bytes 1572872 | tf_op jit(solution)/shard_map/ppermute | solution.py:580
  34.4 8.3 %collective-permute-start.4 = (bf16[128,512]{1,0:T(8,128)(2,1)}, bf16[128,512]{1,0:T(8,128)(2,1)S(1)}, u32[]{:S(2)}, u32[]{:S(2)}) collective-permute-start(bf16[128,512]{1,0:T(8,128)(2,1)} %get-tuple-element.48.refs_2_), channel_id=1, source_target_pairs={{0,1},{1,0},{2,3},{3,2},{4,5},{5,4},{6,7},{7,6},{8,9},{9,8},{10,11... | collective-permute-start | bytes 393224 | tf_op jit(solution)/shard_map/ppermute | solution.py:565
  35.0 15.0 %copy-start.2 = (bf16[128,2048]{1,0:T(8,128)(2,1)}, bf16[128,2048]{1,0:T(8,128)(2,1)S(1)}, u32[]{:S(2)}) copy-start(bf16[128,2048]{1,0:T(8,128)(2,1)S(1)} %collective-permute-done.2.refs_6_.refs_8_) | copy-start | bytes 1572868
  35.0 14.1 %collective-permute-start.5 = (bf16[128,2048]{1,0:T(8,128)(2,1)S(1)}, bf16[128,2048]{1,0:T(8,128)(2,1)S(1)}, u32[]{:S(2)}, u32[]{:S(2)}) collective-permute-start(bf16[128,2048]{1,0:T(8,128)(2,1)S(1)} %collective-permute-done.2.refs_6_.refs_8_), channel_id=1, source_target_pairs={{0,2},{2,0},{4,6},{6,4},{8,10},{10,8},{12,14},{14,12},{16,18},{18,... | collective-permute-start | bytes 1572872 | tf_op jit(solution)/shard_map/ppermute | solution.py:584
  42.7 7.3 %copy-start.20 = (bf16[128,512]{1,0:T(8,128)(2,1)}, bf16[128,512]{1,0:T(8,128)(2,1)S(1)}, u32[]{:S(2)}) copy-start(bf16[128,512]{1,0:T(8,128)(2,1)S(1)} %collective-permute-done.4.refs_3_) | copy-start | bytes 393220
  42.7 7.2 %copy-start.4 = (bf16[128,2048]{1,0:T(8,128)(2,1)}, bf16[128,2048]{1,0:T(8,128)(2,1)S(1)}, u32[]{:S(2)}) copy-start(bf16[128,2048]{1,0:T(8,128)(2,1)S(1)} %collective-permute-done.3.refs_7_.refs_9_) | copy-start | bytes 1572868
  42.7 6.4 %collective-permute-start.6 = (bf16[128,2048]{1,0:T(8,128)(2,1)S(1)}, bf16[128,2048]{1,0:T(8,128)(2,1)S(1)}, u32[]{:S(2)}, u32[]{:S(2)}) collective-permute-start(bf16[128,2048]{1,0:T(8,128)(2,1)S(1)} %collective-permute-done.3.refs_7_.refs_9_), channel_id=1, source_target_pairs={{0,2},{2,0},{4,6},{6,4},{8,10},{10,8},{12,14},{14,12},{16,18},{18,... | collective-permute-start | bytes 1572872 | tf_op jit(solution)/shard_map/ppermute | solution.py:584
  43.2 17.0 %all-to-all-start.1 = ((bf16[16,16,640]{2,1,0:T(8,128)(2,1)}), bf16[16,16,640]{2,1,0:T(8,128)(2,1)S(1)}, u32[]{:S(2)}, u32[]{:S(2)}) async-start(bf16[16,16,640]{2,1,0:T(8,128)(2,1)} %bitcast.15), calls=%async_computation.1 | async-start | bytes 655360 | tf_op jit(solution)/shard_map/all_to_all | solution.py:761
  49.1 1.0 %copy-start.6 = (bf16[128,2048]{1,0:T(8,128)(2,1)}, bf16[128,2048]{1,0:T(8,128)(2,1)S(1)}, u32[]{:S(2)}) copy-start(bf16[128,2048]{1,0:T(8,128)(2,1)S(1)} %collective-permute-done.5.refs_8_.refs_10_) | copy-start | bytes 1572868
  60.9 10.2 %copy-start.10 = (bf16[128,1024]{1,0:T(8,128)(2,1)S(1)}, bf16[128,1024]{1,0:T(8,128)(2,1)}, u32[]{:S(2)}) copy-start(bf16[128,1024]{1,0:T(8,128)(2,1)} %refs_2_.1) | copy-start | bytes 786436
  60.9 10.2 %copy-start.14 = (f32[2048]{0:T(1024)S(1)}, f32[2048]{0:T(1024)}, u32[]{:S(2)}) copy-start(f32[2048]{0:T(1024)} %param.24) | copy-start | bytes 24580
  60.9 10.2 %copy-start.15 = (s32[2]{0:T(128)S(1)}, s32[2]{0:T(128)}, u32[]{:S(2)}) copy-start(s32[2]{0:T(128)} %pad_add_fusion.place_ref) | copy-start | bytes 28
  63.4 7.7 %collective-permute-start.8 = (bf16[128,512]{1,0:T(8,128)(2,1)}, bf16[128,512]{1,0:T(8,128)(2,1)S(1)}, u32[]{:S(2)}, u32[]{:S(2)}) collective-permute-start(bf16[128,512]{1,0:T(8,128)(2,1)} %merge.1.refs_5_), channel_id=1, source_target_pairs={{0,1},{1,0},{2,3},{3,2},{4,5},{5,4},{6,7},{7,6},{8,9},{9,8},{10,11... | collective-permute-start | bytes 393224 | tf_op jit(solution)/shard_map/ppermute | solution.py:565
  65.0 14.6 %collective-permute-start.7 = (bf16[128,1024]{1,0:T(8,128)(2,1)}, bf16[128,1024]{1,0:T(8,128)(2,1)S(1)}, u32[]{:S(2)}, u32[]{:S(2)}) collective-permute-start(bf16[128,1024]{1,0:T(8,128)(2,1)} %get-tuple-element.57), channel_id=1, source_target_pairs={{0,1},{1,0},{2,3},{3,2},{4,5},{5,4},{6,7},{7,6},{8,9},{9,8},{10,11... | collective-permute-start | bytes 786440 | tf_op jit(solution)/shard_map/ppermute | solution.py:617
  65.5 2.5 %copy-start = (bf16[2048,1280]{1,0:T(8,128)(2,1)S(1)}, bf16[2048,1280]{1,0:T(8,128)(2,1)}, u32[]{:S(2)}) copy-start(bf16[2048,1280]{1,0:T(8,128)(2,1)} %refs_0_.4) | copy-start | bytes 15728644
  68.0 3.2 %copy-start.1 = (bf16[512,2048]{1,0:T(8,128)(2,1)S(1)}, bf16[512,2048]{1,0:T(8,128)(2,1)}, u32[]{:S(2)}) copy-start(bf16[512,2048]{1,0:T(8,128)(2,1)} %refs_7_.1) | copy-start | bytes 6291460
  68.0 3.2 %copy-start.3 = (bf16[128,2048]{1,0:T(8,128)(2,1)S(1)}, bf16[128,2048]{1,0:T(8,128)(2,1)}, u32[]{:S(2)}) copy-start(bf16[128,2048]{1,0:T(8,128)(2,1)} %copy-done.2) | copy-start | bytes 1572868
  68.0 3.4 %copy-start.5 = (bf16[128,2048]{1,0:T(8,128)(2,1)S(1)}, bf16[128,2048]{1,0:T(8,128)(2,1)}, u32[]{:S(2)}) copy-start(bf16[128,2048]{1,0:T(8,128)(2,1)} %copy-done.4) | copy-start | bytes 1572868
  68.0 3.5 %copy-start.7 = (bf16[128,2048]{1,0:T(8,128)(2,1)S(1)}, bf16[128,2048]{1,0:T(8,128)(2,1)}, u32[]{:S(2)}) copy-start(bf16[128,2048]{1,0:T(8,128)(2,1)} %copy-done.6) | copy-start | bytes 1572868
  68.0 3.7 %copy-start.9 = (bf16[128,2048]{1,0:T(8,128)(2,1)S(1)}, bf16[128,2048]{1,0:T(8,128)(2,1)}, u32[]{:S(2)}) copy-start(bf16[128,2048]{1,0:T(8,128)(2,1)} %copy-done.8) | copy-start | bytes 1572868
  68.0 3.7 %copy-start.12 = (bf16[128,1024]{1,0:T(8,128)(2,1)S(1)}, bf16[128,1024]{1,0:T(8,128)(2,1)}, u32[]{:S(2)}) copy-start(bf16[128,1024]{1,0:T(8,128)(2,1)} %copy-done.11) | copy-start | bytes 786436
  68.0 3.8 %copy-start.13 = (bf16[128,512]{1,0:T(8,128)(2,1)S(1)}, bf16[128,512]{1,0:T(8,128)(2,1)}, u32[]{:S(2)}) copy-start(bf16[128,512]{1,0:T(8,128)(2,1)} %merge.1.refs_5_) | copy-start | bytes 393220
  68.0 10.0 %slice-start = ((s8[5242880]{0:T(1024)(128)(4,1)}), s8[4194304]{0:T(1024)(128)(4,1)S(1)}, s32[]{:S(2)}) async-start(s8[5242880]{0:T(1024)(128)(4,1)} %bitcast.10), calls=%async_computation.2 | async-start | bytes 8388608
  71.8 6.2 %slice-start.1 = ((s8[5242880]{0:T(1024)(128)(4,1)}), s8[1048576]{0:T(1024)(128)(4,1)S(1)}, s32[]{:S(2)}) async-start(s8[5242880]{0:T(1024)(128)(4,1)} %bitcast.10), calls=%async_computation.3 | async-start | bytes 2097152
  76.4 3.2 %copy-start.18 = (bf16[128,1024]{1,0:T(8,128)(2,1)S(1)}, bf16[128,1024]{1,0:T(8,128)(2,1)}, u32[]{:S(2)}) copy-start(bf16[128,1024]{1,0:T(8,128)(2,1)} %get-tuple-element.56) | copy-start | bytes 786436
  76.4 3.2 %copy-start.19 = (bf16[128,1024]{1,0:T(8,128)(2,1)S(1)}, bf16[128,1024]{1,0:T(8,128)(2,1)}, u32[]{:S(2)}) copy-start(bf16[128,1024]{1,0:T(8,128)(2,1)} %get-tuple-element.55) | copy-start | bytes 786436
  76.4 7.8 %collective-permute-start.9 = (bf16[128,1024]{1,0:T(8,128)(2,1)S(1)}, bf16[128,1024]{1,0:T(8,128)(2,1)S(1)}, u32[]{:S(2)}, u32[]{:S(2)}) collective-permute-start(bf16[128,1024]{1,0:T(8,128)(2,1)S(1)} %get-tuple-element.67), channel_id=1, source_target_pairs={{0,1},{1,0},{2,3},{3,2},{4,5},{5,4},{6,7},{7,6},{8,9},{9,8},{10,11... | collective-permute-start | bytes 786440 | tf_op jit(solution)/shard_map/ppermute | solution.py:559
  (3 other events, 2.3 us)

commit v4 on v3

--- a/solution.py
+++ b/solution.py
@@ -13,13 +13,16 @@
 PAIR = 2 * HEAD_SIZE
 GROUP = 8
 CHUNK = 256
+FILL = 32
 EPS = 1e-05
 FACTOR = HEAD_SIZE ** (-0.5) * math.log2(math.e)
 F32 = jnp.float32
 BF16 = jnp.bfloat16
 MIB = 1024 * 1024
 MOST_VMEM = 62 * MIB
-TAIL_VMEM = 36 * MIB
+REQUEST_VMEM = 40 * MIB
+TAIL_VMEM = 40 * MIB
+MERGE_VMEM = 40 * MIB
 ANY = pl.BlockSpec(memory_space=pl.ANY)
 HBM = pl.BlockSpec(memory_space=pltpu.HBM)
 HELD = pl.BlockSpec(memory_space=pltpu.VMEM)
@@ -133,28 +136,27 @@
 
 
 def request_kernel(count, per_peer, place_ref, *refs):
-    inputs = count + 4
-    sources, (send_ref, q_ref, kv_ref), refs = refs[:inputs], refs[inputs : inputs + 3], refs[inputs + 3 :]
-    held, (send_scr, q_scr, kv_scr, sems) = refs[:inputs], refs[inputs:]
+    inputs = count + 2
+    w_query_ref, keyval_weight_ref, *refs = refs
+    sources, (send_ref, both_ref), refs = refs[:inputs], refs[inputs : inputs + 2], refs[inputs + 2 :]
+    held, (send_scr, both_scr, sems) = refs[:inputs], refs[inputs:]
     copies, started = fetch(sources, held, sems)
-    gain_ref, target_ref, w_query_ref, keyval_weight_ref = held[count:]
-    for copy in started[: count + 2]:
+    gain_ref, target_ref = held[count:]
+    for copy in started:
         copy.wait()
     _, slot_row = slot_places(target_ref[...], per_peer)
     spread = lax.broadcasted_iota(jnp.int32, (send_scr.shape[0], slot_row.shape[1]), 0) == slot_row
     rows = in_order(place_ref, [ref[...] for ref in held[:count]])
     normed = rms_norm(rows.astype(F32), gain_ref[...])
-    started[count + 2].wait()
     queries = jnp.dot(normed, w_query_ref[...], preferred_element_type=F32).astype(BF16)
     send_scr[...] = jnp.dot(
         spread.astype(BF16), queries, preferred_element_type=F32
     ).astype(BF16)
     copies.start(send_scr, send_ref)
-    q_scr[...] = queries
-    copies.start(q_scr, q_ref)
-    started[count + 3].wait()
-    kv_scr[...] = jnp.dot(normed, keyval_weight_ref[...], preferred_element_type=F32).astype(BF16)
-    copies.start(kv_scr, kv_ref)
+    width = queries.shape[1]
+    both_scr[:, :width] = queries
+    both_scr[:, width:] = jnp.dot(normed, keyval_weight_ref[...], preferred_element_type=F32).astype(BF16)
+    copies.start(both_scr, both_ref)
     copies.wait()
 
 
@@ -227,14 +229,14 @@
 
 
 def prompt_kernel(count, place_ref, *refs):
-    inputs = count + 8
+    inputs = count + 7
     sources, (att_ref, past_ref), refs = refs[:inputs], refs[inputs : inputs + 2], refs[inputs + 2 :]
     held, (q_scr, kvx_scr, att_scr, past_scr, *past_scrs, sems) = refs[:inputs], refs[inputs:]
     copies, started = fetch(sources, held, sems)
     for copy in started[: count + 1]:
         copy.wait()
     gain_ref, w_query_ref, keyval_weight_ref, prefix_ref = held[count : count + 4]
-    request_q_ref, request_kv_ref, len_ref, cache_ref = held[count + 4 :]
+    projected_ref, len_ref, cache_ref = held[count + 4 :]
     rows = in_order(place_ref, [ref[...] for ref in held[:count]])
     normed = rms_norm(rows.astype(F32), gain_ref[...])
     started[count + 1].wait()
@@ -282,8 +284,8 @@
     for copy in started[count + 4 :]:
         copy.wait()
     past_attention(
-        request_q_ref[...],
-        request_kv_ref[...],
+        projected_ref[:, : heads * HEAD_SIZE],
+        projected_ref[:, heads * HEAD_SIZE :],
         column_of(len_ref[...]),
         cache_ref,
         past_scr,
@@ -480,16 +482,20 @@
 
 
 def tail_kernel(place_ref, *refs):
-    w_gate, w_up, sources, pieces, w_down_hbm = refs[0], refs[1], refs[2:8], refs[8:12], refs[12]
+    w_gate, sources, pieces, w_up_hbm, w_down_hbm = refs[0], refs[1:7], refs[7:11], refs[11], refs[12]
     send_ref, hidden_ref, residual_ref = refs[13:16]
-    held, (w_out_other, w_down, send_scr, sems) = refs[16:22], refs[22:]
+    held, (w_out_other, w_up, w_down, send_scr, sems) = refs[16:22], refs[22:]
     own_ref, other_ref, gain_ref, att_ref, att_other_ref, w_out_ref = held
     width = send_scr.shape[1]
     hidden_width = w_gate.shape[1]
     away = pl.ds(pl.multiple_of((1 - place_ref[0]) * width, width), width)
     copies, started = fetch(sources, held, sems)
     arriving = start_pieces(copies, place_ref, pieces, w_out_other)
-    down = copies.start(w_down_hbm.at[:, away], w_down)
+    chunks = [
+        pl.ds(start, min(CHUNK, hidden_width - start)) for start in range(0, hidden_width, CHUNK)
+    ]
+    ups = [copies.start(w_up_hbm.at[:, at], w_up.at[:, at]) for at in chunks]
+    downs = [copies.start(w_down_hbm.at[at, away], w_down.at[at]) for at in chunks]
     copies.flying = []
     for copy in started:
         copy.wait()
@@ -503,16 +509,21 @@
     normed = rms_norm(residual.astype(F32), gain_ref[...])
     residual_ref[...] = jnp.where(place_ref[0] == 0, residual[:, :width], residual[:, width:])
     hidden = []
-    for start in range(0, hidden_width, CHUNK):
-        at = slice(start, min(start + CHUNK, hidden_width))
+    for at, copy in zip(chunks, ups):
         gate_act = jnp.dot(normed, w_gate[:, at], preferred_element_type=F32)
+        copy.wait()
         up_act = jnp.dot(normed, w_up[:, at], preferred_element_type=F32)
         hidden.append((gate_act / (1.0 + jnp.exp(-gate_act)) * up_act).astype(BF16))
     hidden = jnp.concatenate(hidden, axis=1)
-    down.wait()
-    send_scr[...] = jnp.dot(hidden, w_down[...], preferred_element_type=F32).astype(BF16)
+    hidden_ref[...] = hidden
+    split = chunks[-1].start
+    for copy in downs[:-1]:
+        copy.wait()
+    total = jnp.dot(hidden[:, :split], w_down[:split], preferred_element_type=F32)
+    downs[-1].wait()
+    total += jnp.dot(hidden[:, split:], w_down[split:], preferred_element_type=F32)
+    send_scr[...] = total.astype(BF16)
     copies.start(send_scr, send_ref)
-    hidden_ref[...] = hidden
     copies.wait()
 
 
@@ -527,25 +538,29 @@
 
 
 def tail(place, parts, attended, gain, w_outs, w_gate, w_up, w_down):
-    attended, w_gate, w_up = lax.optimization_barrier((attended, w_gate, w_up))
+    attended, w_gate = lax.optimization_barrier((attended, w_gate))
     rows, width = parts[0].shape
     hidden = w_up.shape[1]
-    held = load(TAIL_VMEM, w_gate, w_up)
+    held = load(TAIL_VMEM, w_gate)
     sources = (*parts, gain, *swap(attended, 2), w_outs[0])
     half = jax.ShapeDtypeStruct((rows, width), BF16)
     units = jax.ShapeDtypeStruct((rows, hidden), BF16)
     half_down = pltpu.VMEM((hidden, width), BF16)
     send, units, residual = pl.pallas_call(
         tail_kernel,
-        in_specs=[SCALAR] + [HELD] * 2 + [ANY] * 11,
+        in_specs=[SCALAR, HELD] + [ANY] * (len(sources) + 6),
         out_specs=[HBM, HELD, HELD],
         out_shape=[half, units, half],
-        scratch_shapes=scratch_like(*sources, w_outs[0])
-        + [half_down, pltpu.VMEM((rows, width), BF16), pltpu.SemaphoreType.DMA((12,))],
+        scratch_shapes=scratch_like(*sources, w_outs[0], w_up)
+        + [
+            half_down,
+            pltpu.VMEM((rows, width), BF16),
+            pltpu.SemaphoreType.DMA((12 + 2 * -(-hidden // CHUNK),)),
+        ],
         compiler_params=params(TAIL_VMEM),
         cost_estimate=cost(10 * rows * width * hidden, 6 * width * hidden, rows * hidden),
         name="tail",
-    )(place, *held, *sources, *w_outs[1:], w_down)
+    )(place, *held, *sources, *w_outs[1:], w_up, w_down)
     kept = pl.pallas_call(
         keep_kernel,
         in_specs=[SCALAR] + [HELD] * 2 + [ANY],
@@ -606,7 +621,7 @@
         + scratch_like(*operands, *outs)
         + [pltpu.SemaphoreType.DMA((copies,))],
         compiler_params=params(),
-        cost_estimate=cost(6 * rows * model * hidden, 6 * model * hidden, rows * hidden),
+        cost_estimate=cost(FILL * 6 * rows * model * hidden, 6 * model * hidden, rows * hidden),
         name="mlp",
     )(place, *operands, *w_outs, *weights)
 
@@ -661,27 +676,24 @@
     cached = request_keyval_cache.shape[1]
     w_outs, prompt_rows = share_rows(w_out, count, replicas, prompt_rows)
     prompt_parts = swap(prompt_rows, count)
-    operands = (*request_parts, attn_gain, target, w_query, keyval_weight)
+    operands = (*request_parts, attn_gain, target)
+    held = load(REQUEST_VMEM, w_query, keyval_weight)
     outs = [
         jax.ShapeDtypeStruct((slots, width), BF16),
-        jax.ShapeDtypeStruct((requests, width), BF16),
-        jax.ShapeDtypeStruct((requests, kv_width), BF16),
+        jax.ShapeDtypeStruct((requests, width + kv_width), BF16),
     ]
-    send, queries, keyval = pl.pallas_call(
+    send, projected = pl.pallas_call(
         functools.partial(request_kernel, count, per_peer),
-        in_specs=[SCALAR] + [ANY] * len(operands),
-        out_specs=[HBM] * 3,
+        in_specs=[SCALAR, HELD, HELD] + [ANY] * len(operands),
+        out_specs=[HBM] * 2,
         out_shape=outs,
         scratch_shapes=scratch_like(*operands, *outs)
         + [pltpu.SemaphoreType.DMA((len(operands) + 3,))],
-        compiler_params=params(),
-        cost_estimate=cost(
-            2 * requests * model * (width + kv_width), 2 * model * (width + kv_width)
-        ),
+        compiler_params=params(REQUEST_VMEM),
+        cost_estimate=cost(0, 0),
         name="request_project",
-    )(place, *operands)
-
-    send, prompt_parts[-1] = lax.optimization_barrier((send, prompt_parts[-1]))
+    )(place, *held, *operands)
+
     slot_queries = lax.all_to_all(send, "replica", split_axis=0, concat_axis=0, tiled=True)
 
     operands = (
@@ -690,8 +702,7 @@
         w_query,
         keyval_weight,
         prefix_cache,
-        queries,
-        keyval,
+        projected,
         cache_len.reshape(1, requests),
         request_keyval_cache,
     )
@@ -720,7 +731,7 @@
         ],
         compiler_params=params(),
         cost_estimate=cost(
-            2 * prompts * model * (width + kv_width) + 4 * prompts * heads * prefix_len * PAIR,
+            FILL * (2 * prompts * model * (width + kv_width)) + 4 * prompts * heads * prefix_len * PAIR,
             2 * model * (width + kv_width) + 2 * prefix_len * kv_width,
             prompts * heads * prefix_len,
         ),
@@ -753,9 +764,7 @@
         name="slot_attention",
     )(slot_queries, prefix_cache)
 
-    slot_out, w_outs, prompt_attended = lax.optimization_barrier(
-        (slot_out, w_outs, prompt_attended)
-    )
+    slot_out, w_outs = lax.optimization_barrier((slot_out, w_outs))
     if count == 2:
         w_outs = [w_out, *w_outs, *passed, pass_rows(w_outs[1], replicas)]
     back = lax.all_to_all(slot_out, "replica", split_axis=0, concat_axis=0, tiled=True)
@@ -771,7 +780,7 @@
         out_shape=jax.ShapeDtypeStruct((requests, width), BF16),
         scratch_shapes=scratch_like(*operands)
         + [pltpu.VMEM((requests, width), BF16), pltpu.SemaphoreType.DMA((4,))],
-        compiler_params=params(),
+        compiler_params=params(MERGE_VMEM),
         cost_estimate=cost(4 * requests * slots * width, 4 * slots * width),
         name="merge",
     )(*operands)

time: 85.5 us -> 81.4 us (0.952)
  Pallas kernels: 43 us -> 38.4 us
  local copies, waits for them, and re-layouts: 7.68 us -> 10.8 us
  starting transfers between devices: 23.8 us -> 22 us
    unnamed x46 -> x52, local copies, waits for them, and re-layouts: 5.56 us -> 8.55 us
    pallas_call x1 -> x2, Pallas kernels: 3.05 us -> 0.59 us  [load(): pl.pallas_call(load_kernel, in_specs=[ANY] * len(arrays), out_specs=[HELD...]
    pallas_call x1, Pallas kernels: 4.29 us -> 2.24 us  [body(): pl.pallas_call(functools.partial(request_kernel, count, per_peer), in_spe...]
    ppermute x4, waiting for transfers between devices: 3.17 us -> 1.39 us  [swap(): return [block, lax.ppermute(block, 'tensor', [(0, 1), (1, 0)])]]
    ppermute x2, starting transfers between devices: 3.54 us -> 2.04 us  [share_rows(): lax.ppermute(piece, 'tensor', [(0, 1), (1, 0)])]
    ppermute x1, waiting for transfers between devices: 3.78 us -> 5.23 us  [tail(): other = lax.ppermute(send, 'tensor', [(0, 1), (1, 0)])]
    pallas_call x1, Pallas kernels: 4.61 us -> 6.04 us  [tail(): pl.pallas_call(tail_kernel, in_specs=[SCALAR, HELD] + [ANY] * (len(source...]
    pallas_call x1, Pallas kernels: 2.47 us -> 1.07 us  [body(): pl.pallas_call(functools.partial(merge_kernel, per_peer), in_specs=[ANY]...]
  transfers between devices with their start and end apart: 12 -> 12, of which waited for: 4 -> 3; matrix products, arithmetic and copies ran while one was open for 4% -> 4% of each run, Pallas kernels for 48% -> 46%
where the time goes in v4:
time: 81.4 us; the launch traced here: 80.9 us
  Pallas kernels  38.4 us (47%)
  starting transfers between devices  22 us (27%)
  local copies, waits for them, and re-layouts  10.8 us (13%)
  waiting for transfers between devices  6.97 us (9%)
  other arithmetic  1.68 us (2%)
  between operations  0.99 us (1%)
    pallas_call x1, Pallas kernels, finish(): pl.pallas_call(functools.partial(mlp_kernel, count, len(w_outs)), in_spec...  9.89 us
    pallas_call x1, Pallas kernels, body(): pl.pallas_call(functools.partial(prompt_kernel, count), in_specs=[SCALAR]...  9.66 us
    unnamed x52, local copies, waits for them, and re-layouts  8.55 us
    pallas_call x1, Pallas kernels, body(): pl.pallas_call(slot_kernel, in_specs=[ANY, HBM], out_specs=HBM, out_shape...  7.5 us
    all_to_all x1, starting transfers between devices, body(): lax.all_to_all(send, 'replica', split_axis=0, concat_axis=0, tiled=True)  6.42 us
    pallas_call x1, Pallas kernels, tail(): pl.pallas_call(tail_kernel, in_specs=[SCALAR, HELD] + [ANY] * (len(source...  6.04 us
    all_to_all x1, starting transfers between devices, body(): lax.all_to_all(slot_out, 'replica', split_axis=0, concat_axis=0, tiled=True)  5.74 us
    ppermute x1, waiting for transfers between devices, tail(): other = lax.ppermute(send, 'tensor', [(0, 1), (1, 0)])  5.23 us
  transfers between devices with their start and end apart: 12, of which 3 were waited for; matrix products, arithmetic and copies ran while one was open for 4% of the time, Pallas kernels for 46%

profile of v4, /device:TPU:0, one launch (start us, length us, event | category | flops | bytes accessed | tf_op | source)
XLA Modules:
  0.0 80.9 jit_solution(3445420795090148594)
XLA Ops:
  0.7 3.0 %collective-permute-start = (bf16[128,1024]{1,0:T(8,128)(2,1)}, bf16[128,1024]{1,0:T(8,128)(2,1)S(1)}, u32[]{:S(2)}, u32[]{:S(2)}) collective-permute-start(bf16[128,1024]{1,0:T(8,128)(2,1)} %refs_1_.3), channel_id=1, source_target_pairs={{0,1},{1,0},{2,3},{3,2},{4,5},{5,4},{6,7},{7,6},{8,9},{9,8},{10,11... | collective-permute-start | bytes 786440 | tf_op jit(solution)/shard_map/ppermute | solution.py:580
  3.7 2.3 %constant_dynamic-slice_fusion.1 = (bf16[128,2048]{1,0:T(8,128)(2,1)}, bf16[128,2048]{1,0:T(8,128)(2,1)}) fusion(bf16[512,2048]{1,0:T(8,128)(2,1)} %refs_6_.1, s32[]{:T(128)S(6)} %add.23, s32[]{:T(128)S(6)} %select_n.13), kind=kLoop, calls=%fused_computation.4 | loop fusion | bytes 2097160 | tf_op jit(solution)/shard_map/slice | solution.py:593
  6.0 2.0 %collective-permute-start.2 = (bf16[128,2048]{1,0:T(8,128)(2,1)}, bf16[128,2048]{1,0:T(8,128)(2,1)S(1)}, u32[]{:S(2)}, u32[]{:S(2)}) collective-permute-start(bf16[128,2048]{1,0:T(8,128)(2,1)} %get-tuple-element.35), channel_id=1, source_target_pairs={{0,1},{1,0},{2,3},{3,2},{4,5},{5,4},{6,7},{7,6},{8,9},{9,8},{10,11... | collective-permute-start | bytes 1572872 | tf_op jit(solution)/shard_map/ppermute | solution.py:595
  8.0 1.6 %copy-done.2 = bf16[2048,512]{1,0:T(8,128)(2,1)S(1)} copy-done((bf16[2048,512]{1,0:T(8,128)(2,1)S(1)}, bf16[2048,512]{1,0:T(8,128)(2,1)}, u32[]{:S(2)}) %copy-start.2) | copy-done | bytes 2097176
  9.6 1.2 %copy-done.4 = bf16[2048,256]{1,0:T(8,128)(2,1)S(1)} copy-done((bf16[2048,256]{1,0:T(8,128)(2,1)S(1)}, bf16[2048,256]{1,0:T(8,128)(2,1)}, u32[]{:S(2)}) %copy-start.4) | copy-done | bytes 1048600
  10.9 0.2 load.2
  11.2 2.2 %request_project.1 = (bf16[256,512]{1,0:T(8,128)(2,1)}, bf16[128,768]{1,0:T(8,128)(2,1)S(1)}) custom-call(s32[2]{0:T(128)S(1)} %pad_add_fusion.place_ref, bf16[2048,512]{1,0:T(8,128)(2,1)S(1)} %get-tuple-element.29.refs_0_, bf16[2048,256]{1,0:T(8,128)(2,1)S(1)} %get-tuple-element.30.refs_1_, bf16[128,1024]{1,0:T(8,128)(2,1)S(1)} %copy-done.3, ...), custom_call_target="tpu_custom_call" | custom-call | tf_op jit(solution)/shard_map/request_project/pallas_call | solution.py:685
  13.5 0.7 copy-done.19
  14.1 6.4 %all-to-all-start = ((bf16[16,16,512]{2,1,0:T(8,128)(2,1)}), bf16[16,16,512]{2,1,0:T(8,128)(2,1)S(1)}, u32[]{:S(2)}, u32[]{:S(2)}) async-start(bf16[16,16,512]{2,1,0:T(8,128)(2,1)} %bitcast.4), calls=%async_computation | async-start | bytes 524288 | tf_op jit(solution)/shard_map/all_to_all | solution.py:697
  20.6 9.7 %prompt_attention.1 = (bf16[128,512]{1,0:T(8,128)(2,1)}, f32[128,640]{1,0:T(8,128)}) custom-call(s32[2]{0:T(128)} %copy-done.16, bf16[128,1024]{1,0:T(8,128)(2,1)} %refs_0_.3, bf16[128,1024]{1,0:T(8,128)(2,1)} %collective-permute-done.1.refs_1_, f32[1,2048]{1,0:T(1,128)} %bitcast.13, bf16[2048,512]{1,0:T(8,128)(2,1)} %refs_3_.1, bf16[2048,256]{1,0:T(8,128)(2,1)} %refs_4_.1, ...), custom_call_target="tpu_custom_call" | custom-call | flops 13958643712 | bytes 4194304 | tf_op jit(solution)/shard_map/prompt_attention/pallas_call | solution.py:714
  30.3 0.3 all-to-all-done
  30.6 0.7 copy-done.20
  31.3 7.5 %slot_attention.1 = bf16[256,640]{1,0:T(8,128)(2,1)} custom-call(bf16[256,512]{1,0:T(8,128)(2,1)} %bitcast.20, bf16[2048,256]{1,0:T(8,128)(2,1)} %prefix_hbm.1), custom_call_target="tpu_custom_call" | custom-call | flops 2147483648 | bytes 1048576 | tf_op jit(solution)/shard_map/slot_attention/pallas_call | solution.py:746
  39.0 0.4 collective-permute-start.5
  39.4 1.5 %collective-permute-start.4 = (bf16[128,512]{1,0:T(8,128)(2,1)}, bf16[128,512]{1,0:T(8,128)(2,1)S(1)}, u32[]{:S(2)}, u32[]{:S(2)}) collective-permute-start(bf16[128,512]{1,0:T(8,128)(2,1)} %get-tuple-element.40.refs_2_), channel_id=1, source_target_pairs={{0,1},{1,0},{2,3},{3,2},{4,5},{5,4},{6,7},{7,6},{8,9},{9,8},{10,11... | collective-permute-start | bytes 393224 | tf_op jit(solution)/shard_map/ppermute | solution.py:580
  40.9 5.7 %all-to-all-start.1 = ((bf16[16,16,640]{2,1,0:T(8,128)(2,1)}), bf16[16,16,640]{2,1,0:T(8,128)(2,1)S(1)}, u32[]{:S(2)}, u32[]{:S(2)}) async-start(bf16[16,16,640]{2,1,0:T(8,128)(2,1)} %bitcast.19), calls=%async_computation.1 | async-start | bytes 655360 | tf_op jit(solution)/shard_map/all_to_all | solution.py:770
  46.7 0.6 copy-done.23
  47.3 0.2 copy-done.9
  47.5 0.8 copy-done.11
  48.3 9.9 %mlp.1 = (bf16[128,1024]{1,0:T(8,128)(2,1)}, bf16[128,1024]{1,0:T(8,128)(2,1)}, bf16[128,1024]{1,0:T(8,128)(2,1)}) custom-call(s32[2]{0:T(128)} %copy-done.16, bf16[128,1024]{1,0:T(8,128)(2,1)} %refs_0_.3, bf16[128,1024]{1,0:T(8,128)(2,1)} %collective-permute-done.1.refs_1_, bf16[128,512]{1,0:T(8,128)(2,1)} %get-tuple-element.40.refs_2_, ...), custom_call_target="tpu_custom_call" | custom-call | flops 64424509440 | bytes 15728640 | tf_op jit(solution)/shard_map/mlp/pallas_call | solution.py:615
  58.3 1.1 %merge.1.refs_4_ = bf16[128,512]{1,0:T(8,128)(2,1)S(1)} custom-call(s32[1,128]{1,0:T(1,128)S(1)} %bitcast.18, bf16[256,640]{1,0:T(8,128)(2,1)S(1)} %bitcast.12, f32[128,640]{1,0:T(8,128)S(1)} %copy-done.13), custom_call_target="tpu_custom_call" | custom-call | flops 67108864 | bytes 524288 | tf_op jit(solution)/shard_map/merge/pallas_call | solution.py:776
  59.4 0.6 collective-permute-start.8
  60.0 1.5 %collective-permute-start.7 = (bf16[128,1024]{1,0:T(8,128)(2,1)}, bf16[128,1024]{1,0:T(8,128)(2,1)S(1)}, u32[]{:S(2)}, u32[]{:S(2)}) collective-permute-start(bf16[128,1024]{1,0:T(8,128)(2,1)} %get-tuple-element.48), channel_id=1, source_target_pairs={{0,1},{1,0},{2,3},{3,2},{4,5},{5,4},{6,7},{7,6},{8,9},{9,8},{10,11... | collective-permute-start | bytes 786440 | tf_op jit(solution)/shard_map/ppermute | solution.py:632
  61.5 2.5 %copy-done = bf16[2048,1280]{1,0:T(8,128)(2,1)S(1)} copy-done((bf16[2048,1280]{1,0:T(8,128)(2,1)S(1)}, bf16[2048,1280]{1,0:T(8,128)(2,1)}, u32[]{:S(2)}) %copy-start) | copy-done | bytes 5242904
  64.0 0.4 load.3.refs_0_
  64.3 1.4 %collective-permute-done.8.refs_5_ = bf16[128,512]{1,0:T(8,128)(2,1)S(1)} collective-permute-done((bf16[128,512]{1,0:T(8,128)(2,1)S(1)}, bf16[128,512]{1,0:T(8,128)(2,1)S(1)}, u32[]{:S(2)}, u32[]{:S(2)}) %collective-permute-start.8) | collective-permute-done | bytes 131104 | tf_op jit(solution)/shard_map/ppermute | solution.py:580
  65.9 6.0 %tail.1 = (bf16[128,1024]{1,0:T(8,128)(2,1)S(1)}, bf16[128,1280]{1,0:T(8,128)(2,1)S(1)}, bf16[128,1024]{1,0:T(8,128)(2,1)S(1)}) custom-call(s32[2]{0:T(128)S(1)} %copy-done.17, bf16[2048,1280]{1,0:T(8,128)(2,1)S(1)} %load.3.refs_0_, bf16[128,1024]{1,0:T(8,128)(2,1)S(1)} %copy-done.3, bf16[128,1024]{1,0:T(8,128)(2,1)S(1)} %collective-permute-done.refs_3_.refs_2_, ...), custom_call_target="tpu_custom_call" | custom-call | flops 1677721600 | bytes 7864320 | tf_op jit(solution)/shard_map/tail/pallas_call | solution.py:549
  72.0 0.6 collective-permute-start.9
  72.6 1.5 %keep.1 = f32[128,1024]{1,0:T(8,128)S(1)} custom-call(s32[2]{0:T(128)S(1)} %copy-done.17, bf16[128,1280]{1,0:T(8,128)(2,1)S(1)} %get-tuple-element.53.hidden_ref, bf16[128,1024]{1,0:T(8,128)(2,1)S(1)} %get-tuple-element.54.residual_ref, bf16[1280,2048]{1,0:T(8,128)(2,1)S(1)} %bitcast.11), custom_call_target="tpu_custom_call" | custom-call | flops 335544320 | bytes 2621440 | tf_op jit(solution)/shard_map/keep/pallas_call | solution.py:564
  74.1 0.8 %add_convert_fusion.1 = bf16[128,1024]{1,0:T(8,128)(2,1)} fusion(bf16[128,1024]{1,0:T(8,128)(2,1)S(1)} %collective-permute-done.7, bf16[128,1024]{1,0:T(8,128)(2,1)S(1)} %copy-done.21, bf16[128,1024]{1,0:T(8,128)(2,1)S(1)} %copy-done.22), kind=kLoop, calls=%fused_computation.1 | loop fusion | flops 786432 | bytes 1048576 | tf_op jit(solution)/shard_map/convert_element_type | solution.py:634
  74.9 5.2 %collective-permute-done.9 = bf16[128,1024]{1,0:T(8,128)(2,1)S(1)} collective-permute-done((bf16[128,1024]{1,0:T(8,128)(2,1)S(1)}, bf16[128,1024]{1,0:T(8,128)(2,1)S(1)}, u32[]{:S(2)}, u32[]{:S(2)}) %collective-permute-start.9) | collective-permute-done | bytes 262176 | tf_op jit(solution)/shard_map/ppermute | solution.py:574
  80.1 0.8 add_convert_fusion
  (58 shorter events, 0.7 us)
Async XLA Ops:
  0.6 10.5 %copy-start.3 = (bf16[128,1024]{1,0:T(8,128)(2,1)S(1)}, bf16[128,1024]{1,0:T(8,128)(2,1)}, u32[]{:S(2)}) copy-start(bf16[128,1024]{1,0:T(8,128)(2,1)} %refs_1_.3) | copy-start | bytes 786436
  0.6 10.5 %copy-start.14 = (f32[2048]{0:T(1024)S(1)}, f32[2048]{0:T(1024)}, u32[]{:S(2)}) copy-start(f32[2048]{0:T(1024)} %param.20) | copy-start | bytes 24580
  0.7 10.5 %copy-start.18 = (s32[128,1]{0,1:T(1,128)S(1)}, s32[128,1]{0,1:T(1,128)}, u32[]{:S(2)}) copy-start(s32[128,1]{0,1:T(1,128)} %param.18) | copy-start | bytes 1540
  0.7 10.5 %collective-permute-start = (bf16[128,1024]{1,0:T(8,128)(2,1)}, bf16[128,1024]{1,0:T(8,128)(2,1)S(1)}, u32[]{:S(2)}, u32[]{:S(2)}) collective-permute-start(bf16[128,1024]{1,0:T(8,128)(2,1)} %refs_1_.3), channel_id=1, source_target_pairs={{0,1},{1,0},{2,3},{3,2},{4,5},{5,4},{6,7},{7,6},{8,9},{9,8},{10,11... | collective-permute-start | bytes 786440 | tf_op jit(solution)/shard_map/ppermute | solution.py:580
  6.0 14.6 %collective-permute-start.1 = (bf16[128,1024]{1,0:T(8,128)(2,1)}, bf16[128,1024]{1,0:T(8,128)(2,1)}, u32[]{:S(2)}, u32[]{:S(2)}) collective-permute-start(bf16[128,1024]{1,0:T(8,128)(2,1)} %refs_0_.3), channel_id=1, source_target_pairs={{0,1},{1,0},{2,3},{3,2},{4,5},{5,4},{6,7},{7,6},{8,9},{9,8},{10,11... | collective-permute-start | bytes 786440 | tf_op jit(solution)/shard_map/ppermute | solution.py:580
  6.0 24.2 %collective-permute-start.2 = (bf16[128,2048]{1,0:T(8,128)(2,1)}, bf16[128,2048]{1,0:T(8,128)(2,1)S(1)}, u32[]{:S(2)}, u32[]{:S(2)}) collective-permute-start(bf16[128,2048]{1,0:T(8,128)(2,1)} %get-tuple-element.35), channel_id=1, source_target_pairs={{0,1},{1,0},{2,3},{3,2},{4,5},{5,4},{6,7},{7,6},{8,9},{9,8},{10,11... | collective-permute-start | bytes 1572872 | tf_op jit(solution)/shard_map/ppermute | solution.py:595
  8.0 30.8 %collective-permute-start.3 = (bf16[128,2048]{1,0:T(8,128)(2,1)}, bf16[128,2048]{1,0:T(8,128)(2,1)S(1)}, u32[]{:S(2)}, u32[]{:S(2)}) collective-permute-start(bf16[128,2048]{1,0:T(8,128)(2,1)} %get-tuple-element.38), channel_id=1, source_target_pairs={{0,1},{1,0},{2,3},{3,2},{4,5},{5,4},{6,7},{7,6},{8,9},{9,8},{10,11... | collective-permute-start | bytes 1572872 | tf_op jit(solution)/shard_map/ppermute | solution.py:595
  8.0 1.6 %copy-start.2 = (bf16[2048,512]{1,0:T(8,128)(2,1)S(1)}, bf16[2048,512]{1,0:T(8,128)(2,1)}, u32[]{:S(2)}) copy-start(bf16[2048,512]{1,0:T(8,128)(2,1)} %refs_3_.1) | copy-start | bytes 6291460
  11.2 9.4 %copy-start.16 = (s32[2]{0:T(128)}, s32[2]{0:T(128)S(1)}, u32[]{:S(2)}) copy-start(s32[2]{0:T(128)S(1)} %pad_add_fusion.place_ref) | copy-start | bytes 28
  14.1 16.5 %all-to-all-start = ((bf16[16,16,512]{2,1,0:T(8,128)(2,1)}), bf16[16,16,512]{2,1,0:T(8,128)(2,1)S(1)}, u32[]{:S(2)}, u32[]{:S(2)}) async-start(bf16[16,16,512]{2,1,0:T(8,128)(2,1)} %bitcast.4), calls=%async_computation | async-start | bytes 524288 | tf_op jit(solution)/shard_map/all_to_all | solution.py:697
  30.2 10.7 %copy-start.5 = (bf16[128,2048]{1,0:T(8,128)(2,1)}, bf16[128,2048]{1,0:T(8,128)(2,1)S(1)}, u32[]{:S(2)}) copy-start(bf16[128,2048]{1,0:T(8,128)(2,1)S(1)} %collective-permute-done.2.refs_6_.refs_7_) | copy-start | bytes 1572868
  38.8 9.5 %copy-start.7 = (bf16[128,2048]{1,0:T(8,128)(2,1)}, bf16[128,2048]{1,0:T(8,128)(2,1)S(1)}, u32[]{:S(2)}) copy-start(bf16[128,2048]{1,0:T(8,128)(2,1)S(1)} %collective-permute-done.3.refs_7_.refs_8_) | copy-start | bytes 1572868
  38.8 7.8 %collective-permute-start.6 = (bf16[128,2048]{1,0:T(8,128)(2,1)S(1)}, bf16[128,2048]{1,0:T(8,128)(2,1)S(1)}, u32[]{:S(2)}, u32[]{:S(2)}) collective-permute-start(bf16[128,2048]{1,0:T(8,128)(2,1)S(1)} %collective-permute-done.3.refs_7_.refs_8_), channel_id=1, source_target_pairs={{0,2},{2,0},{4,6},{6,4},{8,10},{10,8},{12,14},{14,12},{16,18},{18,... | collective-permute-start | bytes 1572872 | tf_op jit(solution)/shard_map/ppermute | solution.py:599
  39.0 7.7 %collective-permute-start.5 = (bf16[128,2048]{1,0:T(8,128)(2,1)S(1)}, bf16[128,2048]{1,0:T(8,128)(2,1)S(1)}, u32[]{:S(2)}, u32[]{:S(2)}) collective-permute-start(bf16[128,2048]{1,0:T(8,128)(2,1)S(1)} %collective-permute-done.2.refs_6_.refs_7_), channel_id=1, source_target_pairs={{0,2},{2,0},{4,6},{6,4},{8,10},{10,8},{12,14},{14,12},{16,18},{18,... | collective-permute-start | bytes 1572872 | tf_op jit(solution)/shard_map/ppermute | solution.py:599
  39.4 7.2 %collective-permute-start.4 = (bf16[128,512]{1,0:T(8,128)(2,1)}, bf16[128,512]{1,0:T(8,128)(2,1)S(1)}, u32[]{:S(2)}, u32[]{:S(2)}) collective-permute-start(bf16[128,512]{1,0:T(8,128)(2,1)} %get-tuple-element.40.refs_2_), channel_id=1, source_target_pairs={{0,1},{1,0},{2,3},{3,2},{4,5},{5,4},{6,7},{7,6},{8,9},{9,8},{10,11... | collective-permute-start | bytes 393224 | tf_op jit(solution)/shard_map/ppermute | solution.py:580
  40.9 17.3 %all-to-all-start.1 = ((bf16[16,16,640]{2,1,0:T(8,128)(2,1)}), bf16[16,16,640]{2,1,0:T(8,128)(2,1)S(1)}, u32[]{:S(2)}, u32[]{:S(2)}) async-start(bf16[16,16,640]{2,1,0:T(8,128)(2,1)} %bitcast.19), calls=%async_computation.1 | async-start | bytes 655360 | tf_op jit(solution)/shard_map/all_to_all | solution.py:770
  48.3 9.9 %copy-start.13 = (f32[128,640]{1,0:T(8,128)S(1)}, f32[128,640]{1,0:T(8,128)}, u32[]{:S(2)}) copy-start(f32[128,640]{1,0:T(8,128)} %get-tuple-element.50.refs_2_) | copy-start | bytes 983044
  58.2 7.5 %copy-start.6 = (bf16[128,2048]{1,0:T(8,128)(2,1)S(1)}, bf16[128,2048]{1,0:T(8,128)(2,1)}, u32[]{:S(2)}) copy-start(bf16[128,2048]{1,0:T(8,128)(2,1)} %copy-done.5) | copy-start | bytes 1572868
  58.3 7.5 %copy-start.15 = (f32[2048]{0:T(1024)S(1)}, f32[2048]{0:T(1024)}, u32[]{:S(2)}) copy-start(f32[2048]{0:T(1024)} %param.24) | copy-start | bytes 24580
  58.3 7.5 %copy-start.17 = (s32[2]{0:T(128)S(1)}, s32[2]{0:T(128)}, u32[]{:S(2)}) copy-start(s32[2]{0:T(128)} %copy-done.16) | copy-start | bytes 28
  59.4 6.4 %collective-permute-start.8 = (bf16[128,512]{1,0:T(8,128)(2,1)S(1)}, bf16[128,512]{1,0:T(8,128)(2,1)S(1)}, u32[]{:S(2)}, u32[]{:S(2)}) collective-permute-start(bf16[128,512]{1,0:T(8,128)(2,1)S(1)} %merge.1.refs_4_), channel_id=1, source_target_pairs={{0,1},{1,0},{2,3},{3,2},{4,5},{5,4},{6,7},{7,6},{8,9},{9,8},{10,11... | collective-permute-start | bytes 393224 | tf_op jit(solution)/shard_map/ppermute | solution.py:580
  60.0 14.1 %collective-permute-start.7 = (bf16[128,1024]{1,0:T(8,128)(2,1)}, bf16[128,1024]{1,0:T(8,128)(2,1)S(1)}, u32[]{:S(2)}, u32[]{:S(2)}) collective-permute-start(bf16[128,1024]{1,0:T(8,128)(2,1)} %get-tuple-element.48), channel_id=1, source_target_pairs={{0,1},{1,0},{2,3},{3,2},{4,5},{5,4},{6,7},{7,6},{8,9},{9,8},{10,11... | collective-permute-start | bytes 786440 | tf_op jit(solution)/shard_map/ppermute | solution.py:632
  61.4 2.5 %copy-start = (bf16[2048,1280]{1,0:T(8,128)(2,1)S(1)}, bf16[2048,1280]{1,0:T(8,128)(2,1)}, u32[]{:S(2)}) copy-start(bf16[2048,1280]{1,0:T(8,128)(2,1)} %refs_0_.4) | copy-start | bytes 15728644
  63.9 1.8 %copy-start.1 = (bf16[512,2048]{1,0:T(8,128)(2,1)S(1)}, bf16[512,2048]{1,0:T(8,128)(2,1)}, u32[]{:S(2)}) copy-start(bf16[512,2048]{1,0:T(8,128)(2,1)} %refs_6_.1) | copy-start | bytes 6291460
  63.9 1.8 %copy-start.8 = (bf16[128,2048]{1,0:T(8,128)(2,1)S(1)}, bf16[128,2048]{1,0:T(8,128)(2,1)}, u32[]{:S(2)}) copy-start(bf16[128,2048]{1,0:T(8,128)(2,1)} %copy-done.7) | copy-start | bytes 1572868
  63.9 1.8 %copy-start.10 = (bf16[128,2048]{1,0:T(8,128)(2,1)S(1)}, bf16[128,2048]{1,0:T(8,128)(2,1)}, u32[]{:S(2)}) copy-start(bf16[128,2048]{1,0:T(8,128)(2,1)} %copy-done.9) | copy-start | bytes 1572868
  63.9 2.0 %copy-start.12 = (bf16[128,2048]{1,0:T(8,128)(2,1)S(1)}, bf16[128,2048]{1,0:T(8,128)(2,1)}, u32[]{:S(2)}) copy-start(bf16[128,2048]{1,0:T(8,128)(2,1)} %copy-done.11) | copy-start | bytes 1572868
  63.9 8.6 %slice-start = ((s8[5242880]{0:T(1024)(128)(4,1)}), s8[4194304]{0:T(1024)(128)(4,1)S(1)}, s32[]{:S(2)}) async-start(s8[5242880]{0:T(1024)(128)(4,1)} %bitcast.10), calls=%async_computation.2 | async-start | bytes 8388608
  64.3 8.3 %slice-start.1 = ((s8[5242880]{0:T(1024)(128)(4,1)}), s8[1048576]{0:T(1024)(128)(4,1)S(1)}, s32[]{:S(2)}) async-start(s8[5242880]{0:T(1024)(128)(4,1)} %bitcast.10), calls=%async_computation.3 | async-start | bytes 2097152
  72.0 2.1 %copy-start.21 = (bf16[128,1024]{1,0:T(8,128)(2,1)S(1)}, bf16[128,1024]{1,0:T(8,128)(2,1)}, u32[]{:S(2)}) copy-start(bf16[128,1024]{1,0:T(8,128)(2,1)} %get-tuple-element.47) | copy-start | bytes 786436
  72.0 2.1 %copy-start.22 = (bf16[128,1024]{1,0:T(8,128)(2,1)S(1)}, bf16[128,1024]{1,0:T(8,128)(2,1)}, u32[]{:S(2)}) copy-start(bf16[128,1024]{1,0:T(8,128)(2,1)} %get-tuple-element.46) | copy-start | bytes 786436
  72.0 8.2 %collective-permute-start.9 = (bf16[128,1024]{1,0:T(8,128)(2,1)S(1)}, bf16[128,1024]{1,0:T(8,128)(2,1)S(1)}, u32[]{:S(2)}, u32[]{:S(2)}) collective-permute-start(bf16[128,1024]{1,0:T(8,128)(2,1)S(1)} %get-tuple-element.55), channel_id=1, source_target_pairs={{0,1},{1,0},{2,3},{3,2},{4,5},{5,4},{6,7},{7,6},{8,9},{9,8},{10,11... | collective-permute-start | bytes 786440 | tf_op jit(solution)/shard_map/ppermute | solution.py:574
  (6 other events, 4.9 us)

commit v5 on v4

--- a/solution.py
+++ b/solution.py
@@ -19,8 +19,10 @@
 F32 = jnp.float32
 BF16 = jnp.bfloat16
 MIB = 1024 * 1024
-MOST_VMEM = 62 * MIB
+MOST_VMEM = 61 * MIB
+MLP_VMEM = 60 * MIB
 REQUEST_VMEM = 40 * MIB
+SLOT_VMEM = 48 * MIB
 TAIL_VMEM = 40 * MIB
 MERGE_VMEM = 40 * MIB
 ANY = pl.BlockSpec(memory_space=pl.ANY)
@@ -135,11 +137,10 @@
     return [pltpu.VMEM(x.shape, x.dtype) for x in arrays]
 
 
-def request_kernel(count, per_peer, place_ref, *refs):
+def request_kernel(count, per_peer, place_ref, w_query_ref, *refs):
     inputs = count + 2
-    w_query_ref, keyval_weight_ref, *refs = refs
-    sources, (send_ref, both_ref), refs = refs[:inputs], refs[inputs : inputs + 2], refs[inputs + 2 :]
-    held, (send_scr, both_scr, sems) = refs[:inputs], refs[inputs:]
+    sources, send_ref, refs = refs[:inputs], refs[inputs], refs[inputs + 1 :]
+    held, (send_scr, sems) = refs[:inputs], refs[inputs:]
     copies, started = fetch(sources, held, sems)
     gain_ref, target_ref = held[count:]
     for copy in started:
@@ -153,10 +154,6 @@
         spread.astype(BF16), queries, preferred_element_type=F32
     ).astype(BF16)
     copies.start(send_scr, send_ref)
-    width = queries.shape[1]
-    both_scr[:, :width] = queries
-    both_scr[:, width:] = jnp.dot(normed, keyval_weight_ref[...], preferred_element_type=F32).astype(BF16)
-    copies.start(both_scr, both_ref)
     copies.wait()
 
 
@@ -229,21 +226,31 @@
 
 
 def prompt_kernel(count, place_ref, *refs):
-    inputs = count + 7
+    inputs = 2 * count + 6
     sources, (att_ref, past_ref), refs = refs[:inputs], refs[inputs : inputs + 2], refs[inputs + 2 :]
     held, (q_scr, kvx_scr, att_scr, past_scr, *past_scrs, sems) = refs[:inputs], refs[inputs:]
     copies, started = fetch(sources, held, sems)
-    for copy in started[: count + 1]:
+    first = 2 * count + 1
+    for copy in started[:first]:
         copy.wait()
-    gain_ref, w_query_ref, keyval_weight_ref, prefix_ref = held[count : count + 4]
-    projected_ref, len_ref, cache_ref = held[count + 4 :]
-    rows = in_order(place_ref, [ref[...] for ref in held[:count]])
+    gain_ref, w_query_ref, keyval_weight_ref, prefix_ref, len_ref, cache_ref = held[first - 1 :]
+    rows = jnp.concatenate(
+        [
+            in_order(place_ref, [ref[...] for ref in held[at : at + count]])
+            for at in (0, count)
+        ],
+        axis=0,
+    )
     normed = rms_norm(rows.astype(F32), gain_ref[...])
-    started[count + 1].wait()
-    queries = jnp.dot(normed, w_query_ref[...], preferred_element_type=F32).astype(BF16)
-    started[count + 2].wait()
-    keyval = jnp.dot(normed, keyval_weight_ref[...], preferred_element_type=F32).astype(BF16)
-    started[count + 3].wait()
+    started[first].wait()
+    both_queries = jnp.dot(normed, w_query_ref[...], preferred_element_type=F32).astype(BF16)
+    started[first + 1].wait()
+    both_keyval = jnp.dot(
+        normed, keyval_weight_ref[...], preferred_element_type=F32
+    ).astype(BF16)
+    started[first + 2].wait()
+    prompts = held[0].shape[0]
+    queries, keyval = both_queries[:prompts], both_keyval[:prompts]
     heads = queries.shape[1] // HEAD_SIZE
     row_count = queries.shape[0]
     for head in range(heads):
@@ -281,11 +288,11 @@
 
     pipelined(heads // 2, score, soften, settle)
     copies.start(att_scr, att_ref)
-    for copy in started[count + 4 :]:
+    for copy in started[first + 3 :]:
         copy.wait()
     past_attention(
-        projected_ref[:, : heads * HEAD_SIZE],
-        projected_ref[:, heads * HEAD_SIZE :],
+        both_queries[prompts:],
+        both_keyval[prompts:],
         column_of(len_ref[...]),
         cache_ref,
         past_scr,
@@ -295,16 +302,11 @@
     copies.wait()
 
 
-def slot_kernel(q_hbm, prefix_hbm, out_hbm, q_ref, prefix_ref, out_ref, q_scr, kvx_scr, sems):
-    copies, started = fetch((q_hbm, prefix_hbm), (q_ref, prefix_ref), sems)
-    started[0].wait()
+def slot_kernel(q_ref, prefix_ref, out_hbm, out_ref, kvx_scr, sems):
+    copies = Copies(sems)
     slots, width = q_ref.shape
     heads = width // HEAD_SIZE
     queries = q_ref[...]
-    for head in range(heads):
-        q_scr[head] = head_query(queries, head)
-    started[1].wait()
-    kvx_scr[...] = ones_for_keys(prefix_ref[...])
     lanes = lane_ids((slots, PAIR))
     sums = [jnp.zeros((slots, PAIR), F32)]
     even = []
@@ -314,7 +316,10 @@
         return slice(kv * PAIR, (kv + 1) * PAIR)
 
     def score(head):
-        return scores_of(q_scr[head], prefix_ref[:, columns_of(head)])
+        at = columns_of(head)
+        if head % QUERIES_PER_KEY == 0:
+            kvx_scr[:, at] = ones_for_keys(prefix_ref[:, at])
+        return scores_of(head_query(queries, head), prefix_ref[:, at])
 
     def soften(head, scores):
         row_max = jnp.max(scores, axis=1, keepdims=True)
@@ -343,11 +348,7 @@
 
 
 def merge_kernel(per_peer, *refs):
-    sources, att_ref, held, (att_scr, sems) = refs[:3], refs[3], refs[4:7], refs[7:]
-    copies, started = fetch(sources, held, sems)
-    target_ref, back_ref, past_ref = held
-    for copy in started:
-        copy.wait()
+    target_ref, back_ref, past_ref, att_ref = refs
     slot_column, _ = slot_places(target_ref[...], per_peer)
     gather = lane_ids((slot_column.shape[0], back_ref.shape[0])) == slot_column
     width = past_ref.shape[1] - PAIR
@@ -372,9 +373,18 @@
         key_half = lanes < HEAD_SIZE
         prefix_share = jnp.where(key_half, shares[2 * pair][0], shares[2 * pair + 1][0])
         past_share = jnp.where(key_half, shares[2 * pair][1], shares[2 * pair + 1][1])
-        att_scr[:, at] = (prefix_share * prefix[:, at] + past_share * past_ref[:, at]).astype(BF16)
-    copies.start(att_scr, att_ref)
-    copies.wait()
+        att_ref[:, at] = (prefix_share * prefix[:, at] + past_share * past_ref[:, at]).astype(BF16)
+
+
+def apart(hidden, w_down, split, copies):
+    for copy in copies[:-1]:
+        copy.wait()
+    total = None
+    if split:
+        total = jnp.dot(hidden[:, :split], w_down[:split], preferred_element_type=F32)
+    copies[-1].wait()
+    last = jnp.dot(hidden[:, split:], w_down[split:], preferred_element_type=F32)
+    return last if total is None else total + last
 
 
 def mlp_kernel(count, blocks, place_ref, *refs):
@@ -436,10 +446,8 @@
         gate_act = jnp.dot(normed, w_gate[:, at], preferred_element_type=F32)
         up_act = jnp.dot(normed, w_up[:, at], preferred_element_type=F32)
         hidden.append((gate_act / (1.0 + jnp.exp(-gate_act)) * up_act).astype(BF16))
-    for copy in downs:
-        copy.wait()
     hidden = jnp.concatenate(hidden, axis=1)
-    terms = jnp.dot(hidden, w_down[...], preferred_element_type=F32).astype(BF16)
+    terms = apart(hidden, w_down, chunks[-1].start, downs).astype(BF16)
     if count == 2:
         out_scr[0][...] = jnp.where(first, terms[:, :width], terms[:, width:])
         out_scr[1][...] = jnp.where(first, terms[:, width:], terms[:, :width])
@@ -484,9 +492,9 @@
 def tail_kernel(place_ref, *refs):
     w_gate, sources, pieces, w_up_hbm, w_down_hbm = refs[0], refs[1:7], refs[7:11], refs[11], refs[12]
     send_ref, hidden_ref, residual_ref = refs[13:16]
-    held, (w_out_other, w_up, w_down, send_scr, sems) = refs[16:22], refs[22:]
+    held, (w_out_other, w_up, w_down, sems) = refs[16:22], refs[22:]
     own_ref, other_ref, gain_ref, att_ref, att_other_ref, w_out_ref = held
-    width = send_scr.shape[1]
+    width = send_ref.shape[1]
     hidden_width = w_gate.shape[1]
     away = pl.ds(pl.multiple_of((1 - place_ref[0]) * width, width), width)
     copies, started = fetch(sources, held, sems)
@@ -516,15 +524,7 @@
         hidden.append((gate_act / (1.0 + jnp.exp(-gate_act)) * up_act).astype(BF16))
     hidden = jnp.concatenate(hidden, axis=1)
     hidden_ref[...] = hidden
-    split = chunks[-1].start
-    for copy in downs[:-1]:
-        copy.wait()
-    total = jnp.dot(hidden[:, :split], w_down[:split], preferred_element_type=F32)
-    downs[-1].wait()
-    total += jnp.dot(hidden[:, split:], w_down[split:], preferred_element_type=F32)
-    send_scr[...] = total.astype(BF16)
-    copies.start(send_scr, send_ref)
-    copies.wait()
+    send_ref[...] = apart(hidden, w_down, chunks[-1].start, downs).astype(BF16)
 
 
 def keep_kernel(place_ref, hidden_ref, residual_ref, w_down_hbm, out_ref, w_down, sems):
@@ -549,12 +549,11 @@
     send, units, residual = pl.pallas_call(
         tail_kernel,
         in_specs=[SCALAR, HELD] + [ANY] * (len(sources) + 6),
-        out_specs=[HBM, HELD, HELD],
+        out_specs=[HELD] * 3,
         out_shape=[half, units, half],
         scratch_shapes=scratch_like(*sources, w_outs[0], w_up)
         + [
             half_down,
-            pltpu.VMEM((rows, width), BF16),
             pltpu.SemaphoreType.DMA((12 + 2 * -(-hidden // CHUNK),)),
         ],
         compiler_params=params(TAIL_VMEM),
@@ -620,7 +619,7 @@
         scratch_shapes=held
         + scratch_like(*operands, *outs)
         + [pltpu.SemaphoreType.DMA((copies,))],
-        compiler_params=params(),
+        compiler_params=params(MLP_VMEM),
         cost_estimate=cost(FILL * 6 * rows * model * hidden, 6 * model * hidden, rows * hidden),
         name="mlp",
     )(place, *operands, *w_outs, *weights)
@@ -677,32 +676,28 @@
     w_outs, prompt_rows = share_rows(w_out, count, replicas, prompt_rows)
     prompt_parts = swap(prompt_rows, count)
     operands = (*request_parts, attn_gain, target)
-    held = load(REQUEST_VMEM, w_query, keyval_weight)
-    outs = [
-        jax.ShapeDtypeStruct((slots, width), BF16),
-        jax.ShapeDtypeStruct((requests, width + kv_width), BF16),
-    ]
-    send, projected = pl.pallas_call(
+    slot_rows = jax.ShapeDtypeStruct((slots, width), BF16)
+    send = pl.pallas_call(
         functools.partial(request_kernel, count, per_peer),
-        in_specs=[SCALAR, HELD, HELD] + [ANY] * len(operands),
-        out_specs=[HBM] * 2,
-        out_shape=outs,
-        scratch_shapes=scratch_like(*operands, *outs)
-        + [pltpu.SemaphoreType.DMA((len(operands) + 3,))],
+        in_specs=[SCALAR, HELD] + [ANY] * len(operands),
+        out_specs=HBM,
+        out_shape=slot_rows,
+        scratch_shapes=scratch_like(*operands, slot_rows)
+        + [pltpu.SemaphoreType.DMA((len(operands) + 1,))],
         compiler_params=params(REQUEST_VMEM),
         cost_estimate=cost(0, 0),
         name="request_project",
-    )(place, *held, *operands)
+    )(place, *load(REQUEST_VMEM, w_query), *operands)
 
     slot_queries = lax.all_to_all(send, "replica", split_axis=0, concat_axis=0, tiled=True)
 
     operands = (
         *prompt_parts,
+        *request_parts,
         attn_gain,
         w_query,
         keyval_weight,
         prefix_cache,
-        projected,
         cache_len.reshape(1, requests),
         request_keyval_cache,
     )
@@ -745,17 +740,15 @@
     passed = [pass_rows(w_outs[0], replicas)] if count == 2 else []
     slot_out = pl.pallas_call(
         slot_kernel,
-        in_specs=[ANY, HBM],
+        in_specs=[HELD] * 2,
         out_specs=HBM,
         out_shape=jax.ShapeDtypeStruct((slots, width + PAIR), BF16),
-        scratch_shapes=scratch_like(slot_queries, prefix_cache)
-        + [
+        scratch_shapes=[
             pltpu.VMEM((slots, width + PAIR), BF16),
-            pltpu.VMEM((heads, slots, PAIR), BF16),
             pltpu.VMEM((prefix_len, kv_width), BF16),
-            pltpu.SemaphoreType.DMA((3 + heads // 2,)),
+            pltpu.SemaphoreType.DMA((1 + heads // 2,)),
         ],
-        compiler_params=params(),
+        compiler_params=params(SLOT_VMEM),
         cost_estimate=cost(
             4 * slots * heads * prefix_len * PAIR,
             2 * prefix_len * kv_width,
@@ -775,11 +768,9 @@
     operands = (target, back, past)
     request_attended = pl.pallas_call(
         functools.partial(merge_kernel, per_peer),
-        in_specs=[ANY] * len(operands),
-        out_specs=HBM,
+        in_specs=[HELD] * len(operands),
+        out_specs=HELD,
         out_shape=jax.ShapeDtypeStruct((requests, width), BF16),
-        scratch_shapes=scratch_like(*operands)
-        + [pltpu.VMEM((requests, width), BF16), pltpu.SemaphoreType.DMA((4,))],
         compiler_params=params(MERGE_VMEM),
         cost_estimate=cost(4 * requests * slots * width, 4 * slots * width),
         name="merge",

time: 81.4 us -> 80.2 us (0.985)
  Pallas kernels: 38.4 us -> 37.1 us
  local copies, waits for them, and re-layouts: 10.8 us -> 9.58 us
  waiting for transfers between devices: 6.97 us -> 8.01 us
    pallas_call x2, Pallas kernels: 8.57 us -> 6.8 us  [the longest x1 6.15 us: body(): pl.pallas_call(slot_kernel, in_specs=[HELD] * 2, out_specs=HBM, out_shape...]
    ppermute x4, waiting for transfers between devices: 1.39 us -> 2.75 us  [swap(): return [block, lax.ppermute(block, 'tensor', [(0, 1), (1, 0)])]]
    unnamed x52 -> x58, local copies, waits for them, and re-layouts: 8.55 us -> 7.5 us
  transfers between devices with their start and end apart: 12 -> 12, of which waited for: 3 -> 4; matrix products, arithmetic and copies ran while one was open for 4% -> 4% of each run, Pallas kernels for 46% -> 46%
where the time goes in v5:
time: 80.2 us; the launch traced here: 79.8 us
  Pallas kernels  37.1 us (46%)
  starting transfers between devices  22.4 us (28%)
  local copies, waits for them, and re-layouts  9.58 us (12%)
  waiting for transfers between devices  8.01 us (10%)
  other arithmetic  1.68 us (2%)
  between operations  1.02 us (1%)
    pallas_call x1, Pallas kernels, body(): pl.pallas_call(functools.partial(prompt_kernel, count), in_specs=[SCALAR]...  10.4 us
    pallas_call x1, Pallas kernels, finish(): pl.pallas_call(functools.partial(mlp_kernel, count, len(w_outs)), in_spec...  9.89 us
    unnamed x58, local copies, waits for them, and re-layouts  7.5 us
    all_to_all x1, starting transfers between devices, body(): lax.all_to_all(send, 'replica', split_axis=0, concat_axis=0, tiled=True)  6.52 us
    pallas_call x1, Pallas kernels, body(): pl.pallas_call(slot_kernel, in_specs=[HELD] * 2, out_specs=HBM, out_shape...  6.15 us
    all_to_all x1, starting transfers between devices, body(): lax.all_to_all(slot_out, 'replica', split_axis=0, concat_axis=0, tiled=True)  6.01 us
    pallas_call x1, Pallas kernels, tail(): pl.pallas_call(tail_kernel, in_specs=[SCALAR, HELD] + [ANY] * (len(source...  5.9 us
    ppermute x4, starting transfers between devices, swap(): return [block, lax.ppermute(block, 'tensor', [(0, 1), (1, 0)])]  5.12 us
  transfers between devices with their start and end apart: 12, of which 4 were waited for; matrix products, arithmetic and copies ran while one was open for 4% of the time, Pallas kernels for 46%

profile of v5, /device:TPU:0, one launch (start us, length us, event | category | flops | bytes accessed | tf_op | source)
XLA Modules:
  0.0 79.8 jit_solution(18208549891990306792)
XLA Ops:
  0.7 3.0 %collective-permute-start = (bf16[128,1024]{1,0:T(8,128)(2,1)}, bf16[128,1024]{1,0:T(8,128)(2,1)S(1)}, u32[]{:S(2)}, u32[]{:S(2)}) collective-permute-start(bf16[128,1024]{1,0:T(8,128)(2,1)} %refs_1_.1), channel_id=1, source_target_pairs={{0,1},{1,0},{2,3},{3,2},{4,5},{5,4},{6,7},{7,6},{8,9},{9,8},{10,11... | collective-permute-start | bytes 786440 | tf_op jit(solution)/shard_map/ppermute | solution.py:579
  3.7 2.1 %constant_dynamic-slice_fusion.1 = (bf16[128,2048]{1,0:T(8,128)(2,1)S(1)}, bf16[128,2048]{1,0:T(8,128)(2,1)}) fusion(bf16[512,2048]{1,0:T(8,128)(2,1)} %refs_6_.3, s32[]{:T(128)S(6)} %add.23, s32[]{:T(128)S(6)} %select_n.13), kind=kLoop, calls=%fused_computation.4 | loop fusion | bytes 2097160 | tf_op jit(solution)/shard_map/slice | solution.py:592
  5.8 2.0 %collective-permute-start.2 = (bf16[128,2048]{1,0:T(8,128)(2,1)}, bf16[128,2048]{1,0:T(8,128)(2,1)S(1)}, u32[]{:S(2)}, u32[]{:S(2)}) collective-permute-start(bf16[128,2048]{1,0:T(8,128)(2,1)} %get-tuple-element.27), channel_id=1, source_target_pairs={{0,1},{1,0},{2,3},{3,2},{4,5},{5,4},{6,7},{7,6},{8,9},{9,8},{10,11... | collective-permute-start | bytes 1572872 | tf_op jit(solution)/shard_map/ppermute | solution.py:594
  7.8 1.6 %copy-done.2 = bf16[2048,512]{1,0:T(8,128)(2,1)S(1)} copy-done((bf16[2048,512]{1,0:T(8,128)(2,1)S(1)}, bf16[2048,512]{1,0:T(8,128)(2,1)}, u32[]{:S(2)}) %copy-start.2) | copy-done | bytes 2097176
  9.7 1.4 %collective-permute-done.refs_1_.refs_3_.refs_2_ = bf16[128,1024]{1,0:T(8,128)(2,1)S(1)} collective-permute-done((bf16[128,1024]{1,0:T(8,128)(2,1)}, bf16[128,1024]{1,0:T(8,128)(2,1)S(1)}, u32[]{:S(2)}, u32[]{:S(2)}) %collective-permute-start) | collective-permute-done | bytes 262176 | tf_op jit(solution)/shard_map/ppermute | solution.py:579
  11.0 2.2 %request_project.1 = bf16[256,512]{1,0:T(8,128)(2,1)} custom-call(s32[2]{0:T(128)S(1)} %pad_add_fusion.place_ref, bf16[2048,512]{1,0:T(8,128)(2,1)S(1)} %load.2.w_query_ref, bf16[128,1024]{1,0:T(8,128)(2,1)S(1)} %copy-done.3, bf16[128,1024]{1,0:T(8,128)(2,1)S(1)} %collective-permute-done.refs_1_.refs_3_.refs_2_, f32[1,2048]{1,0:T(1,128)S(1)} %bitcast.15, ...), custom_call_target="tpu_custom_call" | custom-call | tf_op jit(solution)/shard_map/request_project/pallas_call | solution.py:680
  13.2 6.5 %all-to-all-start = ((bf16[16,16,512]{2,1,0:T(8,128)(2,1)}), bf16[16,16,512]{2,1,0:T(8,128)(2,1)S(1)}, u32[]{:S(2)}, u32[]{:S(2)}) async-start(bf16[16,16,512]{2,1,0:T(8,128)(2,1)} %bitcast.4), calls=%async_computation | async-start | bytes 524288 | tf_op jit(solution)/shard_map/all_to_all | solution.py:692
  19.8 0.7 copy-done.24
  20.4 10.4 %prompt_attention.1 = (bf16[128,512]{1,0:T(8,128)(2,1)}, f32[128,640]{1,0:T(8,128)}) custom-call(s32[2]{0:T(128)} %copy-done.18, bf16[128,1024]{1,0:T(8,128)(2,1)} %refs_0_.5, bf16[128,1024]{1,0:T(8,128)(2,1)} %copy-done.24, bf16[128,1024]{1,0:T(8,128)(2,1)} %refs_1_.1, bf16[128,1024]{1,0:T(8,128)(2,1)} %copy-done.5, f32[1,2048]{1,0:T(1,128)} %bitcast.14, ...), custom_call_target="tpu_custom_call" | custom-call | flops 13958643712 | bytes 4194304 | tf_op jit(solution)/shard_map/prompt_attention/pallas_call | solution.py:709
  30.9 1.4 %copy-done.21 = bf16[2048,256]{1,0:T(8,128)(2,1)S(1)} copy-done((bf16[2048,256]{1,0:T(8,128)(2,1)S(1)}, bf16[2048,256]{1,0:T(8,128)(2,1)}, u32[]{:S(2)}) %copy-start.21) | copy-done | bytes 1048600
  32.3 6.1 %slot_attention.1 = bf16[256,640]{1,0:T(8,128)(2,1)} custom-call(bf16[256,512]{1,0:T(8,128)(2,1)S(1)} %bitcast.13, bf16[2048,256]{1,0:T(8,128)(2,1)S(1)} %copy-done.21), custom_call_target="tpu_custom_call" | custom-call | flops 2147483648 | bytes 1048576 | tf_op jit(solution)/shard_map/slot_attention/pallas_call | solution.py:741
  38.5 0.5 collective-permute-start.6
  39.1 1.5 %collective-permute-start.4 = (bf16[128,512]{1,0:T(8,128)(2,1)S(1)}, bf16[128,512]{1,0:T(8,128)(2,1)S(1)}, u32[]{:S(2)}, u32[]{:S(2)}) collective-permute-start(bf16[128,512]{1,0:T(8,128)(2,1)S(1)} %copy-done.25), channel_id=1, source_target_pairs={{0,1},{1,0},{2,3},{3,2},{4,5},{5,4},{6,7},{7,6},{8,9},{9,8},{10,11... | collective-permute-start | bytes 393224 | tf_op jit(solution)/shard_map/ppermute | solution.py:579
  40.6 6.0 %all-to-all-start.1 = ((bf16[16,16,640]{2,1,0:T(8,128)(2,1)}), bf16[16,16,640]{2,1,0:T(8,128)(2,1)S(1)}, u32[]{:S(2)}, u32[]{:S(2)}) async-start(bf16[16,16,640]{2,1,0:T(8,128)(2,1)} %bitcast.7), calls=%async_computation.1 | async-start | bytes 655360 | tf_op jit(solution)/shard_map/all_to_all | solution.py:763
  46.6 0.6 copy-done.26
  47.2 0.2 copy-done.11
  47.4 0.2 copy-done.13
  47.6 9.9 %mlp.1 = (bf16[128,1024]{1,0:T(8,128)(2,1)}, bf16[128,1024]{1,0:T(8,128)(2,1)}, bf16[128,1024]{1,0:T(8,128)(2,1)}) custom-call(s32[2]{0:T(128)} %copy-done.18, bf16[128,1024]{1,0:T(8,128)(2,1)} %refs_0_.5, bf16[128,1024]{1,0:T(8,128)(2,1)} %copy-done.24, bf16[128,512]{1,0:T(8,128)(2,1)} %get-tuple-element.32.refs_2_, bf16[128,512]{1,0:T(8,128)(2,1)} %copy-done.26, ...), custom_call_target="tpu_custom_call" | custom-call | flops 64424509440 | bytes 15728640 | tf_op jit(solution)/shard_map/mlp/pallas_call | solution.py:614
  57.5 0.2 all-to-all-done.1
  57.7 0.7 merge.1.refs_4_
  58.4 0.6 collective-permute-start.8
  58.9 1.5 %collective-permute-start.7 = (bf16[128,1024]{1,0:T(8,128)(2,1)}, bf16[128,1024]{1,0:T(8,128)(2,1)S(1)}, u32[]{:S(2)}, u32[]{:S(2)}) collective-permute-start(bf16[128,1024]{1,0:T(8,128)(2,1)} %get-tuple-element.40), channel_id=1, source_target_pairs={{0,1},{1,0},{2,3},{3,2},{4,5},{5,4},{6,7},{7,6},{8,9},{9,8},{10,11... | collective-permute-start | bytes 786440 | tf_op jit(solution)/shard_map/ppermute | solution.py:631
  60.4 2.5 %copy-done = bf16[2048,1280]{1,0:T(8,128)(2,1)S(1)} copy-done((bf16[2048,1280]{1,0:T(8,128)(2,1)S(1)}, bf16[2048,1280]{1,0:T(8,128)(2,1)}, u32[]{:S(2)}) %copy-start) | copy-done | bytes 5242904
  63.0 0.4 load.3.refs_0_
  63.3 1.4 %collective-permute-done.8.refs_5_ = bf16[128,512]{1,0:T(8,128)(2,1)S(1)} collective-permute-done((bf16[128,512]{1,0:T(8,128)(2,1)S(1)}, bf16[128,512]{1,0:T(8,128)(2,1)S(1)}, u32[]{:S(2)}, u32[]{:S(2)}) %collective-permute-start.8) | collective-permute-done | bytes 131104 | tf_op jit(solution)/shard_map/ppermute | solution.py:579
  64.9 0.2 copy-done.14
  65.1 5.9 %tail.1 = (bf16[128,1024]{1,0:T(8,128)(2,1)S(1)}, bf16[128,1280]{1,0:T(8,128)(2,1)S(1)}, bf16[128,1024]{1,0:T(8,128)(2,1)S(1)}) custom-call(s32[2]{0:T(128)S(1)} %copy-done.19, bf16[2048,1280]{1,0:T(8,128)(2,1)S(1)} %load.3.refs_0_, bf16[128,1024]{1,0:T(8,128)(2,1)S(1)} %copy-done.4, bf16[128,1024]{1,0:T(8,128)(2,1)S(1)} %copy-done.6, ...), custom_call_target="tpu_custom_call" | custom-call | flops 1677721600 | bytes 7864320 | tf_op jit(solution)/shard_map/tail/pallas_call | solution.py:549
  71.0 0.6 collective-permute-start.9
  71.6 1.4 %keep.1 = f32[128,1024]{1,0:T(8,128)S(1)} custom-call(s32[2]{0:T(128)S(1)} %copy-done.19, bf16[128,1280]{1,0:T(8,128)(2,1)S(1)} %get-tuple-element.45.hidden_ref, bf16[128,1024]{1,0:T(8,128)(2,1)S(1)} %get-tuple-element.46.residual_ref, bf16[1280,2048]{1,0:T(8,128)(2,1)S(1)} %bitcast.11), custom_call_target="tpu_custom_call" | custom-call | flops 335544320 | bytes 2621440 | tf_op jit(solution)/shard_map/keep/pallas_call | solution.py:563
  73.1 0.8 %add_convert_fusion.1 = bf16[128,1024]{1,0:T(8,128)(2,1)} fusion(bf16[128,1024]{1,0:T(8,128)(2,1)S(1)} %collective-permute-done.7, bf16[128,1024]{1,0:T(8,128)(2,1)S(1)} %copy-done.22, bf16[128,1024]{1,0:T(8,128)(2,1)S(1)} %copy-done.23), kind=kLoop, calls=%fused_computation.1 | loop fusion | flops 786432 | bytes 1048576 | tf_op jit(solution)/shard_map/convert_element_type | solution.py:633
  73.9 5.1 %collective-permute-done.9 = bf16[128,1024]{1,0:T(8,128)(2,1)S(1)} collective-permute-done((bf16[128,1024]{1,0:T(8,128)(2,1)S(1)}, bf16[128,1024]{1,0:T(8,128)(2,1)S(1)}, u32[]{:S(2)}, u32[]{:S(2)}) %collective-permute-start.9) | collective-permute-done | bytes 262176 | tf_op jit(solution)/shard_map/ppermute | solution.py:573
  79.0 0.8 add_convert_fusion
  (64 shorter events, 0.7 us)
Async XLA Ops:
  0.6 10.4 %copy-start.3 = (bf16[128,1024]{1,0:T(8,128)(2,1)S(1)}, bf16[128,1024]{1,0:T(8,128)(2,1)}, u32[]{:S(2)}) copy-start(bf16[128,1024]{1,0:T(8,128)(2,1)} %refs_1_.1) | copy-start | bytes 786436
  0.6 10.4 %copy-start.16 = (f32[2048]{0:T(1024)S(1)}, f32[2048]{0:T(1024)}, u32[]{:S(2)}) copy-start(f32[2048]{0:T(1024)} %param.20) | copy-start | bytes 24580
  0.7 10.4 %copy-start.20 = (s32[128,1]{0,1:T(1,128)S(1)}, s32[128,1]{0,1:T(1,128)}, u32[]{:S(2)}) copy-start(s32[128,1]{0,1:T(1,128)} %param.18) | copy-start | bytes 1540
  0.7 10.3 %collective-permute-start = (bf16[128,1024]{1,0:T(8,128)(2,1)}, bf16[128,1024]{1,0:T(8,128)(2,1)S(1)}, u32[]{:S(2)}, u32[]{:S(2)}) collective-permute-start(bf16[128,1024]{1,0:T(8,128)(2,1)} %refs_1_.1), channel_id=1, source_target_pairs={{0,1},{1,0},{2,3},{3,2},{4,5},{5,4},{6,7},{7,6},{8,9},{9,8},{10,11... | collective-permute-start | bytes 786440 | tf_op jit(solution)/shard_map/ppermute | solution.py:579
  5.8 14.0 %collective-permute-start.1 = (bf16[128,1024]{1,0:T(8,128)(2,1)}, bf16[128,1024]{1,0:T(8,128)(2,1)S(1)}, u32[]{:S(2)}, u32[]{:S(2)}) collective-permute-start(bf16[128,1024]{1,0:T(8,128)(2,1)} %refs_0_.5), channel_id=1, source_target_pairs={{0,1},{1,0},{2,3},{3,2},{4,5},{5,4},{6,7},{7,6},{8,9},{9,8},{10,11... | collective-permute-start | bytes 786440 | tf_op jit(solution)/shard_map/ppermute | solution.py:579
  5.8 25.1 %collective-permute-start.2 = (bf16[128,2048]{1,0:T(8,128)(2,1)}, bf16[128,2048]{1,0:T(8,128)(2,1)S(1)}, u32[]{:S(2)}, u32[]{:S(2)}) collective-permute-start(bf16[128,2048]{1,0:T(8,128)(2,1)} %get-tuple-element.27), channel_id=1, source_target_pairs={{0,1},{1,0},{2,3},{3,2},{4,5},{5,4},{6,7},{7,6},{8,9},{9,8},{10,11... | collective-permute-start | bytes 1572872 | tf_op jit(solution)/shard_map/ppermute | solution.py:594
  7.8 30.7 %collective-permute-start.3 = (bf16[128,2048]{1,0:T(8,128)(2,1)S(1)}, bf16[128,2048]{1,0:T(8,128)(2,1)S(1)}, u32[]{:S(2)}, u32[]{:S(2)}) collective-permute-start(bf16[128,2048]{1,0:T(8,128)(2,1)S(1)} %get-tuple-element.30), channel_id=1, source_target_pairs={{0,1},{1,0},{2,3},{3,2},{4,5},{5,4},{6,7},{7,6},{8,9},{9,8},{10,11... | collective-permute-start | bytes 1572872 | tf_op jit(solution)/shard_map/ppermute | solution.py:594
  9.7 10.1 %copy-start.18 = (s32[2]{0:T(128)}, s32[2]{0:T(128)S(1)}, u32[]{:S(2)}) copy-start(s32[2]{0:T(128)S(1)} %pad_add_fusion.place_ref) | copy-start | bytes 28
  11.0 8.7 %copy-start.5 = (bf16[128,1024]{1,0:T(8,128)(2,1)}, bf16[128,1024]{1,0:T(8,128)(2,1)S(1)}, u32[]{:S(2)}) copy-start(bf16[128,1024]{1,0:T(8,128)(2,1)S(1)} %collective-permute-done.refs_1_.refs_3_.refs_2_) | copy-start | bytes 786436
  13.2 17.7 %all-to-all-start = ((bf16[16,16,512]{2,1,0:T(8,128)(2,1)}), bf16[16,16,512]{2,1,0:T(8,128)(2,1)S(1)}, u32[]{:S(2)}, u32[]{:S(2)}) async-start(bf16[16,16,512]{2,1,0:T(8,128)(2,1)} %bitcast.4), calls=%async_computation | async-start | bytes 524288 | tf_op jit(solution)/shard_map/all_to_all | solution.py:692
  30.9 9.7 %copy-start.7 = (bf16[128,2048]{1,0:T(8,128)(2,1)}, bf16[128,2048]{1,0:T(8,128)(2,1)S(1)}, u32[]{:S(2)}) copy-start(bf16[128,2048]{1,0:T(8,128)(2,1)S(1)} %collective-permute-done.2.refs_6_.refs_7_) | copy-start | bytes 1572868
  32.3 6.8 %copy-start.25 = (bf16[128,512]{1,0:T(8,128)(2,1)S(1)}, bf16[128,512]{1,0:T(8,128)(2,1)}, u32[]{:S(2)}) copy-start(bf16[128,512]{1,0:T(8,128)(2,1)} %get-tuple-element.32.refs_2_) | copy-start | bytes 393220
  38.5 8.2 %copy-start.9 = (bf16[128,2048]{1,0:T(8,128)(2,1)}, bf16[128,2048]{1,0:T(8,128)(2,1)S(1)}, u32[]{:S(2)}) copy-start(bf16[128,2048]{1,0:T(8,128)(2,1)S(1)} %collective-permute-done.3.refs_7_.refs_8_) | copy-start | bytes 1572868
  38.5 8.1 %collective-permute-start.6 = (bf16[128,2048]{1,0:T(8,128)(2,1)S(1)}, bf16[128,2048]{1,0:T(8,128)(2,1)S(1)}, u32[]{:S(2)}, u32[]{:S(2)}) collective-permute-start(bf16[128,2048]{1,0:T(8,128)(2,1)S(1)} %collective-permute-done.3.refs_7_.refs_8_), channel_id=1, source_target_pairs={{0,2},{2,0},{4,6},{6,4},{8,10},{10,8},{12,14},{14,12},{16,18},{18,... | collective-permute-start | bytes 1572872 | tf_op jit(solution)/shard_map/ppermute | solution.py:598
  38.9 7.7 %collective-permute-start.5 = (bf16[128,2048]{1,0:T(8,128)(2,1)S(1)}, bf16[128,2048]{1,0:T(8,128)(2,1)S(1)}, u32[]{:S(2)}, u32[]{:S(2)}) collective-permute-start(bf16[128,2048]{1,0:T(8,128)(2,1)S(1)} %collective-permute-done.2.refs_6_.refs_7_), channel_id=1, source_target_pairs={{0,2},{2,0},{4,6},{6,4},{8,10},{10,8},{12,14},{14,12},{16,18},{18,... | collective-permute-start | bytes 1572872 | tf_op jit(solution)/shard_map/ppermute | solution.py:598
  39.1 7.5 %collective-permute-start.4 = (bf16[128,512]{1,0:T(8,128)(2,1)S(1)}, bf16[128,512]{1,0:T(8,128)(2,1)S(1)}, u32[]{:S(2)}, u32[]{:S(2)}) collective-permute-start(bf16[128,512]{1,0:T(8,128)(2,1)S(1)} %copy-done.25), channel_id=1, source_target_pairs={{0,1},{1,0},{2,3},{3,2},{4,5},{5,4},{6,7},{7,6},{8,9},{9,8},{10,11... | collective-permute-start | bytes 393224 | tf_op jit(solution)/shard_map/ppermute | solution.py:579
  40.6 17.1 %all-to-all-start.1 = ((bf16[16,16,640]{2,1,0:T(8,128)(2,1)}), bf16[16,16,640]{2,1,0:T(8,128)(2,1)S(1)}, u32[]{:S(2)}, u32[]{:S(2)}) async-start(bf16[16,16,640]{2,1,0:T(8,128)(2,1)} %bitcast.7), calls=%async_computation.1 | async-start | bytes 655360 | tf_op jit(solution)/shard_map/all_to_all | solution.py:763
  47.6 10.1 %copy-start.15 = (f32[128,640]{1,0:T(8,128)S(1)}, f32[128,640]{1,0:T(8,128)}, u32[]{:S(2)}) copy-start(f32[128,640]{1,0:T(8,128)} %get-tuple-element.42.refs_2_) | copy-start | bytes 983044
  57.7 7.1 %copy-start.4 = (bf16[128,1024]{1,0:T(8,128)(2,1)S(1)}, bf16[128,1024]{1,0:T(8,128)(2,1)}, u32[]{:S(2)}) copy-start(bf16[128,1024]{1,0:T(8,128)(2,1)} %refs_1_.1) | copy-start | bytes 786436
  57.7 7.1 %copy-start.6 = (bf16[128,1024]{1,0:T(8,128)(2,1)S(1)}, bf16[128,1024]{1,0:T(8,128)(2,1)}, u32[]{:S(2)}) copy-start(bf16[128,1024]{1,0:T(8,128)(2,1)} %copy-done.5) | copy-start | bytes 786436
  57.7 7.1 %copy-start.17 = (f32[2048]{0:T(1024)S(1)}, f32[2048]{0:T(1024)}, u32[]{:S(2)}) copy-start(f32[2048]{0:T(1024)} %param.24) | copy-start | bytes 24580
  57.7 7.1 %copy-start.19 = (s32[2]{0:T(128)S(1)}, s32[2]{0:T(128)}, u32[]{:S(2)}) copy-start(s32[2]{0:T(128)} %copy-done.18) | copy-start | bytes 28
  58.4 6.4 %collective-permute-start.8 = (bf16[128,512]{1,0:T(8,128)(2,1)S(1)}, bf16[128,512]{1,0:T(8,128)(2,1)S(1)}, u32[]{:S(2)}, u32[]{:S(2)}) collective-permute-start(bf16[128,512]{1,0:T(8,128)(2,1)S(1)} %merge.1.refs_4_), channel_id=1, source_target_pairs={{0,1},{1,0},{2,3},{3,2},{4,5},{5,4},{6,7},{7,6},{8,9},{9,8},{10,11... | collective-permute-start | bytes 393224 | tf_op jit(solution)/shard_map/ppermute | solution.py:579
  58.9 14.1 %collective-permute-start.7 = (bf16[128,1024]{1,0:T(8,128)(2,1)}, bf16[128,1024]{1,0:T(8,128)(2,1)S(1)}, u32[]{:S(2)}, u32[]{:S(2)}) collective-permute-start(bf16[128,1024]{1,0:T(8,128)(2,1)} %get-tuple-element.40), channel_id=1, source_target_pairs={{0,1},{1,0},{2,3},{3,2},{4,5},{5,4},{6,7},{7,6},{8,9},{9,8},{10,11... | collective-permute-start | bytes 786440 | tf_op jit(solution)/shard_map/ppermute | solution.py:631
  60.4 2.5 %copy-start = (bf16[2048,1280]{1,0:T(8,128)(2,1)S(1)}, bf16[2048,1280]{1,0:T(8,128)(2,1)}, u32[]{:S(2)}) copy-start(bf16[2048,1280]{1,0:T(8,128)(2,1)} %refs_0_.6) | copy-start | bytes 15728644
  62.9 2.0 %copy-start.12 = (bf16[128,2048]{1,0:T(8,128)(2,1)S(1)}, bf16[128,2048]{1,0:T(8,128)(2,1)}, u32[]{:S(2)}) copy-start(bf16[128,2048]{1,0:T(8,128)(2,1)} %copy-done.11) | copy-start | bytes 1572868
  62.9 2.1 %copy-start.14 = (bf16[128,2048]{1,0:T(8,128)(2,1)S(1)}, bf16[128,2048]{1,0:T(8,128)(2,1)}, u32[]{:S(2)}) copy-start(bf16[128,2048]{1,0:T(8,128)(2,1)} %copy-done.13) | copy-start | bytes 1572868
  63.0 8.7 %slice-start = ((s8[5242880]{0:T(1024)(128)(4,1)}), s8[4194304]{0:T(1024)(128)(4,1)S(1)}, s32[]{:S(2)}) async-start(s8[5242880]{0:T(1024)(128)(4,1)} %bitcast.10), calls=%async_computation.2 | async-start | bytes 8388608
  63.3 8.3 %slice-start.1 = ((s8[5242880]{0:T(1024)(128)(4,1)}), s8[1048576]{0:T(1024)(128)(4,1)S(1)}, s32[]{:S(2)}) async-start(s8[5242880]{0:T(1024)(128)(4,1)} %bitcast.10), calls=%async_computation.3 | async-start | bytes 2097152
  71.0 2.1 %copy-start.22 = (bf16[128,1024]{1,0:T(8,128)(2,1)S(1)}, bf16[128,1024]{1,0:T(8,128)(2,1)}, u32[]{:S(2)}) copy-start(bf16[128,1024]{1,0:T(8,128)(2,1)} %get-tuple-element.39) | copy-start | bytes 786436
  71.0 2.1 %copy-start.23 = (bf16[128,1024]{1,0:T(8,128)(2,1)S(1)}, bf16[128,1024]{1,0:T(8,128)(2,1)}, u32[]{:S(2)}) copy-start(bf16[128,1024]{1,0:T(8,128)(2,1)} %get-tuple-element.38) | copy-start | bytes 786436
  71.0 8.0 %collective-permute-start.9 = (bf16[128,1024]{1,0:T(8,128)(2,1)S(1)}, bf16[128,1024]{1,0:T(8,128)(2,1)S(1)}, u32[]{:S(2)}, u32[]{:S(2)}) collective-permute-start(bf16[128,1024]{1,0:T(8,128)(2,1)S(1)} %get-tuple-element.47), channel_id=1, source_target_pairs={{0,1},{1,0},{2,3},{3,2},{4,5},{5,4},{6,7},{7,6},{8,9},{9,8},{10,11... | collective-permute-start | bytes 786440 | tf_op jit(solution)/shard_map/ppermute | solution.py:573
  (9 other events, 11.7 us)

commit v6 on v5

--- a/solution.py
+++ b/solution.py
@@ -21,6 +21,7 @@
 MIB = 1024 * 1024
 MOST_VMEM = 61 * MIB
 MLP_VMEM = 60 * MIB
+PROMPT_VMEM = 62 * MIB
 REQUEST_VMEM = 40 * MIB
 SLOT_VMEM = 48 * MIB
 TAIL_VMEM = 40 * MIB
@@ -489,11 +490,18 @@
     ]
 
 
+def own_share_kernel(att_ref, w_out_ref, term_ref):
+    term_ref[...] = jnp.dot(
+        att_ref[...], w_out_ref[...], preferred_element_type=F32
+    ).astype(BF16)
+
+
 def tail_kernel(place_ref, *refs):
-    w_gate, sources, pieces, w_up_hbm, w_down_hbm = refs[0], refs[1:7], refs[7:11], refs[11], refs[12]
-    send_ref, hidden_ref, residual_ref = refs[13:16]
-    held, (w_out_other, w_up, w_down, sems) = refs[16:22], refs[22:]
-    own_ref, other_ref, gain_ref, att_ref, att_other_ref, w_out_ref = held
+    w_gate, term_ref, *refs = refs
+    sources, pieces, w_up_hbm, w_down_hbm = refs[:4], refs[4:8], refs[8], refs[9]
+    send_ref, hidden_ref, residual_ref, *refs = refs[10:]
+    held, (w_out_other, w_up, w_down, sems) = refs[:4], refs[4:]
+    own_ref, other_ref, gain_ref, att_other_ref = held
     width = send_ref.shape[1]
     hidden_width = w_gate.shape[1]
     away = pl.ds(pl.multiple_of((1 - place_ref[0]) * width, width), width)
@@ -504,15 +512,11 @@
     ]
     ups = [copies.start(w_up_hbm.at[:, at], w_up.at[:, at]) for at in chunks]
     downs = [copies.start(w_down_hbm.at[at, away], w_down.at[at]) for at in chunks]
-    copies.flying = []
-    for copy in started:
-        copy.wait()
-    rows = in_order(place_ref, [own_ref[...], other_ref[...]]).astype(F32)
-    mixed = jnp.dot(att_ref[...], w_out_ref[...], preferred_element_type=F32)
-    for copy in arriving:
+    for copy in started + arriving:
         copy.wait()
     mixed_other = jnp.dot(att_other_ref[...], w_out_other[...], preferred_element_type=F32)
-    mixed = mixed.astype(BF16).astype(F32) + mixed_other.astype(BF16).astype(F32)
+    rows = in_order(place_ref, [own_ref[...], other_ref[...]]).astype(F32)
+    mixed = term_ref[...].astype(F32) + mixed_other.astype(BF16).astype(F32)
     residual = (rows + mixed).astype(BF16)
     normed = rms_norm(residual.astype(F32), gain_ref[...])
     residual_ref[...] = jnp.where(place_ref[0] == 0, residual[:, :width], residual[:, width:])
@@ -542,19 +546,29 @@
     rows, width = parts[0].shape
     hidden = w_up.shape[1]
     held = load(TAIL_VMEM, w_gate)
-    sources = (*parts, gain, *swap(attended, 2), w_outs[0])
+    term = pl.pallas_call(
+        own_share_kernel,
+        in_specs=[HELD] * 2,
+        out_specs=HELD,
+        out_shape=jax.ShapeDtypeStruct((rows, 2 * width), BF16),
+        compiler_params=params(TAIL_VMEM),
+        cost_estimate=cost(4 * rows * width * attended.shape[1], 2 * w_outs[0].size),
+        name="own_share",
+    )(attended, w_outs[0])
+    held = (*held, term)
+    sources = (*parts, gain, swap(attended, 2)[1])
     half = jax.ShapeDtypeStruct((rows, width), BF16)
     units = jax.ShapeDtypeStruct((rows, hidden), BF16)
     half_down = pltpu.VMEM((hidden, width), BF16)
     send, units, residual = pl.pallas_call(
         tail_kernel,
-        in_specs=[SCALAR, HELD] + [ANY] * (len(sources) + 6),
+        in_specs=[SCALAR, HELD, HELD] + [ANY] * (len(sources) + 6),
         out_specs=[HELD] * 3,
         out_shape=[half, units, half],
         scratch_shapes=scratch_like(*sources, w_outs[0], w_up)
         + [
             half_down,
-            pltpu.SemaphoreType.DMA((12 + 2 * -(-hidden // CHUNK),)),
+            pltpu.SemaphoreType.DMA((8 + 2 * -(-hidden // CHUNK),)),
         ],
         compiler_params=params(TAIL_VMEM),
         cost_estimate=cost(10 * rows * width * hidden, 6 * width * hidden, rows * hidden),
@@ -724,7 +738,7 @@
             pltpu.VMEM((*blocks, kv_width), F32),
             pltpu.SemaphoreType.DMA((len(operands) + 2,)),
         ],
-        compiler_params=params(),
+        compiler_params=params(PROMPT_VMEM),
         cost_estimate=cost(
             FILL * (2 * prompts * model * (width + kv_width)) + 4 * prompts * heads * prefix_len * PAIR,
             2 * model * (width + kv_width) + 2 * prefix_len * kv_width,

time: 80.2 us -> 79.6 us (level)
  waiting for transfers between devices: 8.01 us -> 6.42 us
  local copies, waits for them, and re-layouts: 9.58 us -> 10.8 us
    ppermute x4, waiting for transfers between devices: 2.75 us -> 1.15 us  [swap(): return [block, lax.ppermute(block, 'tensor', [(0, 1), (1, 0)])]]
    unnamed x58, local copies, waits for them, and re-layouts: 7.5 us -> 8.5 us
    pallas_call x1 -> x2, Pallas kernels: 5.9 us -> 5.66 us  [the longest x1 5.22 us: tail(): pl.pallas_call(tail_kernel, in_specs=[SCALAR, HELD, HELD] + [ANY] * (len(...]
  transfers between devices with their start and end apart: 12 -> 12, of which waited for: 4 -> 3; matrix products, arithmetic and copies ran while one was open for 4% -> 4% of each run, Pallas kernels for 46% -> 46%
where the time goes in v6:
time: 79.6 us; the launch traced here: 79.1 us
  Pallas kernels  36.9 us (46%)
  starting transfers between devices  22.4 us (28%)
  local copies, waits for them, and re-layouts  10.8 us (14%)
  waiting for transfers between devices  6.42 us (8%)
  other arithmetic  1.67 us (2%)
  between operations  1.04 us (1%)
    pallas_call x1, Pallas kernels, body(): pl.pallas_call(functools.partial(prompt_kernel, count), in_specs=[SCALAR]...  10.4 us
    pallas_call x1, Pallas kernels, finish(): pl.pallas_call(functools.partial(mlp_kernel, count, len(w_outs)), in_spec...  9.89 us
    unnamed x58, local copies, waits for them, and re-layouts  8.5 us
    all_to_all x1, starting transfers between devices, body(): lax.all_to_all(send, 'replica', split_axis=0, concat_axis=0, tiled=True)  6.52 us
    pallas_call x1, Pallas kernels, body(): pl.pallas_call(slot_kernel, in_specs=[HELD] * 2, out_specs=HBM, out_shape...  6.15 us
    all_to_all x1, starting transfers between devices, body(): lax.all_to_all(slot_out, 'replica', split_axis=0, concat_axis=0, tiled=True)  6.01 us
    pallas_call x1, Pallas kernels, tail(): pl.pallas_call(tail_kernel, in_specs=[SCALAR, HELD, HELD] + [ANY] * (len(...  5.22 us
    ppermute x4, starting transfers between devices, swap(): return [block, lax.ppermute(block, 'tensor', [(0, 1), (1, 0)])]  5.13 us
  transfers between devices with their start and end apart: 12, of which 3 were waited for; matrix products, arithmetic and copies ran while one was open for 4% of the time, Pallas kernels for 46%

profile of v6, /device:TPU:0, one launch (start us, length us, event | category | flops | bytes accessed | tf_op | source)
XLA Modules:
  0.0 79.1 jit_solution(7363530658707244583)
XLA Ops:
  0.7 3.0 %collective-permute-start = (bf16[128,1024]{1,0:T(8,128)(2,1)}, bf16[128,1024]{1,0:T(8,128)(2,1)S(1)}, u32[]{:S(2)}, u32[]{:S(2)}) collective-permute-start(bf16[128,1024]{1,0:T(8,128)(2,1)} %refs_2_.3), channel_id=1, source_target_pairs={{0,1},{1,0},{2,3},{3,2},{4,5},{5,4},{6,7},{7,6},{8,9},{9,8},{10,11... | collective-permute-start | bytes 786440 | tf_op jit(solution)/shard_map/ppermute | solution.py:593
  3.7 2.3 %constant_dynamic-slice_fusion.1 = (bf16[128,2048]{1,0:T(8,128)(2,1)}, bf16[128,2048]{1,0:T(8,128)(2,1)}) fusion(bf16[512,2048]{1,0:T(8,128)(2,1)} %w_out_ref.1, s32[]{:T(128)S(6)} %add.23, s32[]{:T(128)S(6)} %select_n.13), kind=kLoop, calls=%fused_computation.4 | loop fusion | bytes 2097160 | tf_op jit(solution)/shard_map/slice | solution.py:606
  6.0 2.0 %collective-permute-start.2 = (bf16[128,2048]{1,0:T(8,128)(2,1)}, bf16[128,2048]{1,0:T(8,128)(2,1)S(1)}, u32[]{:S(2)}, u32[]{:S(2)}) collective-permute-start(bf16[128,2048]{1,0:T(8,128)(2,1)} %get-tuple-element.27), channel_id=1, source_target_pairs={{0,1},{1,0},{2,3},{3,2},{4,5},{5,4},{6,7},{7,6},{8,9},{9,8},{10,11... | collective-permute-start | bytes 1572872 | tf_op jit(solution)/shard_map/ppermute | solution.py:608
  8.0 1.6 %copy-done.2 = bf16[2048,512]{1,0:T(8,128)(2,1)S(1)} copy-done((bf16[2048,512]{1,0:T(8,128)(2,1)S(1)}, bf16[2048,512]{1,0:T(8,128)(2,1)}, u32[]{:S(2)}) %copy-start.2) | copy-done | bytes 2097176
  9.9 1.1 %collective-permute-done.refs_1_.refs_3_ = bf16[128,1024]{1,0:T(8,128)(2,1)S(1)} collective-permute-done((bf16[128,1024]{1,0:T(8,128)(2,1)}, bf16[128,1024]{1,0:T(8,128)(2,1)S(1)}, u32[]{:S(2)}, u32[]{:S(2)}) %collective-permute-start) | collective-permute-done | bytes 262176 | tf_op jit(solution)/shard_map/ppermute | solution.py:593
  11.0 2.1 %request_project.1 = bf16[256,512]{1,0:T(8,128)(2,1)} custom-call(s32[2]{0:T(128)S(1)} %pad_add_fusion.place_ref, bf16[2048,512]{1,0:T(8,128)(2,1)S(1)} %load.2.w_query_ref, bf16[128,1024]{1,0:T(8,128)(2,1)S(1)} %copy-done.3, bf16[128,1024]{1,0:T(8,128)(2,1)S(1)} %collective-permute-done.refs_1_.refs_3_, f32[1,2048]{1,0:T(1,128)S(1)} %bitcast.17, ...), custom_call_target="tpu_custom_call" | custom-call | tf_op jit(solution)/shard_map/request_project/pallas_call | solution.py:694
  13.2 6.5 %all-to-all-start = ((bf16[16,16,512]{2,1,0:T(8,128)(2,1)}), bf16[16,16,512]{2,1,0:T(8,128)(2,1)S(1)}, u32[]{:S(2)}, u32[]{:S(2)}) async-start(bf16[16,16,512]{2,1,0:T(8,128)(2,1)} %bitcast.4), calls=%async_computation | async-start | bytes 524288 | tf_op jit(solution)/shard_map/all_to_all | solution.py:706
  19.7 0.7 copy-done.24
  20.4 10.4 %prompt_attention.1 = (bf16[128,512]{1,0:T(8,128)(2,1)}, f32[128,640]{1,0:T(8,128)}) custom-call(s32[2]{0:T(128)} %copy-done.18, bf16[128,1024]{1,0:T(8,128)(2,1)} %refs_0_.5, bf16[128,1024]{1,0:T(8,128)(2,1)} %copy-done.24, bf16[128,1024]{1,0:T(8,128)(2,1)} %refs_2_.3, bf16[128,1024]{1,0:T(8,128)(2,1)} %copy-done.5, f32[1,2048]{1,0:T(1,128)} %bitcast.16, ...), custom_call_target="tpu_custom_call" | custom-call | flops 13958643712 | bytes 4194304 | tf_op jit(solution)/shard_map/prompt_attention/pallas_call | solution.py:723
  30.9 1.4 %copy-done.21 = bf16[2048,256]{1,0:T(8,128)(2,1)S(1)} copy-done((bf16[2048,256]{1,0:T(8,128)(2,1)S(1)}, bf16[2048,256]{1,0:T(8,128)(2,1)}, u32[]{:S(2)}) %copy-start.21) | copy-done | bytes 1048600
  32.3 6.1 %slot_attention.1 = bf16[256,640]{1,0:T(8,128)(2,1)} custom-call(bf16[256,512]{1,0:T(8,128)(2,1)S(1)} %bitcast.13, bf16[2048,256]{1,0:T(8,128)(2,1)S(1)} %copy-done.21), custom_call_target="tpu_custom_call" | custom-call | flops 2147483648 | bytes 1048576 | tf_op jit(solution)/shard_map/slot_attention/pallas_call | solution.py:755
  38.5 0.5 collective-permute-start.6
  39.0 1.5 %collective-permute-start.4 = (bf16[128,512]{1,0:T(8,128)(2,1)S(1)}, bf16[128,512]{1,0:T(8,128)(2,1)S(1)}, u32[]{:S(2)}, u32[]{:S(2)}) collective-permute-start(bf16[128,512]{1,0:T(8,128)(2,1)S(1)} %copy-done.25), channel_id=1, source_target_pairs={{0,1},{1,0},{2,3},{3,2},{4,5},{5,4},{6,7},{7,6},{8,9},{9,8},{10,11... | collective-permute-start | bytes 393224 | tf_op jit(solution)/shard_map/ppermute | solution.py:593
  40.5 6.0 %all-to-all-start.1 = ((bf16[16,16,640]{2,1,0:T(8,128)(2,1)}), bf16[16,16,640]{2,1,0:T(8,128)(2,1)S(1)}, u32[]{:S(2)}, u32[]{:S(2)}) async-start(bf16[16,16,640]{2,1,0:T(8,128)(2,1)} %bitcast.7), calls=%async_computation.1 | async-start | bytes 655360 | tf_op jit(solution)/shard_map/all_to_all | solution.py:777
  46.6 0.6 copy-done.26
  47.2 0.2 copy-done.11
  47.4 0.2 copy-done.13
  47.6 9.9 %mlp.1 = (bf16[128,1024]{1,0:T(8,128)(2,1)}, bf16[128,1024]{1,0:T(8,128)(2,1)}, bf16[128,1024]{1,0:T(8,128)(2,1)}) custom-call(s32[2]{0:T(128)} %copy-done.18, bf16[128,1024]{1,0:T(8,128)(2,1)} %refs_0_.5, bf16[128,1024]{1,0:T(8,128)(2,1)} %copy-done.24, bf16[128,512]{1,0:T(8,128)(2,1)} %get-tuple-element.32.refs_2_, bf16[128,512]{1,0:T(8,128)(2,1)} %copy-done.26, ...), custom_call_target="tpu_custom_call" | custom-call | flops 64424509440 | bytes 15728640 | tf_op jit(solution)/shard_map/mlp/pallas_call | solution.py:628
  57.5 0.2 all-to-all-done.1
  57.7 0.7 merge.1.att_ref
  58.3 0.6 collective-permute-start.8
  58.9 1.5 %collective-permute-start.7 = (bf16[128,1024]{1,0:T(8,128)(2,1)}, bf16[128,1024]{1,0:T(8,128)(2,1)S(1)}, u32[]{:S(2)}, u32[]{:S(2)}) collective-permute-start(bf16[128,1024]{1,0:T(8,128)(2,1)} %get-tuple-element.40), channel_id=1, source_target_pairs={{0,1},{1,0},{2,3},{3,2},{4,5},{5,4},{6,7},{7,6},{8,9},{9,8},{10,11... | collective-permute-start | bytes 786440 | tf_op jit(solution)/shard_map/ppermute | solution.py:645
  60.4 2.5 %copy-done = bf16[2048,1280]{1,0:T(8,128)(2,1)S(1)} copy-done((bf16[2048,1280]{1,0:T(8,128)(2,1)S(1)}, bf16[2048,1280]{1,0:T(8,128)(2,1)}, u32[]{:S(2)}) %copy-start) | copy-done | bytes 5242904
  62.9 0.4 load.3.refs_0_
  63.3 1.2 %copy-done.1 = bf16[512,2048]{1,0:T(8,128)(2,1)S(1)} copy-done((bf16[512,2048]{1,0:T(8,128)(2,1)S(1)}, bf16[512,2048]{1,0:T(8,128)(2,1)}, u32[]{:S(2)}) %copy-start.1) | copy-done | bytes 2097176
  64.5 0.4 own_share.1.refs_1_
  65.1 5.2 %tail.1 = (bf16[128,1024]{1,0:T(8,128)(2,1)S(1)}, bf16[128,1280]{1,0:T(8,128)(2,1)S(1)}, bf16[128,1024]{1,0:T(8,128)(2,1)S(1)}) custom-call(s32[2]{0:T(128)S(1)} %copy-done.19, bf16[2048,1280]{1,0:T(8,128)(2,1)S(1)} %load.3.refs_0_, bf16[128,2048]{1,0:T(8,128)(2,1)S(1)} %own_share.1.refs_1_, bf16[128,1024]{1,0:T(8,128)(2,1)S(1)} %copy-done.4, ...), custom_call_target="tpu_custom_call" | custom-call | flops 1677721600 | bytes 7864320 | tf_op jit(solution)/shard_map/tail/pallas_call | solution.py:563
  70.4 0.6 collective-permute-start.9
  71.0 1.5 %keep.1 = f32[128,1024]{1,0:T(8,128)S(1)} custom-call(s32[2]{0:T(128)S(1)} %copy-done.19, bf16[128,1280]{1,0:T(8,128)(2,1)S(1)} %get-tuple-element.45.hidden_ref, bf16[128,1024]{1,0:T(8,128)(2,1)S(1)} %get-tuple-element.46.residual_ref, bf16[1280,2048]{1,0:T(8,128)(2,1)S(1)} %bitcast.11), custom_call_target="tpu_custom_call" | custom-call | flops 335544320 | bytes 2621440 | tf_op jit(solution)/shard_map/keep/pallas_call | solution.py:577
  72.5 0.8 %add_convert_fusion.1 = bf16[128,1024]{1,0:T(8,128)(2,1)} fusion(bf16[128,1024]{1,0:T(8,128)(2,1)S(1)} %collective-permute-done.7, bf16[128,1024]{1,0:T(8,128)(2,1)S(1)} %copy-done.22, bf16[128,1024]{1,0:T(8,128)(2,1)S(1)} %copy-done.23), kind=kLoop, calls=%fused_computation.1 | loop fusion | flops 786432 | bytes 1048576 | tf_op jit(solution)/shard_map/convert_element_type | solution.py:647
  73.3 5.1 %collective-permute-done.9 = bf16[128,1024]{1,0:T(8,128)(2,1)S(1)} collective-permute-done((bf16[128,1024]{1,0:T(8,128)(2,1)S(1)}, bf16[128,1024]{1,0:T(8,128)(2,1)S(1)}, u32[]{:S(2)}, u32[]{:S(2)}) %collective-permute-start.9) | collective-permute-done | bytes 262176 | tf_op jit(solution)/shard_map/ppermute | solution.py:587
  78.4 0.8 add_convert_fusion
  (65 shorter events, 0.6 us)
Async XLA Ops:
  0.6 10.4 %copy-start.3 = (bf16[128,1024]{1,0:T(8,128)(2,1)S(1)}, bf16[128,1024]{1,0:T(8,128)(2,1)}, u32[]{:S(2)}) copy-start(bf16[128,1024]{1,0:T(8,128)(2,1)} %refs_2_.3) | copy-start | bytes 786436
  0.6 10.4 %copy-start.17 = (f32[2048]{0:T(1024)S(1)}, f32[2048]{0:T(1024)}, u32[]{:S(2)}) copy-start(f32[2048]{0:T(1024)} %param.20) | copy-start | bytes 24580
  0.7 10.4 %copy-start.20 = (s32[128,1]{0,1:T(1,128)S(1)}, s32[128,1]{0,1:T(1,128)}, u32[]{:S(2)}) copy-start(s32[128,1]{0,1:T(1,128)} %param.18) | copy-start | bytes 1540
  0.7 10.3 %collective-permute-start = (bf16[128,1024]{1,0:T(8,128)(2,1)}, bf16[128,1024]{1,0:T(8,128)(2,1)S(1)}, u32[]{:S(2)}, u32[]{:S(2)}) collective-permute-start(bf16[128,1024]{1,0:T(8,128)(2,1)} %refs_2_.3), channel_id=1, source_target_pairs={{0,1},{1,0},{2,3},{3,2},{4,5},{5,4},{6,7},{7,6},{8,9},{9,8},{10,11... | collective-permute-start | bytes 786440 | tf_op jit(solution)/shard_map/ppermute | solution.py:593
  6.0 13.7 %collective-permute-start.1 = (bf16[128,1024]{1,0:T(8,128)(2,1)}, bf16[128,1024]{1,0:T(8,128)(2,1)S(1)}, u32[]{:S(2)}, u32[]{:S(2)}) collective-permute-start(bf16[128,1024]{1,0:T(8,128)(2,1)} %refs_0_.5), channel_id=1, source_target_pairs={{0,1},{1,0},{2,3},{3,2},{4,5},{5,4},{6,7},{7,6},{8,9},{9,8},{10,11... | collective-permute-start | bytes 786440 | tf_op jit(solution)/shard_map/ppermute | solution.py:593
  6.0 24.8 %collective-permute-start.2 = (bf16[128,2048]{1,0:T(8,128)(2,1)}, bf16[128,2048]{1,0:T(8,128)(2,1)S(1)}, u32[]{:S(2)}, u32[]{:S(2)}) collective-permute-start(bf16[128,2048]{1,0:T(8,128)(2,1)} %get-tuple-element.27), channel_id=1, source_target_pairs={{0,1},{1,0},{2,3},{3,2},{4,5},{5,4},{6,7},{7,6},{8,9},{9,8},{10,11... | collective-permute-start | bytes 1572872 | tf_op jit(solution)/shard_map/ppermute | solution.py:608
  8.0 30.4 %collective-permute-start.3 = (bf16[128,2048]{1,0:T(8,128)(2,1)}, bf16[128,2048]{1,0:T(8,128)(2,1)S(1)}, u32[]{:S(2)}, u32[]{:S(2)}) collective-permute-start(bf16[128,2048]{1,0:T(8,128)(2,1)} %get-tuple-element.30), channel_id=1, source_target_pairs={{0,1},{1,0},{2,3},{3,2},{4,5},{5,4},{6,7},{7,6},{8,9},{9,8},{10,11... | collective-permute-start | bytes 1572872 | tf_op jit(solution)/shard_map/ppermute | solution.py:608
  9.9 9.8 %copy-start.18 = (s32[2]{0:T(128)}, s32[2]{0:T(128)S(1)}, u32[]{:S(2)}) copy-start(s32[2]{0:T(128)S(1)} %pad_add_fusion.place_ref) | copy-start | bytes 28
  11.0 8.7 %copy-start.5 = (bf16[128,1024]{1,0:T(8,128)(2,1)}, bf16[128,1024]{1,0:T(8,128)(2,1)S(1)}, u32[]{:S(2)}) copy-start(bf16[128,1024]{1,0:T(8,128)(2,1)S(1)} %collective-permute-done.refs_1_.refs_3_) | copy-start | bytes 786436
  13.2 17.7 %all-to-all-start = ((bf16[16,16,512]{2,1,0:T(8,128)(2,1)}), bf16[16,16,512]{2,1,0:T(8,128)(2,1)S(1)}, u32[]{:S(2)}, u32[]{:S(2)}) async-start(bf16[16,16,512]{2,1,0:T(8,128)(2,1)} %bitcast.4), calls=%async_computation | async-start | bytes 524288 | tf_op jit(solution)/shard_map/all_to_all | solution.py:706
  30.8 9.7 %copy-start.7 = (bf16[128,2048]{1,0:T(8,128)(2,1)}, bf16[128,2048]{1,0:T(8,128)(2,1)S(1)}, u32[]{:S(2)}) copy-start(bf16[128,2048]{1,0:T(8,128)(2,1)S(1)} %collective-permute-done.2.refs_6_) | copy-start | bytes 1572868
  32.3 6.8 %copy-start.25 = (bf16[128,512]{1,0:T(8,128)(2,1)S(1)}, bf16[128,512]{1,0:T(8,128)(2,1)}, u32[]{:S(2)}) copy-start(bf16[128,512]{1,0:T(8,128)(2,1)} %get-tuple-element.32.refs_2_) | copy-start | bytes 393220
  38.4 8.2 %copy-start.9 = (bf16[128,2048]{1,0:T(8,128)(2,1)}, bf16[128,2048]{1,0:T(8,128)(2,1)S(1)}, u32[]{:S(2)}) copy-start(bf16[128,2048]{1,0:T(8,128)(2,1)S(1)} %collective-permute-done.3.refs_7_) | copy-start | bytes 1572868
  38.5 8.1 %collective-permute-start.6 = (bf16[128,2048]{1,0:T(8,128)(2,1)S(1)}, bf16[128,2048]{1,0:T(8,128)(2,1)S(1)}, u32[]{:S(2)}, u32[]{:S(2)}) collective-permute-start(bf16[128,2048]{1,0:T(8,128)(2,1)S(1)} %collective-permute-done.3.refs_7_), channel_id=1, source_target_pairs={{0,2},{2,0},{4,6},{6,4},{8,10},{10,8},{12,14},{14,12},{16,18},{18,... | collective-permute-start | bytes 1572872 | tf_op jit(solution)/shard_map/ppermute | solution.py:612
  38.9 7.7 %collective-permute-start.5 = (bf16[128,2048]{1,0:T(8,128)(2,1)S(1)}, bf16[128,2048]{1,0:T(8,128)(2,1)S(1)}, u32[]{:S(2)}, u32[]{:S(2)}) collective-permute-start(bf16[128,2048]{1,0:T(8,128)(2,1)S(1)} %collective-permute-done.2.refs_6_), channel_id=1, source_target_pairs={{0,2},{2,0},{4,6},{6,4},{8,10},{10,8},{12,14},{14,12},{16,18},{18,... | collective-permute-start | bytes 1572872 | tf_op jit(solution)/shard_map/ppermute | solution.py:612
  39.0 7.5 %collective-permute-start.4 = (bf16[128,512]{1,0:T(8,128)(2,1)S(1)}, bf16[128,512]{1,0:T(8,128)(2,1)S(1)}, u32[]{:S(2)}, u32[]{:S(2)}) collective-permute-start(bf16[128,512]{1,0:T(8,128)(2,1)S(1)} %copy-done.25), channel_id=1, source_target_pairs={{0,1},{1,0},{2,3},{3,2},{4,5},{5,4},{6,7},{7,6},{8,9},{9,8},{10,11... | collective-permute-start | bytes 393224 | tf_op jit(solution)/shard_map/ppermute | solution.py:593
  40.5 17.1 %all-to-all-start.1 = ((bf16[16,16,640]{2,1,0:T(8,128)(2,1)}), bf16[16,16,640]{2,1,0:T(8,128)(2,1)S(1)}, u32[]{:S(2)}, u32[]{:S(2)}) async-start(bf16[16,16,640]{2,1,0:T(8,128)(2,1)} %bitcast.7), calls=%async_computation.1 | async-start | bytes 655360 | tf_op jit(solution)/shard_map/all_to_all | solution.py:777
  47.6 10.1 %copy-start.15 = (f32[128,640]{1,0:T(8,128)S(1)}, f32[128,640]{1,0:T(8,128)}, u32[]{:S(2)}) copy-start(f32[128,640]{1,0:T(8,128)} %get-tuple-element.42.refs_2_) | copy-start | bytes 983044
  57.7 7.3 %copy-start.4 = (bf16[128,1024]{1,0:T(8,128)(2,1)S(1)}, bf16[128,1024]{1,0:T(8,128)(2,1)}, u32[]{:S(2)}) copy-start(bf16[128,1024]{1,0:T(8,128)(2,1)} %refs_2_.3) | copy-start | bytes 786436
  57.7 7.3 %copy-start.6 = (bf16[128,1024]{1,0:T(8,128)(2,1)S(1)}, bf16[128,1024]{1,0:T(8,128)(2,1)}, u32[]{:S(2)}) copy-start(bf16[128,1024]{1,0:T(8,128)(2,1)} %copy-done.5) | copy-start | bytes 786436
  57.7 7.3 %copy-start.16 = (f32[2048]{0:T(1024)S(1)}, f32[2048]{0:T(1024)}, u32[]{:S(2)}) copy-start(f32[2048]{0:T(1024)} %param.24) | copy-start | bytes 24580
  57.7 7.4 %copy-start.19 = (s32[2]{0:T(128)S(1)}, s32[2]{0:T(128)}, u32[]{:S(2)}) copy-start(s32[2]{0:T(128)} %copy-done.18) | copy-start | bytes 28
  58.3 6.6 %collective-permute-start.8 = (bf16[128,512]{1,0:T(8,128)(2,1)S(1)}, bf16[128,512]{1,0:T(8,128)(2,1)S(1)}, u32[]{:S(2)}, u32[]{:S(2)}) collective-permute-start(bf16[128,512]{1,0:T(8,128)(2,1)S(1)} %merge.1.att_ref), channel_id=1, source_target_pairs={{0,1},{1,0},{2,3},{3,2},{4,5},{5,4},{6,7},{7,6},{8,9},{9,8},{10,11... | collective-permute-start | bytes 393224 | tf_op jit(solution)/shard_map/ppermute | solution.py:593
  58.9 13.5 %collective-permute-start.7 = (bf16[128,1024]{1,0:T(8,128)(2,1)}, bf16[128,1024]{1,0:T(8,128)(2,1)S(1)}, u32[]{:S(2)}, u32[]{:S(2)}) collective-permute-start(bf16[128,1024]{1,0:T(8,128)(2,1)} %get-tuple-element.40), channel_id=1, source_target_pairs={{0,1},{1,0},{2,3},{3,2},{4,5},{5,4},{6,7},{7,6},{8,9},{9,8},{10,11... | collective-permute-start | bytes 786440 | tf_op jit(solution)/shard_map/ppermute | solution.py:645
  60.4 2.5 %copy-start = (bf16[2048,1280]{1,0:T(8,128)(2,1)S(1)}, bf16[2048,1280]{1,0:T(8,128)(2,1)}, u32[]{:S(2)}) copy-start(bf16[2048,1280]{1,0:T(8,128)(2,1)} %refs_0_.6) | copy-start | bytes 15728644
  62.9 2.1 %copy-start.8 = (bf16[128,2048]{1,0:T(8,128)(2,1)S(1)}, bf16[128,2048]{1,0:T(8,128)(2,1)}, u32[]{:S(2)}) copy-start(bf16[128,2048]{1,0:T(8,128)(2,1)} %copy-done.7) | copy-start | bytes 1572868
  62.9 2.1 %copy-start.10 = (bf16[128,2048]{1,0:T(8,128)(2,1)S(1)}, bf16[128,2048]{1,0:T(8,128)(2,1)}, u32[]{:S(2)}) copy-start(bf16[128,2048]{1,0:T(8,128)(2,1)} %copy-done.9) | copy-start | bytes 1572868
  62.9 2.1 %copy-start.12 = (bf16[128,2048]{1,0:T(8,128)(2,1)S(1)}, bf16[128,2048]{1,0:T(8,128)(2,1)}, u32[]{:S(2)}) copy-start(bf16[128,2048]{1,0:T(8,128)(2,1)} %copy-done.11) | copy-start | bytes 1572868
  62.9 2.2 %copy-start.14 = (bf16[128,2048]{1,0:T(8,128)(2,1)S(1)}, bf16[128,2048]{1,0:T(8,128)(2,1)}, u32[]{:S(2)}) copy-start(bf16[128,2048]{1,0:T(8,128)(2,1)} %copy-done.13) | copy-start | bytes 1572868
  64.5 6.5 %slice-start = ((s8[5242880]{0:T(1024)(128)(4,1)}), s8[4194304]{0:T(1024)(128)(4,1)S(1)}, s32[]{:S(2)}) async-start(s8[5242880]{0:T(1024)(128)(4,1)} %bitcast.10), calls=%async_computation.2 | async-start | bytes 8388608
  65.0 6.0 %slice-start.1 = ((s8[5242880]{0:T(1024)(128)(4,1)}), s8[1048576]{0:T(1024)(128)(4,1)S(1)}, s32[]{:S(2)}) async-start(s8[5242880]{0:T(1024)(128)(4,1)} %bitcast.10), calls=%async_computation.3 | async-start | bytes 2097152
  70.4 8.0 %collective-permute-start.9 = (bf16[128,1024]{1,0:T(8,128)(2,1)S(1)}, bf16[128,1024]{1,0:T(8,128)(2,1)S(1)}, u32[]{:S(2)}, u32[]{:S(2)}) collective-permute-start(bf16[128,1024]{1,0:T(8,128)(2,1)S(1)} %get-tuple-element.47), channel_id=1, source_target_pairs={{0,1},{1,0},{2,3},{3,2},{4,5},{5,4},{6,7},{7,6},{8,9},{9,8},{10,11... | collective-permute-start | bytes 786440 | tf_op jit(solution)/shard_map/ppermute | solution.py:587
  (9 other events, 12.0 us)

commit v7 on v6

--- a/solution.py
+++ b/solution.py
@@ -143,18 +143,20 @@
     sources, send_ref, refs = refs[:inputs], refs[inputs], refs[inputs + 1 :]
     held, (send_scr, sems) = refs[:inputs], refs[inputs:]
     copies, started = fetch(sources, held, sems)
-    gain_ref, target_ref = held[count:]
-    for copy in started:
+    target_ref, gain_ref = held[:2]
+    started[0].wait()
+    _, slot_row = slot_places(target_ref[...], per_peer)
+    slots, half = send_scr.shape[0], send_scr.shape[0] // 2
+    spread = lax.broadcasted_iota(jnp.int32, (slots, slot_row.shape[1]), 0) == slot_row
+    spread = spread.astype(BF16)
+    for copy in started[1:]:
         copy.wait()
-    _, slot_row = slot_places(target_ref[...], per_peer)
-    spread = lax.broadcasted_iota(jnp.int32, (send_scr.shape[0], slot_row.shape[1]), 0) == slot_row
-    rows = in_order(place_ref, [ref[...] for ref in held[:count]])
+    rows = in_order(place_ref, [ref[...] for ref in held[2:]])
     normed = rms_norm(rows.astype(F32), gain_ref[...])
     queries = jnp.dot(normed, w_query_ref[...], preferred_element_type=F32).astype(BF16)
-    send_scr[...] = jnp.dot(
-        spread.astype(BF16), queries, preferred_element_type=F32
-    ).astype(BF16)
-    copies.start(send_scr, send_ref)
+    for at in (slice(0, half), slice(half, slots)):
+        send_scr[at] = jnp.dot(spread[at], queries, preferred_element_type=F32).astype(BF16)
+        copies.start(send_scr.at[at], send_ref.at[at])
     copies.wait()
 
 
@@ -689,7 +691,7 @@
     cached = request_keyval_cache.shape[1]
     w_outs, prompt_rows = share_rows(w_out, count, replicas, prompt_rows)
     prompt_parts = swap(prompt_rows, count)
-    operands = (*request_parts, attn_gain, target)
+    operands = (target, attn_gain, *request_parts)
     slot_rows = jax.ShapeDtypeStruct((slots, width), BF16)
     send = pl.pallas_call(
         functools.partial(request_kernel, count, per_peer),
@@ -697,7 +699,7 @@
         out_specs=HBM,
         out_shape=slot_rows,
         scratch_shapes=scratch_like(*operands, slot_rows)
-        + [pltpu.SemaphoreType.DMA((len(operands) + 1,))],
+        + [pltpu.SemaphoreType.DMA((len(operands) + 2,))],
         compiler_params=params(REQUEST_VMEM),
         cost_estimate=cost(0, 0),
         name="request_project",

time: 79.6 us -> 79.7 us (level)
  no operation moved by 1% of the time
where the time goes in v7:
time: 79.7 us; the launch traced here: 79.2 us
  Pallas kernels  37 us (46%)
  starting transfers between devices  22.4 us (28%)
  local copies, waits for them, and re-layouts  10.8 us (14%)
  waiting for transfers between devices  6.4 us (8%)
  other arithmetic  1.67 us (2%)
  between operations  1.04 us (1%)
    pallas_call x1, Pallas kernels, body(): pl.pallas_call(functools.partial(prompt_kernel, count), in_specs=[SCALAR]...  10.4 us
    pallas_call x1, Pallas kernels, finish(): pl.pallas_call(functools.partial(mlp_kernel, count, len(w_outs)), in_spec...  9.89 us
    unnamed x58, local copies, waits for them, and re-layouts  8.5 us
    all_to_all x1, starting transfers between devices, body(): lax.all_to_all(send, 'replica', split_axis=0, concat_axis=0, tiled=True)  6.52 us
    pallas_call x1, Pallas kernels, body(): pl.pallas_call(slot_kernel, in_specs=[HELD] * 2, out_specs=HBM, out_shape...  6.15 us
    all_to_all x1, starting transfers between devices, body(): lax.all_to_all(slot_out, 'replica', split_axis=0, concat_axis=0, tiled=True)  6.01 us
    pallas_call x1, Pallas kernels, tail(): pl.pallas_call(tail_kernel, in_specs=[SCALAR, HELD, HELD] + [ANY] * (len(...  5.22 us
    ppermute x4, starting transfers between devices, swap(): return [block, lax.ppermute(block, 'tensor', [(0, 1), (1, 0)])]  5.14 us
  transfers between devices with their start and end apart: 12, of which 3 were waited for; matrix products, arithmetic and copies ran while one was open for 4% of the time, Pallas kernels for 46%

profile of v7, /device:TPU:0, one launch (start us, length us, event | category | flops | bytes accessed | tf_op | source)
XLA Modules:
  0.0 79.2 jit_solution(10881688647321528835)
XLA Ops:
  0.7 3.0 %collective-permute-start = (bf16[128,1024]{1,0:T(8,128)(2,1)}, bf16[128,1024]{1,0:T(8,128)(2,1)S(1)}, u32[]{:S(2)}, u32[]{:S(2)}) collective-permute-start(bf16[128,1024]{1,0:T(8,128)(2,1)} %refs_2_.5), channel_id=1, source_target_pairs={{0,1},{1,0},{2,3},{3,2},{4,5},{5,4},{6,7},{7,6},{8,9},{9,8},{10,11... | collective-permute-start | bytes 786440 | tf_op jit(solution)/shard_map/ppermute | solution.py:595
  3.7 2.3 %constant_dynamic-slice_fusion.1 = (bf16[128,2048]{1,0:T(8,128)(2,1)}, bf16[128,2048]{1,0:T(8,128)(2,1)}) fusion(bf16[512,2048]{1,0:T(8,128)(2,1)} %w_out_ref.1, s32[]{:T(128)S(6)} %add.23, s32[]{:T(128)S(6)} %select_n.13), kind=kLoop, calls=%fused_computation.4 | loop fusion | bytes 2097160 | tf_op jit(solution)/shard_map/slice | solution.py:608
  6.0 2.0 %collective-permute-start.2 = (bf16[128,2048]{1,0:T(8,128)(2,1)}, bf16[128,2048]{1,0:T(8,128)(2,1)S(1)}, u32[]{:S(2)}, u32[]{:S(2)}) collective-permute-start(bf16[128,2048]{1,0:T(8,128)(2,1)} %get-tuple-element.27), channel_id=1, source_target_pairs={{0,1},{1,0},{2,3},{3,2},{4,5},{5,4},{6,7},{7,6},{8,9},{9,8},{10,11... | collective-permute-start | bytes 1572872 | tf_op jit(solution)/shard_map/ppermute | solution.py:610
  8.0 1.6 %copy-done.2 = bf16[2048,512]{1,0:T(8,128)(2,1)S(1)} copy-done((bf16[2048,512]{1,0:T(8,128)(2,1)S(1)}, bf16[2048,512]{1,0:T(8,128)(2,1)}, u32[]{:S(2)}) %copy-start.2) | copy-done | bytes 2097176
  9.9 1.1 %collective-permute-done.refs_3_ = bf16[128,1024]{1,0:T(8,128)(2,1)S(1)} collective-permute-done((bf16[128,1024]{1,0:T(8,128)(2,1)}, bf16[128,1024]{1,0:T(8,128)(2,1)S(1)}, u32[]{:S(2)}, u32[]{:S(2)}) %collective-permute-start) | collective-permute-done | bytes 262176 | tf_op jit(solution)/shard_map/ppermute | solution.py:595
  11.0 2.2 %request_project.1 = bf16[256,512]{1,0:T(8,128)(2,1)} custom-call(s32[2]{0:T(128)S(1)} %pad_add_fusion.place_ref, bf16[2048,512]{1,0:T(8,128)(2,1)S(1)} %load.2.w_query_ref, s32[1,128]{1,0:T(1,128)S(1)} %bitcast.18, f32[1,2048]{1,0:T(1,128)S(1)} %bitcast.17, bf16[128,1024]{1,0:T(8,128)(2,1)S(1)} %copy-done.3, bf16[128,1024]{1,0:T(8,128)(2,1)S(1)} %collective-permute-done.refs_3_), custom_call_target="tpu_custom_call" | custom-call | tf_op jit(solution)/shard_map/request_project/pallas_call | solution.py:696
  13.3 6.5 %all-to-all-start = ((bf16[16,16,512]{2,1,0:T(8,128)(2,1)}), bf16[16,16,512]{2,1,0:T(8,128)(2,1)S(1)}, u32[]{:S(2)}, u32[]{:S(2)}) async-start(bf16[16,16,512]{2,1,0:T(8,128)(2,1)} %bitcast.4), calls=%async_computation | async-start | bytes 524288 | tf_op jit(solution)/shard_map/all_to_all | solution.py:708
  19.8 0.7 copy-done.24
  20.5 10.4 %prompt_attention.1 = (bf16[128,512]{1,0:T(8,128)(2,1)}, f32[128,640]{1,0:T(8,128)}) custom-call(s32[2]{0:T(128)} %copy-done.18, bf16[128,1024]{1,0:T(8,128)(2,1)} %refs_0_.3, bf16[128,1024]{1,0:T(8,128)(2,1)} %copy-done.24, bf16[128,1024]{1,0:T(8,128)(2,1)} %refs_2_.5, bf16[128,1024]{1,0:T(8,128)(2,1)} %copy-done.5, f32[1,2048]{1,0:T(1,128)} %bitcast.16, ...), custom_call_target="tpu_custom_call" | custom-call | flops 13958643712 | bytes 4194304 | tf_op jit(solution)/shard_map/prompt_attention/pallas_call | solution.py:725
  31.0 1.4 %copy-done.21 = bf16[2048,256]{1,0:T(8,128)(2,1)S(1)} copy-done((bf16[2048,256]{1,0:T(8,128)(2,1)S(1)}, bf16[2048,256]{1,0:T(8,128)(2,1)}, u32[]{:S(2)}) %copy-start.21) | copy-done | bytes 1048600
  32.4 6.1 %slot_attention.1 = bf16[256,640]{1,0:T(8,128)(2,1)} custom-call(bf16[256,512]{1,0:T(8,128)(2,1)S(1)} %bitcast.13, bf16[2048,256]{1,0:T(8,128)(2,1)S(1)} %copy-done.21), custom_call_target="tpu_custom_call" | custom-call | flops 2147483648 | bytes 1048576 | tf_op jit(solution)/shard_map/slot_attention/pallas_call | solution.py:757
  38.6 0.5 collective-permute-start.6
  39.1 1.5 %collective-permute-start.4 = (bf16[128,512]{1,0:T(8,128)(2,1)S(1)}, bf16[128,512]{1,0:T(8,128)(2,1)S(1)}, u32[]{:S(2)}, u32[]{:S(2)}) collective-permute-start(bf16[128,512]{1,0:T(8,128)(2,1)S(1)} %copy-done.25), channel_id=1, source_target_pairs={{0,1},{1,0},{2,3},{3,2},{4,5},{5,4},{6,7},{7,6},{8,9},{9,8},{10,11... | collective-permute-start | bytes 393224 | tf_op jit(solution)/shard_map/ppermute | solution.py:595
  40.6 6.0 %all-to-all-start.1 = ((bf16[16,16,640]{2,1,0:T(8,128)(2,1)}), bf16[16,16,640]{2,1,0:T(8,128)(2,1)S(1)}, u32[]{:S(2)}, u32[]{:S(2)}) async-start(bf16[16,16,640]{2,1,0:T(8,128)(2,1)} %bitcast.7), calls=%async_computation.1 | async-start | bytes 655360 | tf_op jit(solution)/shard_map/all_to_all | solution.py:779
  46.7 0.6 copy-done.26
  47.3 0.2 copy-done.11
  47.5 0.2 copy-done.13
  47.7 9.9 %mlp.1 = (bf16[128,1024]{1,0:T(8,128)(2,1)}, bf16[128,1024]{1,0:T(8,128)(2,1)}, bf16[128,1024]{1,0:T(8,128)(2,1)}) custom-call(s32[2]{0:T(128)} %copy-done.18, bf16[128,1024]{1,0:T(8,128)(2,1)} %refs_0_.3, bf16[128,1024]{1,0:T(8,128)(2,1)} %copy-done.24, bf16[128,512]{1,0:T(8,128)(2,1)} %get-tuple-element.32.refs_2_, bf16[128,512]{1,0:T(8,128)(2,1)} %copy-done.26, ...), custom_call_target="tpu_custom_call" | custom-call | flops 64424509440 | bytes 15728640 | tf_op jit(solution)/shard_map/mlp/pallas_call | solution.py:630
  57.6 0.2 all-to-all-done.1
  57.8 0.7 merge.1.att_ref
  58.4 0.6 collective-permute-start.8
  59.0 1.5 %collective-permute-start.7 = (bf16[128,1024]{1,0:T(8,128)(2,1)}, bf16[128,1024]{1,0:T(8,128)(2,1)S(1)}, u32[]{:S(2)}, u32[]{:S(2)}) collective-permute-start(bf16[128,1024]{1,0:T(8,128)(2,1)} %get-tuple-element.40), channel_id=1, source_target_pairs={{0,1},{1,0},{2,3},{3,2},{4,5},{5,4},{6,7},{7,6},{8,9},{9,8},{10,11... | collective-permute-start | bytes 786440 | tf_op jit(solution)/shard_map/ppermute | solution.py:647
  60.5 2.5 %copy-done = bf16[2048,1280]{1,0:T(8,128)(2,1)S(1)} copy-done((bf16[2048,1280]{1,0:T(8,128)(2,1)S(1)}, bf16[2048,1280]{1,0:T(8,128)(2,1)}, u32[]{:S(2)}) %copy-start) | copy-done | bytes 5242904
  63.0 0.4 load.3.refs_0_
  63.4 1.2 %copy-done.1 = bf16[512,2048]{1,0:T(8,128)(2,1)S(1)} copy-done((bf16[512,2048]{1,0:T(8,128)(2,1)S(1)}, bf16[512,2048]{1,0:T(8,128)(2,1)}, u32[]{:S(2)}) %copy-start.1) | copy-done | bytes 2097176
  64.6 0.4 own_share.1.refs_1_
  65.2 5.2 %tail.1 = (bf16[128,1024]{1,0:T(8,128)(2,1)S(1)}, bf16[128,1280]{1,0:T(8,128)(2,1)S(1)}, bf16[128,1024]{1,0:T(8,128)(2,1)S(1)}) custom-call(s32[2]{0:T(128)S(1)} %copy-done.19, bf16[2048,1280]{1,0:T(8,128)(2,1)S(1)} %load.3.refs_0_, bf16[128,2048]{1,0:T(8,128)(2,1)S(1)} %own_share.1.refs_1_, bf16[128,1024]{1,0:T(8,128)(2,1)S(1)} %copy-done.4, ...), custom_call_target="tpu_custom_call" | custom-call | flops 1677721600 | bytes 7864320 | tf_op jit(solution)/shard_map/tail/pallas_call | solution.py:565
  70.5 0.6 collective-permute-start.9
  71.1 1.5 %keep.1 = f32[128,1024]{1,0:T(8,128)S(1)} custom-call(s32[2]{0:T(128)S(1)} %copy-done.19, bf16[128,1280]{1,0:T(8,128)(2,1)S(1)} %get-tuple-element.45.hidden_ref, bf16[128,1024]{1,0:T(8,128)(2,1)S(1)} %get-tuple-element.46.residual_ref, bf16[1280,2048]{1,0:T(8,128)(2,1)S(1)} %bitcast.11), custom_call_target="tpu_custom_call" | custom-call | flops 335544320 | bytes 2621440 | tf_op jit(solution)/shard_map/keep/pallas_call | solution.py:579
  72.6 0.8 %add_convert_fusion.1 = bf16[128,1024]{1,0:T(8,128)(2,1)} fusion(bf16[128,1024]{1,0:T(8,128)(2,1)S(1)} %collective-permute-done.7, bf16[128,1024]{1,0:T(8,128)(2,1)S(1)} %copy-done.22, bf16[128,1024]{1,0:T(8,128)(2,1)S(1)} %copy-done.23), kind=kLoop, calls=%fused_computation.1 | loop fusion | flops 786432 | bytes 1048576 | tf_op jit(solution)/shard_map/convert_element_type | solution.py:649
  73.4 5.1 %collective-permute-done.9 = bf16[128,1024]{1,0:T(8,128)(2,1)S(1)} collective-permute-done((bf16[128,1024]{1,0:T(8,128)(2,1)S(1)}, bf16[128,1024]{1,0:T(8,128)(2,1)S(1)}, u32[]{:S(2)}, u32[]{:S(2)}) %collective-permute-start.9) | collective-permute-done | bytes 262176 | tf_op jit(solution)/shard_map/ppermute | solution.py:589
  78.5 0.8 add_convert_fusion
  (65 shorter events, 0.6 us)
Async XLA Ops:
  0.6 10.4 %copy-start.3 = (bf16[128,1024]{1,0:T(8,128)(2,1)S(1)}, bf16[128,1024]{1,0:T(8,128)(2,1)}, u32[]{:S(2)}) copy-start(bf16[128,1024]{1,0:T(8,128)(2,1)} %refs_2_.5) | copy-start | bytes 786436
  0.6 10.4 %copy-start.17 = (f32[2048]{0:T(1024)S(1)}, f32[2048]{0:T(1024)}, u32[]{:S(2)}) copy-start(f32[2048]{0:T(1024)} %param.20) | copy-start | bytes 24580
  0.7 10.4 %copy-start.20 = (s32[128,1]{0,1:T(1,128)S(1)}, s32[128,1]{0,1:T(1,128)}, u32[]{:S(2)}) copy-start(s32[128,1]{0,1:T(1,128)} %param.18) | copy-start | bytes 1540
  0.7 10.3 %collective-permute-start = (bf16[128,1024]{1,0:T(8,128)(2,1)}, bf16[128,1024]{1,0:T(8,128)(2,1)S(1)}, u32[]{:S(2)}, u32[]{:S(2)}) collective-permute-start(bf16[128,1024]{1,0:T(8,128)(2,1)} %refs_2_.5), channel_id=1, source_target_pairs={{0,1},{1,0},{2,3},{3,2},{4,5},{5,4},{6,7},{7,6},{8,9},{9,8},{10,11... | collective-permute-start | bytes 786440 | tf_op jit(solution)/shard_map/ppermute | solution.py:595
  6.0 13.8 %collective-permute-start.1 = (bf16[128,1024]{1,0:T(8,128)(2,1)}, bf16[128,1024]{1,0:T(8,128)(2,1)S(1)}, u32[]{:S(2)}, u32[]{:S(2)}) collective-permute-start(bf16[128,1024]{1,0:T(8,128)(2,1)} %refs_0_.3), channel_id=1, source_target_pairs={{0,1},{1,0},{2,3},{3,2},{4,5},{5,4},{6,7},{7,6},{8,9},{9,8},{10,11... | collective-permute-start | bytes 786440 | tf_op jit(solution)/shard_map/ppermute | solution.py:595
  6.0 24.9 %collective-permute-start.2 = (bf16[128,2048]{1,0:T(8,128)(2,1)}, bf16[128,2048]{1,0:T(8,128)(2,1)S(1)}, u32[]{:S(2)}, u32[]{:S(2)}) collective-permute-start(bf16[128,2048]{1,0:T(8,128)(2,1)} %get-tuple-element.27), channel_id=1, source_target_pairs={{0,1},{1,0},{2,3},{3,2},{4,5},{5,4},{6,7},{7,6},{8,9},{9,8},{10,11... | collective-permute-start | bytes 1572872 | tf_op jit(solution)/shard_map/ppermute | solution.py:610
  8.0 30.6 %collective-permute-start.3 = (bf16[128,2048]{1,0:T(8,128)(2,1)}, bf16[128,2048]{1,0:T(8,128)(2,1)S(1)}, u32[]{:S(2)}, u32[]{:S(2)}) collective-permute-start(bf16[128,2048]{1,0:T(8,128)(2,1)} %get-tuple-element.30), channel_id=1, source_target_pairs={{0,1},{1,0},{2,3},{3,2},{4,5},{5,4},{6,7},{7,6},{8,9},{9,8},{10,11... | collective-permute-start | bytes 1572872 | tf_op jit(solution)/shard_map/ppermute | solution.py:610
  9.9 10.0 %copy-start.18 = (s32[2]{0:T(128)}, s32[2]{0:T(128)S(1)}, u32[]{:S(2)}) copy-start(s32[2]{0:T(128)S(1)} %pad_add_fusion.place_ref) | copy-start | bytes 28
  11.0 8.8 %copy-start.5 = (bf16[128,1024]{1,0:T(8,128)(2,1)}, bf16[128,1024]{1,0:T(8,128)(2,1)S(1)}, u32[]{:S(2)}) copy-start(bf16[128,1024]{1,0:T(8,128)(2,1)S(1)} %collective-permute-done.refs_3_) | copy-start | bytes 786436
  13.3 17.7 %all-to-all-start = ((bf16[16,16,512]{2,1,0:T(8,128)(2,1)}), bf16[16,16,512]{2,1,0:T(8,128)(2,1)S(1)}, u32[]{:S(2)}, u32[]{:S(2)}) async-start(bf16[16,16,512]{2,1,0:T(8,128)(2,1)} %bitcast.4), calls=%async_computation | async-start | bytes 524288 | tf_op jit(solution)/shard_map/all_to_all | solution.py:708
  31.0 9.7 %copy-start.7 = (bf16[128,2048]{1,0:T(8,128)(2,1)}, bf16[128,2048]{1,0:T(8,128)(2,1)S(1)}, u32[]{:S(2)}) copy-start(bf16[128,2048]{1,0:T(8,128)(2,1)S(1)} %collective-permute-done.2.refs_6_) | copy-start | bytes 1572868
  32.4 6.8 %copy-start.25 = (bf16[128,512]{1,0:T(8,128)(2,1)S(1)}, bf16[128,512]{1,0:T(8,128)(2,1)}, u32[]{:S(2)}) copy-start(bf16[128,512]{1,0:T(8,128)(2,1)} %get-tuple-element.32.refs_2_) | copy-start | bytes 393220
  38.6 8.2 %copy-start.9 = (bf16[128,2048]{1,0:T(8,128)(2,1)}, bf16[128,2048]{1,0:T(8,128)(2,1)S(1)}, u32[]{:S(2)}) copy-start(bf16[128,2048]{1,0:T(8,128)(2,1)S(1)} %collective-permute-done.3.refs_7_) | copy-start | bytes 1572868
  38.6 8.1 %collective-permute-start.6 = (bf16[128,2048]{1,0:T(8,128)(2,1)S(1)}, bf16[128,2048]{1,0:T(8,128)(2,1)S(1)}, u32[]{:S(2)}, u32[]{:S(2)}) collective-permute-start(bf16[128,2048]{1,0:T(8,128)(2,1)S(1)} %collective-permute-done.3.refs_7_), channel_id=1, source_target_pairs={{0,2},{2,0},{4,6},{6,4},{8,10},{10,8},{12,14},{14,12},{16,18},{18,... | collective-permute-start | bytes 1572872 | tf_op jit(solution)/shard_map/ppermute | solution.py:614
  39.0 7.7 %collective-permute-start.5 = (bf16[128,2048]{1,0:T(8,128)(2,1)S(1)}, bf16[128,2048]{1,0:T(8,128)(2,1)S(1)}, u32[]{:S(2)}, u32[]{:S(2)}) collective-permute-start(bf16[128,2048]{1,0:T(8,128)(2,1)S(1)} %collective-permute-done.2.refs_6_), channel_id=1, source_target_pairs={{0,2},{2,0},{4,6},{6,4},{8,10},{10,8},{12,14},{14,12},{16,18},{18,... | collective-permute-start | bytes 1572872 | tf_op jit(solution)/shard_map/ppermute | solution.py:614
  39.1 7.5 %collective-permute-start.4 = (bf16[128,512]{1,0:T(8,128)(2,1)S(1)}, bf16[128,512]{1,0:T(8,128)(2,1)S(1)}, u32[]{:S(2)}, u32[]{:S(2)}) collective-permute-start(bf16[128,512]{1,0:T(8,128)(2,1)S(1)} %copy-done.25), channel_id=1, source_target_pairs={{0,1},{1,0},{2,3},{3,2},{4,5},{5,4},{6,7},{7,6},{8,9},{9,8},{10,11... | collective-permute-start | bytes 393224 | tf_op jit(solution)/shard_map/ppermute | solution.py:595
  40.6 17.1 %all-to-all-start.1 = ((bf16[16,16,640]{2,1,0:T(8,128)(2,1)}), bf16[16,16,640]{2,1,0:T(8,128)(2,1)S(1)}, u32[]{:S(2)}, u32[]{:S(2)}) async-start(bf16[16,16,640]{2,1,0:T(8,128)(2,1)} %bitcast.7), calls=%async_computation.1 | async-start | bytes 655360 | tf_op jit(solution)/shard_map/all_to_all | solution.py:779
  47.7 10.1 %copy-start.15 = (f32[128,640]{1,0:T(8,128)S(1)}, f32[128,640]{1,0:T(8,128)}, u32[]{:S(2)}) copy-start(f32[128,640]{1,0:T(8,128)} %get-tuple-element.42.refs_2_) | copy-start | bytes 983044
  57.8 7.3 %copy-start.4 = (bf16[128,1024]{1,0:T(8,128)(2,1)S(1)}, bf16[128,1024]{1,0:T(8,128)(2,1)}, u32[]{:S(2)}) copy-start(bf16[128,1024]{1,0:T(8,128)(2,1)} %refs_2_.5) | copy-start | bytes 786436
  57.8 7.3 %copy-start.6 = (bf16[128,1024]{1,0:T(8,128)(2,1)S(1)}, bf16[128,1024]{1,0:T(8,128)(2,1)}, u32[]{:S(2)}) copy-start(bf16[128,1024]{1,0:T(8,128)(2,1)} %copy-done.5) | copy-start | bytes 786436
  57.8 7.3 %copy-start.16 = (f32[2048]{0:T(1024)S(1)}, f32[2048]{0:T(1024)}, u32[]{:S(2)}) copy-start(f32[2048]{0:T(1024)} %param.24) | copy-start | bytes 24580
  57.8 7.4 %copy-start.19 = (s32[2]{0:T(128)S(1)}, s32[2]{0:T(128)}, u32[]{:S(2)}) copy-start(s32[2]{0:T(128)} %copy-done.18) | copy-start | bytes 28
  58.4 6.6 %collective-permute-start.8 = (bf16[128,512]{1,0:T(8,128)(2,1)S(1)}, bf16[128,512]{1,0:T(8,128)(2,1)S(1)}, u32[]{:S(2)}, u32[]{:S(2)}) collective-permute-start(bf16[128,512]{1,0:T(8,128)(2,1)S(1)} %merge.1.att_ref), channel_id=1, source_target_pairs={{0,1},{1,0},{2,3},{3,2},{4,5},{5,4},{6,7},{7,6},{8,9},{9,8},{10,11... | collective-permute-start | bytes 393224 | tf_op jit(solution)/shard_map/ppermute | solution.py:595
  59.0 13.5 %collective-permute-start.7 = (bf16[128,1024]{1,0:T(8,128)(2,1)}, bf16[128,1024]{1,0:T(8,128)(2,1)S(1)}, u32[]{:S(2)}, u32[]{:S(2)}) collective-permute-start(bf16[128,1024]{1,0:T(8,128)(2,1)} %get-tuple-element.40), channel_id=1, source_target_pairs={{0,1},{1,0},{2,3},{3,2},{4,5},{5,4},{6,7},{7,6},{8,9},{9,8},{10,11... | collective-permute-start | bytes 786440 | tf_op jit(solution)/shard_map/ppermute | solution.py:647
  60.5 2.5 %copy-start = (bf16[2048,1280]{1,0:T(8,128)(2,1)S(1)}, bf16[2048,1280]{1,0:T(8,128)(2,1)}, u32[]{:S(2)}) copy-start(bf16[2048,1280]{1,0:T(8,128)(2,1)} %refs_0_.4) | copy-start | bytes 15728644
  63.0 2.1 %copy-start.8 = (bf16[128,2048]{1,0:T(8,128)(2,1)S(1)}, bf16[128,2048]{1,0:T(8,128)(2,1)}, u32[]{:S(2)}) copy-start(bf16[128,2048]{1,0:T(8,128)(2,1)} %copy-done.7) | copy-start | bytes 1572868
  63.0 2.1 %copy-start.10 = (bf16[128,2048]{1,0:T(8,128)(2,1)S(1)}, bf16[128,2048]{1,0:T(8,128)(2,1)}, u32[]{:S(2)}) copy-start(bf16[128,2048]{1,0:T(8,128)(2,1)} %copy-done.9) | copy-start | bytes 1572868
  63.0 2.1 %copy-start.12 = (bf16[128,2048]{1,0:T(8,128)(2,1)S(1)}, bf16[128,2048]{1,0:T(8,128)(2,1)}, u32[]{:S(2)}) copy-start(bf16[128,2048]{1,0:T(8,128)(2,1)} %copy-done.11) | copy-start | bytes 1572868
  63.0 2.2 %copy-start.14 = (bf16[128,2048]{1,0:T(8,128)(2,1)S(1)}, bf16[128,2048]{1,0:T(8,128)(2,1)}, u32[]{:S(2)}) copy-start(bf16[128,2048]{1,0:T(8,128)(2,1)} %copy-done.13) | copy-start | bytes 1572868
  64.6 6.5 %slice-start = ((s8[5242880]{0:T(1024)(128)(4,1)}), s8[4194304]{0:T(1024)(128)(4,1)S(1)}, s32[]{:S(2)}) async-start(s8[5242880]{0:T(1024)(128)(4,1)} %bitcast.10), calls=%async_computation.2 | async-start | bytes 8388608
  65.1 6.0 %slice-start.1 = ((s8[5242880]{0:T(1024)(128)(4,1)}), s8[1048576]{0:T(1024)(128)(4,1)S(1)}, s32[]{:S(2)}) async-start(s8[5242880]{0:T(1024)(128)(4,1)} %bitcast.10), calls=%async_computation.3 | async-start | bytes 2097152
  70.5 8.0 %collective-permute-start.9 = (bf16[128,1024]{1,0:T(8,128)(2,1)S(1)}, bf16[128,1024]{1,0:T(8,128)(2,1)S(1)}, u32[]{:S(2)}, u32[]{:S(2)}) collective-permute-start(bf16[128,1024]{1,0:T(8,128)(2,1)S(1)} %get-tuple-element.47), channel_id=1, source_target_pairs={{0,1},{1,0},{2,3},{3,2},{4,5},{5,4},{6,7},{7,6},{8,9},{9,8},{10,11... | collective-permute-start | bytes 786440 | tf_op jit(solution)/shard_map/ppermute | solution.py:589
  (9 other events, 12.0 us)
